TPU v7x, 32 devices: a whole 2x2x4 slice. The times are simulated.
32 devices in a mesh: facet: 8 (over z, x), freq: 4 (over y, core).
Axes of the slice: x: 2, y: 2, z: 4, core: 2. Of those that a mesh axis runs over, the one named last changes fastest.
Arguments:
- visibilities: float32 [8, 10, 2, 128, 128], P('facet', None, None, 'freq'), may hold values from -6 to 6
- coords: float32 [8, 10, 3, 128], P('facet'), may hold values from -1500 to 1500, as said below
- corners: int32 [2, 8, 10], replicated, may hold values from 0 to 480
- owners: int32 [2], replicated, may hold values from 0 to 7, as said below
- assign: int32 [8, 20], P('facet'), may hold values from 0 to 19, as said below
- counts: int32 [8], P('facet'), may hold values from 2 to 20, as said below
Outputs:
- dirty: float32 [8, 512, 512], P('facet', 'freq')
Inputs may be any that keep to these rules, and one draw needn't show every extreme that they name: `owners`: the two sets lie in different slots, one of them in the last slot. `assign`: each facet's row is a permutation of the 20 block numbers; only its first counts entries are gridded. `counts`: some facet grids all 20 blocks. `coords`: at every channel, u and v of each row of a block lie within 12 cells of the centre of that block's subgrid.
All inputs are finite; a program needn't handle non-finite values.
Results may differ from a plain program's by a relative error of at most 0.0037.
Values sent between devices are 32-bit elements; how exact they have to be, the bound alone decides.
No kernel may reach another device: no remote copies, remote signals or barrier semaphores. Data moves between devices by JAX's collectives and lax.ppermute only.
A program may use at most 64 MiB of HBM per device.

v0:
```python
import math

import jax
import jax.numpy as jnp
from jax import lax
from jax.sharding import PartitionSpec as P

SUB = 32
G = 512


two_pi = 2.0 * math.pi
field_width = 0.02
band_spread = 0.02
batch_items = 8
highest = lax.Precision.HIGHEST


def spread(value, axis, source):
    kept = jnp.where(lax.axis_index(axis) == source, value, 0).astype(value.dtype)
    return lax.psum(kept, axis)


def facet_center(facet_id, facet_total):
    row_total = facet_total // 8
    column = (facet_id % 8).astype(jnp.float32) - 3.5
    row_pos = (facet_id // 8).astype(jnp.float32) - (row_total - 1) / 2.0
    radius = field_width * field_width * (column * column + row_pos * row_pos)
    w_shift = -radius / (1.0 + jnp.sqrt(1.0 - radius))
    return (column, row_pos, w_shift)


def subgrid_tables():
    offsets = jnp.arange(SUB, dtype=jnp.int32) - SUB // 2
    position = offsets.astype(jnp.float32)
    profile = 1.0 - 0.8 * (position / (SUB / 2.0)) ** 2
    taper_square = profile[:, None] * profile[None, :]
    phase_index = offsets[:, None] * offsets[None, :] % SUB
    phase_angle = -two_pi * phase_index.astype(jnp.float32) / SUB
    return (position, taper_square, jnp.cos(phase_angle), jnp.sin(phase_angle))


def image_tables():
    offsets = jnp.arange(G, dtype=jnp.int32) - G // 2
    phase_index = offsets[:, None] * offsets[None, :] % G
    phase_angle = two_pi * phase_index.astype(jnp.float32) / G
    return (jnp.cos(phase_angle), jnp.sin(phase_angle))


def subgrid_terms(
    vis_blocks, coord_blocks, freq_ratio, corner_u, corner_v, column, row_pos, w_shift, tables
):
    position = tables[0]
    item_total = vis_blocks.shape[0]
    scaled = coord_blocks[:, :, None, :] * freq_ratio[None, None, :, None]
    u_cells = scaled[:, 0]
    v_cells = scaled[:, 1]
    w_waves = scaled[:, 2]
    rotation = two_pi * (
        u_cells * column[:, None, None]
        + v_cells * row_pos[:, None, None]
        + w_waves * w_shift[:, None, None]
    )
    rot_real = jnp.cos(rotation)
    rot_imag = jnp.sin(rotation)
    vis_real = vis_blocks[:, 0] * rot_real - vis_blocks[:, 1] * rot_imag
    vis_imag = vis_blocks[:, 0] * rot_imag + vis_blocks[:, 1] * rot_real
    centre_shift = G // 2 - SUB // 2
    delta_u = (u_cells + (centre_shift - corner_u).astype(jnp.float32)[:, None, None]).reshape(
        item_total, 1, -1
    )
    delta_v = (v_cells + (centre_shift - corner_v).astype(jnp.float32)[:, None, None]).reshape(
        item_total, 1, -1
    )
    angle_u = two_pi / SUB * delta_u * position[None, :, None]
    left_factor = jnp.concatenate([jnp.cos(angle_u), jnp.sin(angle_u)], axis=2).astype(jnp.bfloat16)
    angle_v = two_pi / SUB * delta_v * position[None, :, None]
    wave_real = jnp.cos(angle_v)
    wave_imag = jnp.sin(angle_v)
    flat_real = vis_real.reshape(item_total, 1, -1)
    flat_imag = vis_imag.reshape(item_total, 1, -1)
    right_real = flat_real * wave_real - flat_imag * wave_imag
    right_imag = flat_real * wave_imag + flat_imag * wave_real
    upper_rows = jnp.concatenate([right_real, -right_imag], axis=2)
    lower_rows = jnp.concatenate([right_imag, right_real], axis=2)
    right_factor = jnp.concatenate([upper_rows, lower_rows], axis=1).astype(jnp.bfloat16)
    return (left_factor, right_factor)


def subgrid_finish(product, tables):
    taper_square, dft_real, dft_imag = (tables[1], tables[2], tables[3])
    image_real = product[:, :, :SUB] * taper_square
    image_imag = product[:, :, SUB:] * taper_square
    half_real = jnp.einsum("pl,slm->spm", dft_real, image_real, precision=highest) - jnp.einsum(
        "pl,slm->spm", dft_imag, image_imag, precision=highest
    )
    half_imag = jnp.einsum("pl,slm->spm", dft_real, image_imag, precision=highest) + jnp.einsum(
        "pl,slm->spm", dft_imag, image_real, precision=highest
    )
    uv_real = jnp.einsum("spm,qm->spq", half_real, dft_real, precision=highest) - jnp.einsum(
        "spm,qm->spq", half_imag, dft_imag, precision=highest
    )
    uv_imag = jnp.einsum("spm,qm->spq", half_real, dft_imag, precision=highest) + jnp.einsum(
        "spm,qm->spq", half_imag, dft_real, precision=highest
    )
    return jnp.stack([uv_real, uv_imag], axis=1)


def add_pieces(uv_grid, pieces, corner_u, corner_v, weights):
    zero_index = jnp.zeros((), jnp.int32)
    for item in range(batch_items):
        anchor = (zero_index, corner_u[item], corner_v[item])
        current = lax.dynamic_slice(uv_grid, anchor, (2, SUB, SUB))
        uv_grid = lax.dynamic_update_slice(uv_grid, current + pieces[item] * weights[item], anchor)
    return uv_grid


def broadcast_set(visibilities, coords, set_owner):
    return (spread(visibilities, "facet", set_owner), spread(coords, "facet", set_owner))


def grid_items(block_data, list_pair, end_item, count_first, centre_pair, freq_ratio, tables):
    vis_all, coord_all, corner_all = block_data
    first_list, second_list = list_pair
    first_centre, second_centre = centre_pair
    list_length = first_list.shape[0]

    def grid_step(batch_index, grid_pair):
        item_index = batch_index * batch_items + jnp.arange(batch_items, dtype=jnp.int32)
        is_live = item_index < end_item
        is_later = item_index >= count_first
        slot_index = jnp.clip(
            jnp.where(is_later, item_index - count_first, item_index), 0, list_length - 1
        )
        block_index = jnp.where(
            is_later, jnp.take(second_list, slot_index), jnp.take(first_list, slot_index)
        )
        column = jnp.where(is_later, second_centre[0], first_centre[0])
        row_pos = jnp.where(is_later, second_centre[1], first_centre[1])
        w_shift = jnp.where(is_later, second_centre[2], first_centre[2])
        corner_u = jnp.take(corner_all[0], block_index)
        corner_v = jnp.take(corner_all[1], block_index)
        left_factor, right_factor = subgrid_terms(
            jnp.take(vis_all, block_index, axis=0),
            jnp.take(coord_all, block_index, axis=0),
            freq_ratio,
            corner_u,
            corner_v,
            column,
            row_pos,
            w_shift,
            tables,
        )
        product = jnp.einsum(
            "slk,smk->slm", left_factor, right_factor, preferred_element_type=jnp.float32
        )
        pieces = subgrid_finish(product, tables)
        first_weight = jnp.logical_and(is_live, jnp.logical_not(is_later)).astype(jnp.float32)
        return (add_pieces(grid_pair[0], pieces, corner_u, corner_v, first_weight),)

    empty_grid = jnp.zeros((2, G, G), jnp.float32)
    initial = (empty_grid,)
    batch_total = (end_item + batch_items - 1) // batch_items
    return lax.fori_loop(0, batch_total, grid_step, initial)


def on_device(visibilities, coords, corners, owners, assign, counts):
    facet_total = lax.axis_size("facet")
    band_total = lax.axis_size("freq")
    facet_index = lax.axis_index("facet")
    band_index = lax.axis_index("freq")
    local_channels = visibilities.shape[3]
    block_count = visibilities.shape[1]
    block_rows = visibilities.shape[4]
    channel_total = local_channels * band_total
    channel = band_index * local_channels + jnp.arange(local_channels, dtype=jnp.int32)
    freq_ratio = 1.0 + band_spread * channel.astype(jnp.float32) / channel_total
    first_vis, first_coords = broadcast_set(visibilities, coords, owners[0])
    second_vis, second_coords = broadcast_set(visibilities, coords, owners[1])
    vis_all = jnp.concatenate([first_vis, second_vis], axis=0).reshape(
        2 * block_count, 2, local_channels, block_rows
    )
    coord_all = jnp.concatenate([first_coords, second_coords], axis=0).reshape(
        2 * block_count, 3, block_rows
    )
    corner_all = jnp.take(corners, owners, axis=1).reshape(2, 2 * block_count)
    block_data = (vis_all, coord_all, corner_all)
    tables = subgrid_tables()
    own_list = assign[0]
    own_count = counts[0]
    own_centre = facet_center(facet_index, facet_total)
    (uv_grid,) = grid_items(
        block_data,
        (own_list, own_list),
        own_count,
        own_count,
        (own_centre, own_centre),
        freq_ratio,
        tables,
    )
    row_share = G // band_total
    cos_table, sin_table = image_tables()
    image_scale = 1.0 / (SUB * SUB * math.sqrt(2 * block_count * block_rows * channel_total))
    summed = lax.psum(uv_grid, "freq")
    first_row = band_index * row_share
    rows_real = lax.dynamic_slice_in_dim(cos_table, first_row, row_share, 0)
    rows_imag = lax.dynamic_slice_in_dim(sin_table, first_row, row_share, 0)
    half_real = jnp.dot(
        rows_real, summed[0], precision=highest, preferred_element_type=jnp.float32
    ) - jnp.dot(rows_imag, summed[1], precision=highest, preferred_element_type=jnp.float32)
    half_imag = jnp.dot(
        rows_real, summed[1], precision=highest, preferred_element_type=jnp.float32
    ) + jnp.dot(rows_imag, summed[0], precision=highest, preferred_element_type=jnp.float32)
    image_part = (
        jnp.dot(half_real, cos_table, precision=highest, preferred_element_type=jnp.float32)
        - jnp.dot(half_imag, sin_table, precision=highest, preferred_element_type=jnp.float32)
    ) * image_scale
    return image_part[None]


def solution(mesh):
    placed = (
        P("facet", None, None, "freq", None),
        P("facet", None, None, None),
        P(),
        P(),
        P("facet", None),
        P("facet"),
    )
    return jax.shard_map(
        on_device, mesh=mesh, in_specs=placed, out_specs=P("facet", "freq", None), check_vma=False
    )
```

profile of v0, /device:TPU:0, one launch (start us, length us, event | category | flops | bytes accessed | tf_op | source)
XLA Modules:
  0.0 449.8 jit_solution(2948390887537652216)
XLA Ops:
  6.5 1.3 fusion.178
  9.1 1.9 broadcast_select_fusion.5
  12.5 0.7 broadcast_select_fusion.7
  13.3 39.2 %all-reduce = (f32[1,10,3,128]{3,0,2,1:T(1,128)S(1)}, f32[1,10,3,128]{3,0,2,1:T(1,128)S(1)}) all-reduce(f32[1,10,3,128]{3,0,2,1:T(1,128)S(1)} %get-tuple-element.335, f32[1,10,3,128]{3,0,2,1:T(1,128)S(1)} %get-tuple-element.334), channel_id=1, replica_groups=mesh['facet'=8,'freq'=4] {'facet'}, use_global_device_ids=true, to_apply=%region_3.4 | all-reduce | flops 7680 | bytes 61440 | tf_op jit(solution)/shard_map/psum | solution.py:21
  55.8 32.0 %all-reduce.7.cloned.1.call-done = (f32[1,10,2,32,128]{4,3,2,1,0:T(8,128)}, f32[1,10,2,32,128]{4,3,2,1,0:T(8,128)}) async-done(((f32[1,10,2,32,128]{4,3,2,1,0:T(8,128)}, f32[1,10,2,32,128]{4,3,2,1,0:T(8,128)}), (f32[1,10,2,32,128]{4,3,2,1,0:T(8,128)}, f32[1,10,2,32,128]{4,3,2,1,0:T(8,128)})) %all-reduce.7.cloned.1.call-update) | async-done | bytes 655376 | tf_op jit(solution)/shard_map/psum | solution.py:21
  87.7 1.1 pad_maximum_fusion.1
  89.1 95.3 %while.13 = (s32[]{:T(128)}, f32[2,512,512]{2,1,0:T(8,128)S(1)}, s32[]{:T(128)}, s32[2,20]{1,0:T(2,128)}, s32[]{:T(128)}, /*index=5*/s32[20]{0:T(128)S(1)}, f32[...) while((s32[]{:T(128)}, f32[2,512,512]{2,1,0:T(8,128)S(1)}, ...), condition=%wide.region_5.7_spmd.clone.clone.clone, body=%wide.region_4.6_spmd.clone.clone.clone.sunk | while | flops 351148544 | bytes 27451612 | solution.py:164
  91.2 0.7 slice_bitcast_fusion.14
  93.8 1.4 gather_fusion.1
  96.6 0.8 broadcast_select_fusion.14
  97.9 31.2 %fusion.238 = (bf16[8,32,4096]{2,1,0:T(8,128)(2,1)S(1)}, bf16[8,32,4096]{2,1,0:T(8,128)(2,1)S(1)}, bf16[8,32,4096]{2,1,0:T(8,128)(2,1)S(1)}, bf16[8,32,4096]{2,1,0:T(8,128)(2,1)S(1)}, bf16[8,32,4096]{2,1,0:T(8,128)(2,1)S(1)}) fusion(f32[32]{0:T(128)S(1)} %add_convert_fusion.2, f32[8,4096]{1,0:T(8,128)S(1)} %get-tuple-element.477, ...), kind=kLoop, calls=%fused_computation.33.clone.1 | loop fusion | flops 14680064 | bytes 11010176 | tf_op jit(solution)/shard_map/convert.6
  129.1 3.3 fusion.239
  136.1 0.7 fusion.248
  141.7 0.8 fusion.251
  142.5 1.2 dynamic_update_slice.56
  148.5 1.2 dynamic_update_slice.57
  153.9 1.4 dynamic_update_slice.58
  159.5 1.4 dynamic_update_slice.59
  164.9 0.7 fusion.255
  165.6 1.4 dynamic_update_slice.60
  171.6 1.2 dynamic_update_slice.61
  177.3 1.2 dynamic_update_slice.62
  183.1 1.2 dynamic_update_slice.63
  184.5 1.3 copy-done.2
  185.8 4.2 fusion.152
  190.0 236.6 %all-reduce.5.cloned.1.call-done = f32[2,512,512]{2,1,0:T(8,128)} async-done(((f32[2,512,512]{2,1,0:T(8,128)}), f32[2,512,512]{2,1,0:T(8,128)}) %all-reduce.5.cloned.1.call-update) | async-done | bytes 2097168 | tf_op jit(solution)/shard_map/psum | solution.py:204
  426.6 1.9 fusion.150
  428.5 1.9 convolution_subtract_fusion.3
  430.5 4.6 %fusion.154 = f32[128,512]{1,0:T(8,128)S(1)} fusion(f32[128,512]{1,0:T(8,128)S(1)} %convolution_subtract_fusion.3, s32[512]{0:T(512)S(1)} %iota_add_fusion.1), kind=kOutput, calls=%fused_computation.220 | convolution fusion | flops 406323200 | bytes 526336 | tf_op jit(solution)/shard_map/dot_general | solution.py:215
  435.1 1.7 fusion.151
  436.8 0.7 convolution_add_fusion.2
  437.5 5.5 %fusion.146 = f32[1,128,512]{2,1,0:T(8,128)} fusion(f32[128,512]{1,0:T(8,128)S(1)} %fusion.154, f32[128,512]{1,0:T(8,128)S(1)} %convolution_add_fusion.2, s32[512]{0:T(512)S(1)} %iota_add_fusion.1), kind=kOutput, calls=%fused_computation.207 | convolution fusion | flops 406454272 | bytes 788480 | tf_op jit(solution)/shard_map/dot_general | solution.py:216
  (71 shorter events, 19.2 us)
Async XLA Ops:
  6.5 46.6 %copy-start = (s32[2,8,10]{2,1,0:T(8,128)S(1)}, s32[2,8,10]{2,1,0:T(8,128)}, u32[]{:S(2)}) copy-start(s32[2,8,10]{2,1,0:T(8,128)} %param.12) | copy-start | bytes 1924
  6.5 81.2 %all-reduce.7.cloned.1.call-start = ((), (), s32[]{:S(2)}) async-start(), calls=%async_computation.1 | async-start | bytes 1310720 | tf_op jit(solution)/shard_map/psum | solution.py:21
  11.0 78.1 %copy-start.1 = (s32[1,20]{1,0:T(1,128)S(1)}, s32[1,20]{1,0:T(1,128)}, u32[]{:S(2)}) copy-start(s32[1,20]{1,0:T(1,128)} %param.14) | copy-start | bytes 244
  11.1 415.5 %all-reduce.5.cloned.1.call-start = ((), (), s32[]{:S(2)}) async-start(), calls=%async_computation | async-start | bytes 4194304 | tf_op jit(solution)/shard_map/psum | solution.py:204
  91.1 4.2 copy-start.8
  91.2 4.2 copy-start.7
  129.1 3.3 copy-start.9
  132.3 3.8 copy-start.5
  132.4 3.8 copy-start.6
  184.5 1.3 copy-start.2
  190.0 238.6 %copy-start.4 = (f32[512,512]{1,0:T(8,128)}, f32[512,512]{1,0:T(8,128)S(1)}, u32[]{:S(2)}) copy-start(f32[512,512]{1,0:T(8,128)S(1)} %get-tuple-element.337) | copy-start | bytes 3145732
  430.5 4.6 %copy-start.3 = (f32[2,512,512]{2,1,0:T(8,128)S(1)}, f32[2,512,512]{2,1,0:T(8,128)}, u32[]{:S(2)}) copy-start(f32[2,512,512]{2,1,0:T(8,128)} %all-reduce.5.cloned.1.call-done) | copy-start | bytes 6291460
Sparse Core Ops, SparseCore 0:
  11.2 76.4 all-reduce.6
  185.9 240.6 all-reduce.4
where the time goes:
time: 453 us; the launch traced here: 450 us
  waiting for transfers between devices  269 us (59%)
  other arithmetic  51.8 us (11%)
  blocking collectives  39.2 us (9%)
  loops' own time  30.8 us (7%)
  matrix products  23.2 us (5%)
  local copies, waits for them, and re-layouts  20.6 us (5%)
  between operations  15.6 us (3%)
    psum x1, waiting for transfers between devices, on_device(): summed = lax.psum(uv_grid, 'freq')  237 us
    psum x1, blocking collectives, spread(): return lax.psum(kept, axis)  39.2 us
    psum x1, waiting for transfers between devices, spread(): return lax.psum(kept, axis)  32 us
    another operation x1, other arithmetic  31.2 us
    another operation x1, loops' own time, grid_items(): return lax.fori_loop(0, batch_total, grid_step, initial)  30.8 us
    dynamic_update_slice x8, local copies, waits for them, and re-layouts, add_pieces(): lax.dynamic_update_slice(uv_grid, current + pieces[item] * weights[item],...  10.1 us
  transfers between devices with their start and end apart: 2, of which 2 were waited for; matrix products, arithmetic and copies ran while one was open for 2% of the time, Pallas kernels for 0%

commit v1 on v0

v1 whole, which is shorter than its diff:
```python
import math

import jax
import jax.numpy as jnp
import numpy as np
from jax import lax
from jax.experimental import pallas as pl
from jax.experimental.pallas import tpu as pltpu
from jax.sharding import PartitionSpec as P

SUB = 32
G = 512
HALF = SUB // 2
COLUMNS = 8

two_pi = 2.0 * math.pi
field_width = 0.02
band_spread = 0.02
centre_shift = G // 2 - SUB // 2

SIN_POLY = (6.2831853, -41.34170041, 81.6051314, -76.70301553, 42.02592778, -14.89984801, 3.23813768)
COS_POLY = (0.99999999, -19.7392045, 64.9391175, -85.45013994, 60.16763282, -25.96760244, 6.52865863)


def poly(square, coefficients):
    total = jnp.full_like(square, coefficients[-1])
    for coefficient in coefficients[-2::-1]:
        total = total * square + coefficient
    return total


def cos_sin(turns):
    rest = turns - jnp.round(turns)
    square = rest * rest
    return poly(square, COS_POLY), rest * poly(square, SIN_POLY)


def times(a, b):
    return a[0] * b[0] - a[1] * b[1], a[0] * b[1] + a[1] * b[0]


def swap_low(value):
    return (value & ~3) | ((value & 1) << 1) | ((value >> 1) & 1)


def grid_kernel(
    owners_ref, corners_ref, coords_ref, vis_ref, keep_ref, send_ref, z_ref, base_ref, step_ref, left_ref, right_ref
):
    me = lax.axis_index("facet")
    band = lax.axis_index("freq")
    band_total = lax.axis_size("freq")
    facet_rows = lax.axis_size("facet") // COLUMNS
    core = band & 1
    facet_row = pl.program_id(0)
    block = pl.program_id(1)
    channels, lanes = vis_ref.shape[3], vis_ref.shape[4]
    half_blocks = pl.num_programs(1) // 2

    @pl.when(jnp.logical_or(owners_ref[0] == me, owners_ref[1] == me))
    def _():
        corner_u = corners_ref[0, me, block]
        corner_v = corners_ref[1, me, block]
        channel = (band * channels + lax.broadcasted_iota(jnp.int32, (channels, lanes), 0)).astype(jnp.float32)
        ratio = 1.0 + band_spread * channel / (channels * band_total)
        u_cells = coords_ref[0, 0, 0:1, :] * ratio
        v_cells = coords_ref[0, 0, 1:2, :] * ratio
        w_waves = coords_ref[0, 0, 2:3, :] * ratio
        shift_u = centre_shift - corner_u
        delta_u = u_cells + shift_u.astype(jnp.float32)
        delta_v = v_cells + (centre_shift - corner_v).astype(jnp.float32)
        row_pos = facet_row.astype(jnp.float32) - (facet_rows - 1) / 2.0
        row_vec = jnp.full((8, lanes), row_pos, jnp.float32)
        common = (
            v_cells * row_pos - (delta_u + delta_v) * (0.5 / SUB) + 0.5 * (shift_u & 1).astype(jnp.float32)
        )
        vis = (vis_ref[0, 0, 0], vis_ref[0, 0, 1])
        for g in range(COLUMNS // 2):
            radius = field_width * field_width * ((g + 0.5) ** 2 + row_vec * row_vec)
            w_shift = (-radius / (1.0 + jnp.sqrt(1.0 - radius)))[0:1]
            turned = times(vis, cos_sin(common + w_waves * w_shift))
            z_ref[2 * g] = turned[0]
            z_ref[2 * g + 1] = turned[1]
        for axis, delta in enumerate((delta_u, delta_v)):
            wave = cos_sin(delta * (0.5 / SUB))
            step = times(wave, wave)
            for j in range(8):
                base_ref[2 * axis, pl.ds(j, channels, stride=8), :] = wave[0]
                base_ref[2 * axis + 1, pl.ds(j, channels, stride=8), :] = wave[1]
                if j < 7:
                    wave = times(wave, step)
            for _ in range(3):
                step = times(step, step)
            step_ref[2 * axis] = step[0]
            step_ref[2 * axis + 1] = step[1]

        chunk = channels // 4
        product = None
        for first in range(0, channels, chunk):
            for c in range(first, first + chunk):
                at = slice(c * lanes, (c + 1) * lanes)
                step = (step_ref[0, c : c + 1, :], step_ref[1, c : c + 1, :])
                twice = 2.0 * step[0]
                wave = (base_ref[0, 8 * c : 8 * c + 8, :], base_ref[1, 8 * c : 8 * c + 8, :])
                after = times(wave, step)
                for i in range(COLUMNS):
                    for part in range(2):
                        left_ref[128 * part + 16 * i : 128 * part + 16 * i + 16, at] = jnp.concatenate(
                            [wave[part], after[part]], axis=0
                        ).astype(jnp.bfloat16)
                    if i < COLUMNS - 1:
                        wave = tuple(twice * after[part] - wave[part] for part in range(2))
                        after = tuple(twice * wave[part] - after[part] for part in range(2))
                step = (step_ref[2, c : c + 1, :], step_ref[3, c : c + 1, :])
                wave = (base_ref[2, 8 * c : 8 * c + 8, :], base_ref[3, 8 * c : 8 * c + 8, :])
                after = times(wave, step)
                both = tuple(jnp.concatenate([wave[part], after[part]], axis=0) for part in range(2))
                for g in range(COLUMNS // 2):
                    for part in range(2):
                        turned = z_ref[2 * g + part, c : c + 1, :]
                        for kind in range(2):
                            row = 64 * g + 32 * part + 16 * kind
                            right_ref[row : row + 16, at] = (turned * both[kind]).astype(jnp.bfloat16)
            at = slice(first * lanes, (first + chunk) * lanes)
            term = lax.dot_general(
                right_ref[:, at],
                left_ref[:, at],
                (((1,), (1,)), ((), ())),
                preferred_element_type=jnp.float32,
            )
            product = term if product is None else product + term

        group = lax.broadcasted_iota(jnp.int32, (HALF, 128), 1) // SUB
        half = block // half_blocks
        row = pl.multiple_of((block - half * half_blocks) * HALF, HALF)
        for sign in (1, -1):
            for g in range(COLUMNS // 2):
                part = [product[64 * g + 16 * k : 64 * g + 16 * k + 16] for k in range(4)]
                (rcc, rcs), (rsc, rss), (icc, ics), (isc, iss) = [(x[:, :128], x[:, 128:]) for x in part]
                kinds = (rcc - sign * ics, -(sign * rss + isc), icc + sign * rcs, rsc - sign * iss)
                tile = None
                for t in range(4):
                    moved = kinds[t] if t == g else pltpu.roll(kinds[t], SUB * ((t - g) % 4), 1)
                    tile = moved if tile is None else jnp.where(group == t, moved, tile)
                facet = facet_row * COLUMNS + (COLUMNS // 2 + g if sign == 1 else COLUMNS // 2 - 1 - g)
                straight = facet ^ me
                crossed = swap_low(straight)

                @pl.when(half == core)
                def _():
                    keep_ref[jnp.where(core == 1, crossed, straight), pl.ds(row, HALF), :] = tile

                @pl.when(half != core)
                def _():
                    send_ref[jnp.where(core == 0, crossed, straight), pl.ds(row, HALF), :] = tile


def grid_blocks(owners, corners, coords, visibilities):
    facet_total = lax.axis_size("facet")
    _, blocks, _, channels, lanes = visibilities.shape
    half_rows = blocks // 2 * HALF
    out = jax.ShapeDtypeStruct((facet_total, half_rows, 128), jnp.float32)
    return pl.pallas_call(
        grid_kernel,
        grid=(facet_total // COLUMNS, blocks),
        in_specs=[
            pl.BlockSpec(memory_space=pltpu.SMEM),
            pl.BlockSpec(memory_space=pltpu.SMEM),
            pl.BlockSpec((1, 1, 3, lanes), lambda r, b: (0, b, 0, 0)),
            pl.BlockSpec((1, 1, 2, channels, lanes), lambda r, b: (0, b, 0, 0, 0)),
        ],
        out_specs=[pl.BlockSpec(out.shape, lambda r, b: (0, 0, 0))] * 2,
        out_shape=[out, out],
        scratch_shapes=[
            pltpu.VMEM((COLUMNS, channels, lanes), jnp.float32),
            pltpu.VMEM((4, 8 * channels, lanes), jnp.float32),
            pltpu.VMEM((4, channels, lanes), jnp.float32),
            pltpu.VMEM((256, channels * lanes), jnp.bfloat16),
            pltpu.VMEM((256, channels * lanes), jnp.bfloat16),
        ],
        compiler_params=pltpu.CompilerParams(vmem_limit_bytes=48 * 1024 * 1024),
        name="grid_blocks",
    )(owners, corners, coords, visibilities)


def image_tables(band_total, scale):
    offsets = np.arange(SUB) - HALF
    pixels = np.arange(G) - G // 2
    taper = 1.0 - 0.8 * (offsets / HALF) ** 2
    spread = np.exp(2j * np.pi * np.outer(pixels, offsets) / G)
    table = spread @ np.exp(-2j * np.pi * np.outer(offsets, offsets) / SUB) * taper
    share = G // band_total
    first = np.zeros((2, band_total, 4, SUB, 4, share))
    for sign in range(2):
        for band in range(band_total):
            wave = table[band * share : (band + 1) * share, :: 1 if sign == 0 else -1].T
            for odd in range(2):
                first[sign, band, odd, :, 2 * odd] = wave.real
                first[sign, band, odd, :, 2 * odd + 1] = wave.imag
                first[sign, band, 2 + odd, :, 2 * odd] = -wave.imag
                first[sign, band, 2 + odd, :, 2 * odd + 1] = wave.real
    upper, lower = table.T[HALF:], table.T[HALF - 1 :: -1]
    second = np.stack([(upper + lower).real, (upper + lower).imag, (upper - lower).real, (upper - lower).imag]) * scale
    return first.reshape(2 * band_total, 4 * SUB, 4 * share).astype(np.float32), second.astype(np.float32)


def two_parts(value):
    high = value.astype(jnp.bfloat16)
    return high, (value - high.astype(jnp.float32)).astype(jnp.bfloat16)


def product_of(a, b, dims):
    def dot(x, y):
        return lax.dot_general(x, y, (dims, ((), ())), preferred_element_type=jnp.float32)

    return dot(a[0], b[0]) + (dot(a[0], b[1]) + dot(a[1], b[0]))


def image_kernel(
    table_ref, owners_ref, corners_ref, assign_ref, counts_ref, own_ref, other_ref, first_ref, second_ref, out_ref,
    turn_ref, weight_ref, left_ref, right_ref,
):
    band = lax.axis_index("freq")
    core = band & 1
    blocks = corners_ref.shape[2]
    share, pixels = out_ref.shape[1], out_ref.shape[2]
    half_rows = own_ref.shape[1]
    total = 2 * blocks

    for item in range(total):
        weight_ref[assign_ref[0, item]] = (item < counts_ref[0]).astype(jnp.int32)
    across = lax.broadcasted_iota(jnp.int32, (1, pixels), 1) - pixels // 2
    down = lax.broadcasted_iota(jnp.int32, (1, share), 1) - pixels // 2 + band * share
    for b in range(total):
        owner = owners_ref[b // blocks]
        turn_ref[b : b + 1, 0:pixels] = across * (corners_ref[1, owner, b % blocks] - centre_shift)
        turn_ref[b : b + 1, pixels : pixels + share] = down * (corners_ref[0, owner, b % blocks] - centre_shift)
    turns = (turn_ref[...] & (G - 1)).astype(jnp.float32) * (1.0 / G)
    turn_cos, turn_sin = cos_sin(turns)

    mine = core == 0
    pieces = []
    for s in range(2):
        own, other = own_ref[s], other_ref[s]
        pieces += [jnp.where(mine, own, other), jnp.where(mine, other, own)]
    subs = jnp.concatenate(pieces, axis=0)
    half = product_of(two_parts(subs), two_parts(first_ref[0]), ((1,), (0,)))
    second = [second_ref[k] for k in range(4)]
    for b in range(total):
        weight = weight_ref[b].astype(jnp.float32)
        c, s = turn_cos[b : b + 1, pixels:] * weight, turn_sin[b : b + 1, pixels:] * weight
        rows = half[HALF * b : HALF * b + HALF]
        for odd in range(2):
            real, imag = rows[:, 2 * odd * share : (2 * odd + 1) * share], rows[:, (2 * odd + 1) * share : (2 * odd + 2) * share]
            real, imag = times((real, imag), (c, s))
            for k, value in enumerate((real, imag)):
                at = 4 * HALF * b + (2 * odd + k) * HALF
                high, low = two_parts(value)
                left_ref[0, at : at + HALF] = high
                left_ref[1, at : at + HALF] = low
        c, s = turn_cos[b : b + 1, :pixels], turn_sin[b : b + 1, :pixels]
        for odd in range(2):
            real, imag = times((second[2 * odd], second[2 * odd + 1]), (c, s))
            for k, value in enumerate((real, -imag)):
                at = 4 * HALF * b + (2 * odd + k) * HALF
                high, low = two_parts(value)
                right_ref[0, at : at + HALF] = high
                right_ref[1, at : at + HALF] = low
    out_ref[0] = product_of((left_ref[0], left_ref[1]), (right_ref[0], right_ref[1]), ((0,), (0,)))


def image_blocks(owners, corners, assign, counts, own, other, channel_total, block_rows):
    facet_index, band_index = lax.axis_index("facet"), lax.axis_index("freq")
    band_total = lax.axis_size("freq")
    blocks = corners.shape[2]
    share = G // band_total
    scale = 1.0 / (SUB * SUB * math.sqrt(2 * blocks * block_rows * channel_total))
    first, second = image_tables(band_total, scale)
    left_half = (facet_index % COLUMNS < COLUMNS // 2).astype(jnp.int32)
    table = (left_half * band_total + band_index).reshape(1)
    rows = 2 * blocks * 4 * HALF
    smem = pl.BlockSpec(memory_space=pltpu.SMEM)
    return pl.pallas_call(
        image_kernel,
        grid_spec=pltpu.PrefetchScalarGridSpec(
            num_scalar_prefetch=1,
            grid=(1,),
            in_specs=[
                smem,
                smem,
                smem,
                smem,
                pl.BlockSpec(own.shape, lambda i, t: (0, 0, 0)),
                pl.BlockSpec(own.shape, lambda i, t: (0, 0, 0)),
                pl.BlockSpec((1,) + first.shape[1:], lambda i, t: (t[0], 0, 0)),
                pl.BlockSpec(second.shape, lambda i, t: (0, 0, 0)),
            ],
            out_specs=pl.BlockSpec((1, share, G), lambda i, t: (0, 0, 0)),
            scratch_shapes=[
                pltpu.VMEM((2 * blocks, G + share), jnp.int32),
                pltpu.SMEM((2 * blocks,), jnp.int32),
                pltpu.VMEM((2, rows, share), jnp.bfloat16),
                pltpu.VMEM((2, rows, G), jnp.bfloat16),
            ],
        ),
        out_shape=jax.ShapeDtypeStruct((1, share, G), jnp.float32),
        compiler_params=pltpu.CompilerParams(vmem_limit_bytes=48 * 1024 * 1024),
        name="image_blocks",
    )(table, owners, corners, assign, counts, own, other, jnp.asarray(first), jnp.asarray(second))


def swap(value, partner):
    facet_total, band_total = lax.axis_size("facet"), lax.axis_size("freq")
    pairs = []
    for f in range(facet_total):
        for q in range(band_total):
            to_f, to_q = partner(f, q)
            pairs.append((f * band_total + q, to_f * band_total + to_q))
    return lax.ppermute(value, ("facet", "freq"), pairs)


def on_device(visibilities, coords, corners, owners, assign, counts):
    facet_total, band_total = lax.axis_size("facet"), lax.axis_size("freq")
    facet_index, band_index = lax.axis_index("facet"), lax.axis_index("freq")
    channel_total = visibilities.shape[3] * band_total
    keep, send = grid_blocks(owners, corners, coords, visibilities)
    half_rows = keep.shape[1]
    held = (keep + swap(send, lambda f, q: (f, q ^ 1)))[None]
    for k in range(facet_total.bit_length() - 1):
        even, odd = (k, k ^ 1) if k < 2 else (k, k)
        parts = held.reshape(held.shape[0], -1, 2, half_rows, 128)
        kept, sent = parts[:, :, 0], parts[:, :, 1]
        came = swap(sent, lambda f, q: (f ^ (1 << (odd if q & 1 else even)), q))
        bit = jnp.where(band_index & 1 == 1, odd, even)
        other = ((owners ^ facet_index) >> bit & 1) == 1
        held = jnp.where(other[:, None, None, None], came, kept)
    held = held.reshape(2, half_rows, 128)
    for k in range(1, band_total.bit_length() - 1):
        held = held + swap(held, lambda f, q: (f, q ^ (1 << k)))
    other = swap(held, lambda f, q: (f, q ^ 1))
    return image_blocks(owners, corners, assign, counts, held, other, channel_total, visibilities.shape[4])


def solution(mesh):
    placed = (
        P("facet", None, None, "freq", None),
        P("facet", None, None, None),
        P(),
        P(),
        P("facet", None),
        P("facet"),
    )
    return jax.shard_map(
        on_device, mesh=mesh, in_specs=placed, out_specs=P("facet", "freq", None), check_vma=False
    )
```

time: 453 us -> 56.4 us (0.12)
  waiting for transfers between devices: 269 us -> 16.8 us
  other arithmetic: 51.8 us -> 0.99 us
  blocking collectives: 39.2 us -> 0 us
  loops' own time: 30.8 us -> 0 us
  starting transfers between devices: 0.04 us -> 30.3 us
  matrix products: 23.2 us -> 0 us
  local copies, waits for them, and re-layouts: 20.6 us -> 3.1 us
  between operations: 15.6 us -> 0.76 us
    psum x2 -> x0, waiting for transfers between devices: 269 us -> none  [the longest x1 237 us: on_device(): summed = lax.psum(uv_grid, 'freq')]
    psum x1 -> x0, blocking collectives: 39.2 us -> none  [spread(): return lax.psum(kept, axis)]
    another operation x1 -> x0, other arithmetic: 31.2 us -> none
    another operation x1 -> x0, loops' own time: 30.8 us -> none  [grid_items(): return lax.fori_loop(0, batch_total, grid_step, initial)]
    ppermute x0 -> x6, starting transfers between devices: none -> 30.3 us  [swap(): return lax.ppermute(value, ('facet', 'freq'), pairs)]
    dot_general x15 -> x0, matrix products: 23.2 us -> none  [the longest x1 5.52 us: on_device(): jnp.dot(half_imag, sin_table, precision=highest, preferred_element_type=j...]
    ppermute x0 -> x6, waiting for transfers between devices: none -> 16.8 us  [swap(): return lax.ppermute(value, ('facet', 'freq'), pairs)]
    dynamic_update_slice x8 -> x0, local copies, waits for them, and re-layouts: 10.1 us -> none  [add_pieces(): lax.dynamic_update_slice(uv_grid, current + pieces[item] * weights[item],...]
  transfers between devices with their start and end apart: 2 -> 6, of which waited for: 2 -> 6; matrix products, arithmetic and copies ran while one was open for 2% -> 1% of each run, Pallas kernels for 0% -> 0%
where the time goes in v1:
time: 56.4 us; the launch traced here: 56.1 us
  starting transfers between devices  30.3 us (54%)
  waiting for transfers between devices  16.8 us (30%)
  Pallas kernels  4.15 us (7%)
  local copies, waits for them, and re-layouts  3.1 us (5%)
  other arithmetic  0.99 us (2%)
  between operations  0.76 us (1%)
    ppermute x6, starting transfers between devices, swap(): return lax.ppermute(value, ('facet', 'freq'), pairs)  30.3 us
    ppermute x6, waiting for transfers between devices, swap(): return lax.ppermute(value, ('facet', 'freq'), pairs)  16.8 us
    pallas_call x1, Pallas kernels, image_blocks(): pl.pallas_call(image_kernel, grid_spec=pltpu.PrefetchScalarGridSpec(num_s...  3.1 us
    unnamed x17, local copies, waits for them, and re-layouts  3.06 us
  transfers between devices with their start and end apart: 6, of which 6 were waited for; matrix products, arithmetic and copies ran while one was open for 1% of the time, Pallas kernels for 0%

profile of v1, /device:TPU:0, one launch (start us, length us, event | category | flops | bytes accessed | tf_op | source)
XLA Modules:
  0.0 56.1 jit_solution(3868525048623775160)
XLA Ops:
  0.0 0.7 %copy.10.coords_ref = f32[1,10,3,128]{3,2,1,0:T(4,128)S(1)} copy(f32[1,10,3,128]{3,0,2,1:T(1,128)} %param.9) | data formatting | bytes 30720 | tf_op args[1]
  0.7 0.0 copy-start.1
  0.7 1.0 %copy-done.1 = f32[1,10,2,32,128]{4,3,2,1,0:T(8,128)S(1)} copy-done((f32[1,10,2,32,128]{4,3,2,1,0:T(8,128)S(1)}, f32[1,10,2,32,128]{4,3,2,1,0:T(8,128)}, u32[]{:S(2)}) %copy-start.1) | copy-done | bytes 327704
  1.7 0.0 copy-start.3
  1.7 0.7 %copy-done.3 = s32[2,8,10]{2,1,0:T(8,128)S(1)} copy-done((s32[2,8,10]{2,1,0:T(8,128)S(1)}, s32[2,8,10]{2,1,0:T(8,128)}, u32[]{:S(2)}) %copy-start.3) | copy-done | bytes 664
  2.4 0.0 copy-start.5
  2.4 0.7 %copy-done.5 = s32[2]{0:T(128)S(1)} copy-done((s32[2]{0:T(128)S(1)}, s32[2]{0:T(128)}, u32[]{:S(2)}) %copy-start.5) | copy-done | bytes 32
  3.1 0.0 copy-start.7
  3.1 1.0 %grid_blocks.1 = (f32[8,80,128]{2,1,0:T(8,128)S(1)}, f32[8,80,128]{2,1,0:T(8,128)S(1)}) custom-call(s32[2]{0:T(128)S(1)} %copy-done.5, s32[2,8,10]{2,1,0:T(8,128)S(1)} %copy-done.3, f32[1,10,3,128]{3,2,1,0:T(4,128)S(1)} %copy.10.coords_ref, f32[1,10,2,32,128]{4,3,2,1,0:T(8,128)S(1)} %copy-done.1), custom_call_target="tpu_custom_call" | custom-call | tf_op jit(solution)/shard_map/grid_blocks/pallas_call | solution.py:162
  4.1 0.5 collective-permute-start
  4.6 1.3 %collective-permute-done = f32[8,80,128]{2,1,0:T(8,128)S(1)} collective-permute-done((f32[8,80,128]{2,1,0:T(8,128)S(1)}, f32[8,80,128]{2,1,0:T(8,128)S(1)}, u32[]{:S(2)}, u32[]{:S(2)}) %collective-permute-start) | collective-permute-done | bytes 327712 | tf_op jit(solution)/shard_map/ppermute | solution.py:318
  5.9 0.1 add.15
  6.0 25.9 %collective-permute-start.1 = (f32[1,4,80,128]{3,2,1,0:T(8,128)S(1)}, f32[1,4,80,128]{3,2,1,0:T(8,128)S(1)}, u32[]{:S(2)}, u32[]{:S(2)}) collective-permute-start(f32[1,4,80,128]{3,2,1,0:T(8,128)S(1)} %get-tuple-element.9), channel_id=1, source_target_pairs={{0,4},{1,9},{2,6},{3,11},{4,0},{5,13},{6,2},{7,15},{8,12},{9,1},{1... | collective-permute-start | bytes 491528 | tf_op jit(solution)/shard_map/ppermute | solution.py:318
  31.9 0.7 %and_compare_fusion.2 = (pred[2]{0:T(512)(128)(4,1)S(1)}, pred[2]{0:T(512)(128)(4,1)S(1)}, pred[2]{0:T(512)(128)(4,1)S(1)}) fusion(s32[2]{0:T(128)} %owners_ref.3, s32[]{:T(128)S(6)} %axis_index.15, s32[]{:T(128)S(6)} %select_n.29, s32[]{:T(128)S(6)} %select_n.30), kind=kLoop, calls=%fused_computation.12 | loop fusion | flops 20 | bytes 26 | tf_op jit(solution)/shard_map/eq | solution.py:334
  32.5 2.6 %collective-permute-done.1 = f32[1,4,80,128]{3,2,1,0:T(8,128)S(1)} collective-permute-done((f32[1,4,80,128]{3,2,1,0:T(8,128)S(1)}, f32[1,4,80,128]{3,2,1,0:T(8,128)S(1)}, u32[]{:S(2)}, u32[]{:S(2)}) %collective-permute-start.1) | collective-permute-done | bytes 163872 | tf_op jit(solution)/shard_map/ppermute | solution.py:318
  35.2 0.1 broadcast_select_fusion
  35.3 0.1 collective-permute-start.2
  35.4 5.3 %collective-permute-done.2 = f32[2,2,80,128]{3,2,0,1:T(8,128)S(1)} collective-permute-done((f32[2,2,80,128]{3,2,0,1:T(8,128)S(1)}, f32[2,2,80,128]{3,2,0,1:T(8,128)S(1)}, u32[]{:S(2)}, u32[]{:S(2)}) %collective-permute-start.2) | collective-permute-done | bytes 163872 | tf_op jit(solution)/shard_map/ppermute | solution.py:318
  40.7 0.1 fusion.1
  40.8 2.2 %collective-permute-start.3 = (f32[2,1,80,128]{3,2,0,1:T(8,128)S(1)}, f32[2,1,80,128]{3,2,0,1:T(8,128)S(1)}, u32[]{:S(2)}, u32[]{:S(2)}) collective-permute-start(f32[2,1,80,128]{3,2,0,1:T(8,128)S(1)} %slice_bitcast_fusion.4), channel_id=1, source_target_pairs={{0,16},{1,17},{2,18},{3,19},{4,20},{5,21},{6,22},{7,23},{8,24},{9,... | collective-permute-start | bytes 245768 | tf_op jit(solution)/shard_map/ppermute | solution.py:318
  43.0 4.1 %collective-permute-done.3 = f32[2,1,80,128]{3,2,0,1:T(8,128)S(1)} collective-permute-done((f32[2,1,80,128]{3,2,0,1:T(8,128)S(1)}, f32[2,1,80,128]{3,2,0,1:T(8,128)S(1)}, u32[]{:S(2)}, u32[]{:S(2)}) %collective-permute-start.3) | collective-permute-done | bytes 81952 | tf_op jit(solution)/shard_map/ppermute | solution.py:318
  47.1 0.1 fusion.3
  47.1 1.5 %collective-permute-start.4 = (f32[2,80,128]{2,1,0:T(8,128)S(1)}, f32[2,80,128]{2,1,0:T(8,128)S(1)}, u32[]{:S(2)}, u32[]{:S(2)}) collective-permute-start(f32[2,80,128]{2,1,0:T(8,128)S(1)} %fusion.3), channel_id=1, source_target_pairs={{0,2},{1,3},{2,0},{3,1},{4,6},{5,7},{6,4},{7,5},{8,10},{9,11},{10,... | collective-permute-start | bytes 245768 | tf_op jit(solution)/shard_map/ppermute | solution.py:318
  48.7 2.9 %collective-permute-done.4 = f32[2,80,128]{2,1,0:T(8,128)S(1)} collective-permute-done((f32[2,80,128]{2,1,0:T(8,128)S(1)}, f32[2,80,128]{2,1,0:T(8,128)S(1)}, u32[]{:S(2)}, u32[]{:S(2)}) %collective-permute-start.4) | collective-permute-done | bytes 81952 | tf_op jit(solution)/shard_map/ppermute | solution.py:318
  51.6 0.1 collective-permute-start.5
  52.4 0.6 %collective-permute-done.5.other_ref = f32[2,80,128]{2,1,0:T(8,128)S(1)} collective-permute-done((f32[2,80,128]{2,1,0:T(8,128)S(1)}, f32[2,80,128]{2,1,0:T(8,128)S(1)}, u32[]{:S(2)}, u32[]{:S(2)}) %collective-permute-start.5) | collective-permute-done | bytes 81952 | tf_op jit(solution)/shard_map/ppermute | solution.py:318
  53.0 0.0 copy-done
  53.0 0.0 copy-done.2
  53.0 0.0 copy-done.4
  53.0 0.0 copy-done.6
  53.0 0.0 copy-done.7
  53.0 3.1 %image_blocks.1 = f32[1,128,512]{2,1,0:T(8,128)} custom-call(s32[1]{0:T(128)} %bitcast.table_ref, s32[2]{0:T(128)S(1)} %copy-done.6, s32[2,8,10]{2,1,0:T(8,128)S(1)} %copy-done.4, s32[1,20]{1,0:T(1,128)S(1)} %copy-done.7, s32[1]{0:T(128)S(6)} %copy.21.counts_ref, f32[2,80,128]{2,1,0:T(8,128)S(1)} %add.16.own_ref, ...), custom_call_target="tpu_custom_call" | custom-call | tf_op jit(solution)/shard_map/image_blocks/pallas_call | solution.py:282
  (8 shorter events, 0.1 us)
Async XLA Ops:
  0.7 1.0 %copy-start.1 = (f32[1,10,2,32,128]{4,3,2,1,0:T(8,128)S(1)}, f32[1,10,2,32,128]{4,3,2,1,0:T(8,128)}, u32[]{:S(2)}) copy-start(f32[1,10,2,32,128]{4,3,2,1,0:T(8,128)} %vis_ref.1) | copy-start | bytes 983044
  1.7 0.7 %copy-start.3 = (s32[2,8,10]{2,1,0:T(8,128)S(1)}, s32[2,8,10]{2,1,0:T(8,128)}, u32[]{:S(2)}) copy-start(s32[2,8,10]{2,1,0:T(8,128)} %corners_ref.3) | copy-start | bytes 1924
  2.4 0.7 %copy-start.5 = (s32[2]{0:T(128)S(1)}, s32[2]{0:T(128)}, u32[]{:S(2)}) copy-start(s32[2]{0:T(128)} %owners_ref.3) | copy-start | bytes 28
  3.0 49.9 %copy-start = (f32[8,128,512]{2,1,0:T(8,128)S(1)}, f32[8,128,512]{2,1,0:T(8,128)}, u32[]{:S(2)}) copy-start(f32[8,128,512]{2,1,0:T(8,128)} %constant.35.clone.first_ref) | copy-start | bytes 6291460
  3.0 49.9 %copy-start.2 = (f32[4,16,512]{2,1,0:T(8,128)S(1)}, f32[4,16,512]{2,1,0:T(8,128)}, u32[]{:S(2)}) copy-start(f32[4,16,512]{2,1,0:T(8,128)} %constant.36.clone.second_ref) | copy-start | bytes 393220
  3.0 49.9 %copy-start.4 = (s32[2,8,10]{2,1,0:T(8,128)S(1)}, s32[2,8,10]{2,1,0:T(8,128)}, u32[]{:S(2)}) copy-start(s32[2,8,10]{2,1,0:T(8,128)} %corners_ref.3) | copy-start | bytes 1924
  3.1 49.9 %copy-start.6 = (s32[2]{0:T(128)S(1)}, s32[2]{0:T(128)}, u32[]{:S(2)}) copy-start(s32[2]{0:T(128)} %owners_ref.3) | copy-start | bytes 28
  3.1 49.9 %copy-start.7 = (s32[1,20]{1,0:T(1,128)S(1)}, s32[1,20]{1,0:T(1,128)}, u32[]{:S(2)}) copy-start(s32[1,20]{1,0:T(1,128)} %assign_ref.1) | copy-start | bytes 244
  4.1 1.8 %collective-permute-start = (f32[8,80,128]{2,1,0:T(8,128)S(1)}, f32[8,80,128]{2,1,0:T(8,128)S(1)}, u32[]{:S(2)}, u32[]{:S(2)}) collective-permute-start(f32[8,80,128]{2,1,0:T(8,128)S(1)} %get-tuple-element.8), channel_id=1, source_target_pairs={{0,1},{1,0},{2,3},{3,2},{4,5},{5,4},{6,7},{7,6},{8,9},{9,8},{10,11... | collective-permute-start | bytes 983048 | tf_op jit(solution)/shard_map/ppermute | solution.py:318
  6.0 29.2 %collective-permute-start.1 = (f32[1,4,80,128]{3,2,1,0:T(8,128)S(1)}, f32[1,4,80,128]{3,2,1,0:T(8,128)S(1)}, u32[]{:S(2)}, u32[]{:S(2)}) collective-permute-start(f32[1,4,80,128]{3,2,1,0:T(8,128)S(1)} %get-tuple-element.9), channel_id=1, source_target_pairs={{0,4},{1,9},{2,6},{3,11},{4,0},{5,13},{6,2},{7,15},{8,12},{9,1},{1... | collective-permute-start | bytes 491528 | tf_op jit(solution)/shard_map/ppermute | solution.py:318
  35.3 5.4 %collective-permute-start.2 = (f32[2,2,80,128]{3,2,0,1:T(8,128)S(1)}, f32[2,2,80,128]{3,2,0,1:T(8,128)S(1)}, u32[]{:S(2)}, u32[]{:S(2)}) collective-permute-start(f32[2,2,80,128]{3,2,0,1:T(8,128)S(1)} %slice_bitcast_fusion.1), channel_id=1, source_target_pairs={{0,8},{1,5},{2,10},{3,7},{4,12},{5,1},{6,14},{7,3},{8,0},{9,13},{1... | collective-permute-start | bytes 491528 | tf_op jit(solution)/shard_map/ppermute | solution.py:318
  40.8 6.3 %collective-permute-start.3 = (f32[2,1,80,128]{3,2,0,1:T(8,128)S(1)}, f32[2,1,80,128]{3,2,0,1:T(8,128)S(1)}, u32[]{:S(2)}, u32[]{:S(2)}) collective-permute-start(f32[2,1,80,128]{3,2,0,1:T(8,128)S(1)} %slice_bitcast_fusion.4), channel_id=1, source_target_pairs={{0,16},{1,17},{2,18},{3,19},{4,20},{5,21},{6,22},{7,23},{8,24},{9,... | collective-permute-start | bytes 245768 | tf_op jit(solution)/shard_map/ppermute | solution.py:318
  47.1 4.4 %collective-permute-start.4 = (f32[2,80,128]{2,1,0:T(8,128)S(1)}, f32[2,80,128]{2,1,0:T(8,128)S(1)}, u32[]{:S(2)}, u32[]{:S(2)}) collective-permute-start(f32[2,80,128]{2,1,0:T(8,128)S(1)} %fusion.3), channel_id=1, source_target_pairs={{0,2},{1,3},{2,0},{3,1},{4,6},{5,7},{6,4},{7,5},{8,10},{9,11},{10,... | collective-permute-start | bytes 245768 | tf_op jit(solution)/shard_map/ppermute | solution.py:318
  51.6 1.3 %collective-permute-start.5 = (f32[2,80,128]{2,1,0:T(8,128)S(1)}, f32[2,80,128]{2,1,0:T(8,128)S(1)}, u32[]{:S(2)}, u32[]{:S(2)}) collective-permute-start(f32[2,80,128]{2,1,0:T(8,128)S(1)} %add.16.own_ref), channel_id=1, source_target_pairs={{0,1},{1,0},{2,3},{3,2},{4,5},{5,4},{6,7},{7,6},{8,9},{9,8},{10,11... | collective-permute-start | bytes 245768 | tf_op jit(solution)/shard_map/ppermute | solution.py:318

commit v2 on v1

--- a/solution.py
+++ b/solution.py
@@ -12,6 +12,8 @@
 G = 512
 HALF = SUB // 2
 COLUMNS = 8
+ROWS, BASE = 24, 40
+PAD = 16
 
 two_pi = 2.0 * math.pi
 field_width = 0.02
@@ -44,7 +46,8 @@
 
 
 def grid_kernel(
-    owners_ref, corners_ref, coords_ref, vis_ref, keep_ref, send_ref, z_ref, base_ref, step_ref, left_ref, right_ref
+    owners_hbm, corners_hbm, coords_hbm, vis_hbm, keep_ref, send_ref,
+    owners_ref, corners_ref, coords_ref, vis_ref, small_sems, vis_sems, z_ref, base_ref, left_ref, right_ref,
 ):
     me = lax.axis_index("facet")
     band = lax.axis_index("freq")
@@ -53,18 +56,39 @@
     core = band & 1
     facet_row = pl.program_id(0)
     block = pl.program_id(1)
-    channels, lanes = vis_ref.shape[3], vis_ref.shape[4]
-    half_blocks = pl.num_programs(1) // 2
-
-    @pl.when(jnp.logical_or(owners_ref[0] == me, owners_ref[1] == me))
+    blocks = pl.num_programs(1)
+    channels, lanes = vis_ref.shape[2], vis_ref.shape[3]
+    half_blocks = blocks // 2
+
+    small = [
+        pltpu.make_async_copy(source, target, small_sems.at[k])
+        for k, (source, target) in enumerate(
+            ((owners_hbm, owners_ref), (corners_hbm, corners_ref), (coords_hbm, coords_ref))
+        )
+    ]
+    large = [pltpu.make_async_copy(vis_hbm.at[0, b], vis_ref.at[b], vis_sems.at[b]) for b in range(vis_ref.shape[0])]
+
+    @pl.when((facet_row == 0) & (block == 0))
     def _():
+        for copy in small + large:
+            copy.start()
+        for copy in small:
+            copy.wait()
+
+    for b, copy in enumerate(large):
+
+        @pl.when((facet_row == 0) & (block == b))
+        def _():
+            copy.wait()
+
+    def build():
         corner_u = corners_ref[0, me, block]
         corner_v = corners_ref[1, me, block]
         channel = (band * channels + lax.broadcasted_iota(jnp.int32, (channels, lanes), 0)).astype(jnp.float32)
         ratio = 1.0 + band_spread * channel / (channels * band_total)
-        u_cells = coords_ref[0, 0, 0:1, :] * ratio
-        v_cells = coords_ref[0, 0, 1:2, :] * ratio
-        w_waves = coords_ref[0, 0, 2:3, :] * ratio
+        u_cells = coords_ref[block, 0] * ratio
+        v_cells = coords_ref[block, 1] * ratio
+        w_waves = coords_ref[block, 2] * ratio
         shift_u = centre_shift - corner_u
         delta_u = u_cells + shift_u.astype(jnp.float32)
         delta_v = v_cells + (centre_shift - corner_v).astype(jnp.float32)
@@ -73,65 +97,65 @@
         common = (
             v_cells * row_pos - (delta_u + delta_v) * (0.5 / SUB) + 0.5 * (shift_u & 1).astype(jnp.float32)
         )
-        vis = (vis_ref[0, 0, 0], vis_ref[0, 0, 1])
+        vis = (vis_ref[block, 0], vis_ref[block, 1])
         for g in range(COLUMNS // 2):
             radius = field_width * field_width * ((g + 0.5) ** 2 + row_vec * row_vec)
             w_shift = (-radius / (1.0 + jnp.sqrt(1.0 - radius)))[0:1]
             turned = times(vis, cos_sin(common + w_waves * w_shift))
-            z_ref[2 * g] = turned[0]
-            z_ref[2 * g + 1] = turned[1]
+            z_ref[pl.ds(2 * g, channels, stride=ROWS), :] = turned[0]
+            z_ref[pl.ds(2 * g + 1, channels, stride=ROWS), :] = turned[1]
         for axis, delta in enumerate((delta_u, delta_v)):
             wave = cos_sin(delta * (0.5 / SUB))
             step = times(wave, wave)
             for j in range(8):
-                base_ref[2 * axis, pl.ds(j, channels, stride=8), :] = wave[0]
-                base_ref[2 * axis + 1, pl.ds(j, channels, stride=8), :] = wave[1]
+                base_ref[pl.ds(16 * axis + j, channels, stride=BASE), :] = wave[0]
+                base_ref[pl.ds(16 * axis + 8 + j, channels, stride=BASE), :] = wave[1]
                 if j < 7:
                     wave = times(wave, step)
             for _ in range(3):
                 step = times(step, step)
-            step_ref[2 * axis] = step[0]
-            step_ref[2 * axis + 1] = step[1]
-
-        chunk = channels // 4
+            z_ref[pl.ds(COLUMNS + 2 * axis, channels, stride=ROWS), :] = step[0]
+            z_ref[pl.ds(COLUMNS + 2 * axis + 1, channels, stride=ROWS), :] = step[1]
+        for c in range(channels):
+
+            def row_of(k):
+                return z_ref[ROWS * c + k : ROWS * c + k + 1, :]
+
+            def base_of(k):
+                return base_ref[BASE * c + 8 * k : BASE * c + 8 * k + 8, :]
+
+            step = (row_of(COLUMNS), row_of(COLUMNS + 1))
+            twice = 2.0 * step[0]
+            wave = (base_of(0), base_of(1))
+            after = times(wave, step)
+            for i in range(COLUMNS):
+                for part in range(2):
+                    left_ref[c, 128 * part + 16 * i : 128 * part + 16 * i + 16] = jnp.concatenate(
+                        [wave[part], after[part]], axis=0
+                    ).astype(jnp.bfloat16)
+                if i < COLUMNS - 1:
+                    wave = tuple(twice * after[part] - wave[part] for part in range(2))
+                    after = tuple(twice * wave[part] - after[part] for part in range(2))
+            step = (row_of(COLUMNS + 2), row_of(COLUMNS + 3))
+            wave = (base_of(2), base_of(3))
+            after = times(wave, step)
+            both = tuple(jnp.concatenate([wave[part], after[part]], axis=0) for part in range(2))
+            for g in range(COLUMNS // 2):
+                for part in range(2):
+                    turned = row_of(2 * g + part)
+                    for kind in range(2):
+                        row = 64 * g + 32 * part + 16 * kind
+                        right_ref[c, row : row + 16] = (turned * both[kind]).astype(jnp.bfloat16)
+
+    def finish():
         product = None
-        for first in range(0, channels, chunk):
-            for c in range(first, first + chunk):
-                at = slice(c * lanes, (c + 1) * lanes)
-                step = (step_ref[0, c : c + 1, :], step_ref[1, c : c + 1, :])
-                twice = 2.0 * step[0]
-                wave = (base_ref[0, 8 * c : 8 * c + 8, :], base_ref[1, 8 * c : 8 * c + 8, :])
-                after = times(wave, step)
-                for i in range(COLUMNS):
-                    for part in range(2):
-                        left_ref[128 * part + 16 * i : 128 * part + 16 * i + 16, at] = jnp.concatenate(
-                            [wave[part], after[part]], axis=0
-                        ).astype(jnp.bfloat16)
-                    if i < COLUMNS - 1:
-                        wave = tuple(twice * after[part] - wave[part] for part in range(2))
-                        after = tuple(twice * wave[part] - after[part] for part in range(2))
-                step = (step_ref[2, c : c + 1, :], step_ref[3, c : c + 1, :])
-                wave = (base_ref[2, 8 * c : 8 * c + 8, :], base_ref[3, 8 * c : 8 * c + 8, :])
-                after = times(wave, step)
-                both = tuple(jnp.concatenate([wave[part], after[part]], axis=0) for part in range(2))
-                for g in range(COLUMNS // 2):
-                    for part in range(2):
-                        turned = z_ref[2 * g + part, c : c + 1, :]
-                        for kind in range(2):
-                            row = 64 * g + 32 * part + 16 * kind
-                            right_ref[row : row + 16, at] = (turned * both[kind]).astype(jnp.bfloat16)
-            at = slice(first * lanes, (first + chunk) * lanes)
-            term = lax.dot_general(
-                right_ref[:, at],
-                left_ref[:, at],
-                (((1,), (1,)), ((), ())),
-                preferred_element_type=jnp.float32,
-            )
+        for c in range(0, channels, 2):
+            right = jnp.concatenate([right_ref[c, 0:256], right_ref[c + 1, 0:256]], axis=1)
+            left = jnp.concatenate([left_ref[c, 0:256], left_ref[c + 1, 0:256]], axis=1)
+            term = lax.dot_general(right, left, (((1,), (1,)), ((), ())), preferred_element_type=jnp.float32)
             product = term if product is None else product + term
-
         group = lax.broadcasted_iota(jnp.int32, (HALF, 128), 1) // SUB
-        half = block // half_blocks
-        row = pl.multiple_of((block - half * half_blocks) * HALF, HALF)
+        tiles = []
         for sign in (1, -1):
             for g in range(COLUMNS // 2):
                 part = [product[64 * g + 16 * k : 64 * g + 16 * k + 16] for k in range(4)]
@@ -142,16 +166,27 @@
                     moved = kinds[t] if t == g else pltpu.roll(kinds[t], SUB * ((t - g) % 4), 1)
                     tile = moved if tile is None else jnp.where(group == t, moved, tile)
                 facet = facet_row * COLUMNS + (COLUMNS // 2 + g if sign == 1 else COLUMNS // 2 - 1 - g)
-                straight = facet ^ me
-                crossed = swap_low(straight)
-
-                @pl.when(half == core)
-                def _():
-                    keep_ref[jnp.where(core == 1, crossed, straight), pl.ds(row, HALF), :] = tile
-
-                @pl.when(half != core)
-                def _():
-                    send_ref[jnp.where(core == 0, crossed, straight), pl.ds(row, HALF), :] = tile
+                tiles.append((facet ^ me, tile))
+        return tiles
+
+    def store(tiles):
+        half = block // half_blocks
+        row = pl.multiple_of((block - half * half_blocks) * HALF, HALF)
+
+        @pl.when(half == core)
+        def _():
+            for place, tile in tiles:
+                keep_ref[jnp.where(core == 1, swap_low(place), place), pl.ds(row, HALF), :] = tile
+
+        @pl.when(half != core)
+        def _():
+            for place, tile in tiles:
+                send_ref[jnp.where(core == 0, swap_low(place), place), pl.ds(row, HALF), :] = tile
+
+    @pl.when(jnp.logical_or(owners_ref[0] == me, owners_ref[1] == me))
+    def _():
+        build()
+        store(finish())
 
 
 def grid_blocks(owners, corners, coords, visibilities):
@@ -162,24 +197,24 @@
     return pl.pallas_call(
         grid_kernel,
         grid=(facet_total // COLUMNS, blocks),
-        in_specs=[
-            pl.BlockSpec(memory_space=pltpu.SMEM),
-            pl.BlockSpec(memory_space=pltpu.SMEM),
-            pl.BlockSpec((1, 1, 3, lanes), lambda r, b: (0, b, 0, 0)),
-            pl.BlockSpec((1, 1, 2, channels, lanes), lambda r, b: (0, b, 0, 0, 0)),
+        in_specs=[pl.BlockSpec(memory_space=pltpu.HBM)] * 4,
+        out_specs=[pl.BlockSpec(out.shape, lambda r, b: (0, 0, 0))] * 2,
+        scratch_shapes=[
+            pltpu.SMEM(owners.shape, jnp.int32),
+            pltpu.SMEM(corners.shape, jnp.int32),
+            pltpu.VMEM((blocks, 3, 1, lanes), jnp.float32),
+            pltpu.VMEM((blocks, 2, channels, lanes), jnp.float32),
+            pltpu.SemaphoreType.DMA((3,)),
+            pltpu.SemaphoreType.DMA((blocks,)),
+            pltpu.VMEM((ROWS * channels, lanes), jnp.float32),
+            pltpu.VMEM((BASE * channels, lanes), jnp.float32),
+            pltpu.VMEM((channels, 256 + PAD, lanes), jnp.bfloat16),
+            pltpu.VMEM((channels, 256 + PAD, lanes), jnp.bfloat16),
         ],
-        out_specs=[pl.BlockSpec(out.shape, lambda r, b: (0, 0, 0))] * 2,
         out_shape=[out, out],
-        scratch_shapes=[
-            pltpu.VMEM((COLUMNS, channels, lanes), jnp.float32),
-            pltpu.VMEM((4, 8 * channels, lanes), jnp.float32),
-            pltpu.VMEM((4, channels, lanes), jnp.float32),
-            pltpu.VMEM((256, channels * lanes), jnp.bfloat16),
-            pltpu.VMEM((256, channels * lanes), jnp.bfloat16),
-        ],
-        compiler_params=pltpu.CompilerParams(vmem_limit_bytes=48 * 1024 * 1024),
+        compiler_params=pltpu.CompilerParams(vmem_limit_bytes=62 * 1024 * 1024),
         name="grid_blocks",
-    )(owners, corners, coords, visibilities)
+    )(owners, corners, coords.reshape(blocks, 3, 1, lanes), visibilities)
 
 
 def image_tables(band_total, scale):

time: 56.4 us -> 47.1 us (0.84)
  starting transfers between devices: 30.3 us -> 7.15 us
  Pallas kernels: 4.15 us -> 19.7 us
  local copies, waits for them, and re-layouts: 3.1 us -> 0.07 us
  other arithmetic: 0.99 us -> 1.93 us
    ppermute x6, starting transfers between devices: 30.3 us -> 7.15 us  [swap(): return lax.ppermute(value, ('facet', 'freq'), pairs)]
    pallas_call x1, Pallas kernels: 1.05 us -> 16.6 us  [grid_blocks(): pl.pallas_call(grid_kernel, grid=(facet_total // COLUMNS, blocks), in_spe...]
    unnamed x17 -> x10, local copies, waits for them, and re-layouts: 3.06 us -> 0.02 us
    add x1, other arithmetic: 0.06 us -> 1.01 us  [on_device(): held = (keep + swap(send, lambda f, q: (f, q ^ 1)))[None]]
where the time goes in v2:
time: 47.1 us; the launch traced here: 46.8 us
  Pallas kernels  19.7 us (42%)
  waiting for transfers between devices  17.2 us (37%)
  starting transfers between devices  7.15 us (15%)
  other arithmetic  1.93 us (4%)
  between operations  0.77 us (2%)
    ppermute x6, waiting for transfers between devices, swap(): return lax.ppermute(value, ('facet', 'freq'), pairs)  17.2 us
    pallas_call x1, Pallas kernels, grid_blocks(): pl.pallas_call(grid_kernel, grid=(facet_total // COLUMNS, blocks), in_spe...  16.6 us
    ppermute x6, starting transfers between devices, swap(): return lax.ppermute(value, ('facet', 'freq'), pairs)  7.15 us
    pallas_call x1, Pallas kernels, image_blocks(): pl.pallas_call(image_kernel, grid_spec=pltpu.PrefetchScalarGridSpec(num_s...  3.1 us
    add x1, other arithmetic, on_device(): held = (keep + swap(send, lambda f, q: (f, q ^ 1)))[None]  1.01 us
  transfers between devices with their start and end apart: 6, of which 6 were waited for; matrix products, arithmetic and copies ran while one was open for 1% of the time, Pallas kernels for 0%

profile of v2, /device:TPU:0, one launch (start us, length us, event | category | flops | bytes accessed | tf_op | source)
XLA Modules:
  0.0 46.8 jit_solution(762943296731291651)
XLA Ops:
  0.0 0.0 copy-start.1
  0.0 0.0 copy-start.2
  0.0 0.0 copy-start.3
  0.0 0.0 copy-start.4
  0.0 16.6 %grid_blocks.1 = (f32[8,80,128]{2,1,0:T(8,128)}, f32[8,80,128]{2,1,0:T(8,128)}) custom-call(s32[2]{0:T(128)} %owners_ref.1, s32[2,8,10]{2,1,0:T(8,128)} %corners_ref.1, f32[10,3,1,128]{3,2,1,0:T(1,128)} %bitcast.34, f32[1,10,2,32,128]{4,3,2,1,0:T(8,128)} %vis_hbm.1), custom_call_target="tpu_custom_call" | custom-call | tf_op jit(solution)/shard_map/grid_blocks/pallas_call | solution.py:197
  16.6 0.0 copy-start
  16.6 0.5 %collective-permute-start = (f32[8,80,128]{2,1,0:T(8,128)}, f32[8,80,128]{2,1,0:T(8,128)S(1)}, u32[]{:S(2)}, u32[]{:S(2)}) collective-permute-start(f32[8,80,128]{2,1,0:T(8,128)} %get-tuple-element.8), channel_id=1, source_target_pairs={{0,1},{1,0},{2,3},{3,2},{4,5},{5,4},{6,7},{7,6},{8,9},{9,8},{10,11... | collective-permute-start | bytes 983048 | tf_op jit(solution)/shard_map/ppermute | solution.py:353
  17.2 1.5 %collective-permute-done = f32[8,80,128]{2,1,0:T(8,128)S(1)} collective-permute-done((f32[8,80,128]{2,1,0:T(8,128)}, f32[8,80,128]{2,1,0:T(8,128)S(1)}, u32[]{:S(2)}, u32[]{:S(2)}) %collective-permute-start) | collective-permute-done | bytes 327712 | tf_op jit(solution)/shard_map/ppermute | solution.py:353
  18.7 1.0 %add.15 = f32[8,80,128]{2,1,0:T(8,128)S(1)} add(f32[8,80,128]{2,1,0:T(8,128)} %get-tuple-element.7, f32[8,80,128]{2,1,0:T(8,128)S(1)} %collective-permute-done) | non-fusion elementwise | flops 81920 | bytes 983040 | tf_op jit(solution)/shard_map/add | solution.py:362
  19.7 0.1 collective-permute-start.1
  19.8 0.7 %and_compare_fusion.2 = (pred[2]{0:T(512)(128)(4,1)S(1)}, pred[2]{0:T(512)(128)(4,1)S(1)}, pred[2]{0:T(512)(128)(4,1)S(1)}) fusion(s32[2]{0:T(128)} %owners_ref.1, s32[]{:T(128)S(6)} %axis_index.15, s32[]{:T(128)S(6)} %select_n.29, s32[]{:T(128)S(6)} %select_n.30), kind=kLoop, calls=%fused_computation.12 | loop fusion | flops 20 | bytes 26 | tf_op jit(solution)/shard_map/eq | solution.py:369
  20.4 4.6 %collective-permute-done.1 = f32[1,4,80,128]{3,2,1,0:T(8,128)S(1)} collective-permute-done((f32[1,4,80,128]{3,2,1,0:T(8,128)S(1)}, f32[1,4,80,128]{3,2,1,0:T(8,128)S(1)}, u32[]{:S(2)}, u32[]{:S(2)}) %collective-permute-start.1) | collective-permute-done | bytes 163872 | tf_op jit(solution)/shard_map/ppermute | solution.py:353
  25.1 0.1 broadcast_select_fusion
  25.2 0.1 collective-permute-start.2
  25.3 5.3 %collective-permute-done.2 = f32[2,2,80,128]{3,2,0,1:T(8,128)S(1)} collective-permute-done((f32[2,2,80,128]{3,2,0,1:T(8,128)S(1)}, f32[2,2,80,128]{3,2,0,1:T(8,128)S(1)}, u32[]{:S(2)}, u32[]{:S(2)}) %collective-permute-start.2) | collective-permute-done | bytes 163872 | tf_op jit(solution)/shard_map/ppermute | solution.py:353
  30.6 0.1 fusion.1
  30.7 3.0 %collective-permute-start.3 = (f32[2,1,80,128]{3,2,0,1:T(8,128)S(1)}, f32[2,1,80,128]{3,2,0,1:T(8,128)S(1)}, u32[]{:S(2)}, u32[]{:S(2)}) collective-permute-start(f32[2,1,80,128]{3,2,0,1:T(8,128)S(1)} %slice_bitcast_fusion.4), channel_id=1, source_target_pairs={{0,16},{1,17},{2,18},{3,19},{4,20},{5,21},{6,22},{7,23},{8,24},{9,... | collective-permute-start | bytes 245768 | tf_op jit(solution)/shard_map/ppermute | solution.py:353
  33.7 2.8 %collective-permute-done.3 = f32[2,1,80,128]{3,2,0,1:T(8,128)S(1)} collective-permute-done((f32[2,1,80,128]{3,2,0,1:T(8,128)S(1)}, f32[2,1,80,128]{3,2,0,1:T(8,128)S(1)}, u32[]{:S(2)}, u32[]{:S(2)}) %collective-permute-start.3) | collective-permute-done | bytes 81952 | tf_op jit(solution)/shard_map/ppermute | solution.py:353
  36.5 0.1 fusion.3
  36.6 3.4 %collective-permute-start.4 = (f32[2,80,128]{2,1,0:T(8,128)S(1)}, f32[2,80,128]{2,1,0:T(8,128)S(1)}, u32[]{:S(2)}, u32[]{:S(2)}) collective-permute-start(f32[2,80,128]{2,1,0:T(8,128)S(1)} %fusion.3), channel_id=1, source_target_pairs={{0,2},{1,3},{2,0},{3,1},{4,6},{5,7},{6,4},{7,5},{8,10},{9,11},{10,... | collective-permute-start | bytes 245768 | tf_op jit(solution)/shard_map/ppermute | solution.py:353
  39.9 2.4 %collective-permute-done.4 = f32[2,80,128]{2,1,0:T(8,128)S(1)} collective-permute-done((f32[2,80,128]{2,1,0:T(8,128)S(1)}, f32[2,80,128]{2,1,0:T(8,128)S(1)}, u32[]{:S(2)}, u32[]{:S(2)}) %collective-permute-start.4) | collective-permute-done | bytes 81952 | tf_op jit(solution)/shard_map/ppermute | solution.py:353
  42.4 0.1 collective-permute-start.5
  43.1 0.6 %collective-permute-done.5.other_ref = f32[2,80,128]{2,1,0:T(8,128)S(1)} collective-permute-done((f32[2,80,128]{2,1,0:T(8,128)S(1)}, f32[2,80,128]{2,1,0:T(8,128)S(1)}, u32[]{:S(2)}, u32[]{:S(2)}) %collective-permute-start.5) | collective-permute-done | bytes 81952 | tf_op jit(solution)/shard_map/ppermute | solution.py:353
  43.7 0.0 copy-done.1
  43.7 0.0 copy-done.2
  43.7 0.0 copy-done.3
  43.7 0.0 copy-done.4
  43.7 0.0 copy-done
  43.7 3.1 %image_blocks.1 = f32[1,128,512]{2,1,0:T(8,128)} custom-call(s32[1]{0:T(128)} %bitcast.table_ref, s32[2]{0:T(128)S(1)} %copy-done.3, s32[2,8,10]{2,1,0:T(8,128)S(1)} %copy-done.2, s32[1,20]{1,0:T(1,128)S(1)} %copy-done.4, s32[1]{0:T(128)S(6)} %copy.19.counts_ref, f32[2,80,128]{2,1,0:T(8,128)S(1)} %add.16.own_ref, ...), custom_call_target="tpu_custom_call" | custom-call | tf_op jit(solution)/shard_map/image_blocks/pallas_call | solution.py:317
  (4 shorter events, 0.1 us)
Async XLA Ops:
  0.0 43.7 %copy-start.1 = (f32[4,16,512]{2,1,0:T(8,128)S(1)}, f32[4,16,512]{2,1,0:T(8,128)}, u32[]{:S(2)}) copy-start(f32[4,16,512]{2,1,0:T(8,128)} %constant.36.clone.second_ref) | copy-start | bytes 393220
  0.0 43.7 %copy-start.2 = (s32[2,8,10]{2,1,0:T(8,128)S(1)}, s32[2,8,10]{2,1,0:T(8,128)}, u32[]{:S(2)}) copy-start(s32[2,8,10]{2,1,0:T(8,128)} %corners_ref.1) | copy-start | bytes 1924
  0.0 43.7 %copy-start.3 = (s32[2]{0:T(128)S(1)}, s32[2]{0:T(128)}, u32[]{:S(2)}) copy-start(s32[2]{0:T(128)} %owners_ref.1) | copy-start | bytes 28
  0.0 43.7 %copy-start.4 = (s32[1,20]{1,0:T(1,128)S(1)}, s32[1,20]{1,0:T(1,128)}, u32[]{:S(2)}) copy-start(s32[1,20]{1,0:T(1,128)} %assign_ref.1) | copy-start | bytes 244
  16.6 27.1 %copy-start = (f32[8,128,512]{2,1,0:T(8,128)S(1)}, f32[8,128,512]{2,1,0:T(8,128)}, u32[]{:S(2)}) copy-start(f32[8,128,512]{2,1,0:T(8,128)} %constant.35.clone.first_ref) | copy-start | bytes 6291460
  16.6 2.0 %collective-permute-start = (f32[8,80,128]{2,1,0:T(8,128)}, f32[8,80,128]{2,1,0:T(8,128)S(1)}, u32[]{:S(2)}, u32[]{:S(2)}) collective-permute-start(f32[8,80,128]{2,1,0:T(8,128)} %get-tuple-element.8), channel_id=1, source_target_pairs={{0,1},{1,0},{2,3},{3,2},{4,5},{5,4},{6,7},{7,6},{8,9},{9,8},{10,11... | collective-permute-start | bytes 983048 | tf_op jit(solution)/shard_map/ppermute | solution.py:353
  19.7 5.4 %collective-permute-start.1 = (f32[1,4,80,128]{3,2,1,0:T(8,128)S(1)}, f32[1,4,80,128]{3,2,1,0:T(8,128)S(1)}, u32[]{:S(2)}, u32[]{:S(2)}) collective-permute-start(f32[1,4,80,128]{3,2,1,0:T(8,128)S(1)} %get-tuple-element.9), channel_id=1, source_target_pairs={{0,4},{1,9},{2,6},{3,11},{4,0},{5,13},{6,2},{7,15},{8,12},{9,1},{1... | collective-permute-start | bytes 491528 | tf_op jit(solution)/shard_map/ppermute | solution.py:353
  25.2 5.4 %collective-permute-start.2 = (f32[2,2,80,128]{3,2,0,1:T(8,128)S(1)}, f32[2,2,80,128]{3,2,0,1:T(8,128)S(1)}, u32[]{:S(2)}, u32[]{:S(2)}) collective-permute-start(f32[2,2,80,128]{3,2,0,1:T(8,128)S(1)} %slice_bitcast_fusion.1), channel_id=1, source_target_pairs={{0,8},{1,5},{2,10},{3,7},{4,12},{5,1},{6,14},{7,3},{8,0},{9,13},{1... | collective-permute-start | bytes 491528 | tf_op jit(solution)/shard_map/ppermute | solution.py:353
  30.7 5.8 %collective-permute-start.3 = (f32[2,1,80,128]{3,2,0,1:T(8,128)S(1)}, f32[2,1,80,128]{3,2,0,1:T(8,128)S(1)}, u32[]{:S(2)}, u32[]{:S(2)}) collective-permute-start(f32[2,1,80,128]{3,2,0,1:T(8,128)S(1)} %slice_bitcast_fusion.4), channel_id=1, source_target_pairs={{0,16},{1,17},{2,18},{3,19},{4,20},{5,21},{6,22},{7,23},{8,24},{9,... | collective-permute-start | bytes 245768 | tf_op jit(solution)/shard_map/ppermute | solution.py:353
  36.6 5.8 %collective-permute-start.4 = (f32[2,80,128]{2,1,0:T(8,128)S(1)}, f32[2,80,128]{2,1,0:T(8,128)S(1)}, u32[]{:S(2)}, u32[]{:S(2)}) collective-permute-start(f32[2,80,128]{2,1,0:T(8,128)S(1)} %fusion.3), channel_id=1, source_target_pairs={{0,2},{1,3},{2,0},{3,1},{4,6},{5,7},{6,4},{7,5},{8,10},{9,11},{10,... | collective-permute-start | bytes 245768 | tf_op jit(solution)/shard_map/ppermute | solution.py:353
  42.4 1.3 %collective-permute-start.5 = (f32[2,80,128]{2,1,0:T(8,128)S(1)}, f32[2,80,128]{2,1,0:T(8,128)S(1)}, u32[]{:S(2)}, u32[]{:S(2)}) collective-permute-start(f32[2,80,128]{2,1,0:T(8,128)S(1)} %add.16.own_ref), channel_id=1, source_target_pairs={{0,1},{1,0},{2,3},{3,2},{4,5},{5,4},{6,7},{7,6},{8,9},{9,8},{10,11... | collective-permute-start | bytes 245768 | tf_op jit(solution)/shard_map/ppermute | solution.py:353

commit v3 on v2

v3 whole, which is shorter than its diff:
```python
import math

import jax
import jax.numpy as jnp
import ml_dtypes
import numpy as np
from jax import lax
from jax.experimental import pallas as pl
from jax.experimental.pallas import tpu as pltpu
from jax.sharding import PartitionSpec as P

SUB = 32
G = 512
HALF = SUB // 2
COLUMNS = 8
ROWS, BASE = 24, 40
PAD = 16

two_pi = 2.0 * math.pi
field_width = 0.02
band_spread = 0.02
centre_shift = G // 2 - SUB // 2

SIN_POLY = (6.2831853, -41.34170041, 81.6051314, -76.70301553, 42.02592778, -14.89984801, 3.23813768)
COS_POLY = (0.99999999, -19.7392045, 64.9391175, -85.45013994, 60.16763282, -25.96760244, 6.52865863)


def poly(square, coefficients):
    total = jnp.full_like(square, coefficients[-1])
    for coefficient in coefficients[-2::-1]:
        total = total * square + coefficient
    return total


def cos_sin(turns):
    rest = turns - jnp.round(turns)
    square = rest * rest
    return poly(square, COS_POLY), rest * poly(square, SIN_POLY)


def times(a, b):
    return a[0] * b[0] - a[1] * b[1], a[0] * b[1] + a[1] * b[0]


def dot(a, b, over):
    return lax.dot_general(a, b, (((1,), (over,)), ((), ())), preferred_element_type=jnp.float32)


def swap_low(value):
    return (value & ~3) | ((value & 1) << 1) | ((value >> 1) & 1)


def grid_kernel(meta_ref, own_ref, other_ref, keep_ref, send_ref, z_ref, base_ref, left_ref, right_ref):
    me = lax.axis_index("facet")
    band = lax.axis_index("freq")
    band_total = lax.axis_size("freq")
    facet_rows = lax.axis_size("facet") // COLUMNS
    core = band & 1
    facet_row = pl.program_id(0)
    step = pl.program_id(1)
    half_blocks = own_ref.shape[0]
    channels, lanes = other_ref.shape[3], other_ref.shape[4]
    block = core * half_blocks + step

    def build(k):
        corner_u = meta_ref[block]
        corner_v = meta_ref[2 * half_blocks + block]
        first_channel = (band ^ k) * channels
        channel = (first_channel + lax.broadcasted_iota(jnp.int32, (channels, lanes), 0)).astype(jnp.float32)
        ratio = 1.0 + band_spread * channel / (channels * band_total)
        u_cells = own_ref[step, 2 * channels : 2 * channels + 1] * ratio
        v_cells = own_ref[step, 2 * channels + 1 : 2 * channels + 2] * ratio
        w_waves = own_ref[step, 2 * channels + 2 : 2 * channels + 3] * ratio
        shift_u = centre_shift - corner_u
        delta_u = u_cells + shift_u.astype(jnp.float32)
        delta_v = v_cells + (centre_shift - corner_v).astype(jnp.float32)
        row_pos = facet_row.astype(jnp.float32) - (facet_rows - 1) / 2.0
        row_vec = jnp.full((8, lanes), row_pos, jnp.float32)
        common = (
            v_cells * row_pos - (delta_u + delta_v) * (0.5 / SUB) + 0.5 * (shift_u & 1).astype(jnp.float32)
        )
        if k == 0:
            vis = (own_ref[step, 0:channels], own_ref[step, channels : 2 * channels])
        else:
            vis = (other_ref[0, block, 0], other_ref[0, block, 1])
        for g in range(COLUMNS // 2):
            radius = field_width * field_width * ((g + 0.5) ** 2 + row_vec * row_vec)
            w_shift = (-radius / (1.0 + jnp.sqrt(1.0 - radius)))[0:1]
            turned = times(vis, cos_sin(common + w_waves * w_shift))
            z_ref[k, pl.ds(2 * g, channels, stride=ROWS), :] = turned[0]
            z_ref[k, pl.ds(2 * g + 1, channels, stride=ROWS), :] = turned[1]
        for axis, delta in enumerate((delta_u, delta_v)):
            wave = cos_sin(delta * (0.5 / SUB))
            turn = times(wave, wave)
            for j in range(8):
                base_ref[k, pl.ds(16 * axis + j, channels, stride=BASE), :] = wave[0]
                base_ref[k, pl.ds(16 * axis + 8 + j, channels, stride=BASE), :] = wave[1]
                if j < 7:
                    wave = times(wave, turn)
            for _ in range(3):
                turn = times(turn, turn)
            z_ref[k, pl.ds(COLUMNS + 2 * axis, channels, stride=ROWS), :] = turn[0]
            z_ref[k, pl.ds(COLUMNS + 2 * axis + 1, channels, stride=ROWS), :] = turn[1]
        for c in range(channels):

            def row_of(i):
                return z_ref[k, ROWS * c + i : ROWS * c + i + 1, :]

            def base_of(i):
                return base_ref[k, BASE * c + 8 * i : BASE * c + 8 * i + 8, :]

            at = k * channels + c
            turn = (row_of(COLUMNS), row_of(COLUMNS + 1))
            twice = 2.0 * turn[0]
            wave = (base_of(0), base_of(1))
            after = times(wave, turn)
            for i in range(COLUMNS):
                for part in range(2):
                    left_ref[at, 128 * part + 16 * i : 128 * part + 16 * i + 16] = jnp.concatenate(
                        [wave[part], after[part]], axis=0
                    ).astype(jnp.bfloat16)
                if i < COLUMNS - 1:
                    wave = tuple(twice * after[part] - wave[part] for part in range(2))
                    after = tuple(twice * wave[part] - after[part] for part in range(2))
            turn = (row_of(COLUMNS + 2), row_of(COLUMNS + 3))
            wave = (base_of(2), base_of(3))
            after = times(wave, turn)
            both = tuple(jnp.concatenate([wave[part], after[part]], axis=0) for part in range(2))
            for g in range(COLUMNS // 2):
                for part in range(2):
                    turned = row_of(2 * g + part)
                    for kind in range(2):
                        row = 64 * g + 32 * part + 16 * kind
                        right_ref[at, row : row + 16] = (turned * both[kind]).astype(jnp.bfloat16)

    def finish():
        product = None
        for c in range(0, 2 * channels, 2):
            right = jnp.concatenate([right_ref[c, 0:256], right_ref[c + 1, 0:256]], axis=1)
            left = jnp.concatenate([left_ref[c, 0:256], left_ref[c + 1, 0:256]], axis=1)
            term = dot(right, left, 1)
            product = term if product is None else product + term
        group = lax.broadcasted_iota(jnp.int32, (HALF, 128), 1) // SUB
        tiles = [None] * COLUMNS
        for sign in (1, -1):
            for g in range(COLUMNS // 2):
                part = [product[64 * g + 16 * k : 64 * g + 16 * k + 16] for k in range(4)]
                (rcc, rcs), (rsc, rss), (icc, ics), (isc, iss) = [(x[:, :128], x[:, 128:]) for x in part]
                kinds = (rcc - sign * ics, -(sign * rss + isc), icc + sign * rcs, rsc - sign * iss)
                tile = None
                for t in range(4):
                    moved = kinds[t] if t == g else pltpu.roll(kinds[t], SUB * ((t - g) % 4), 1)
                    tile = moved if tile is None else jnp.where(group == t, moved, tile)
                tiles[COLUMNS // 2 + g if sign == 1 else COLUMNS // 2 - 1 - g] = tile
        return tiles

    def store(tiles):
        tiles = [jnp.where(core == 1, tiles[swap_low(i)], tiles[i]) if swap_low(i) != i else tiles[i] for i in range(COLUMNS)]
        mine = jnp.where(core == 1, swap_low(me), me)
        row = pl.multiple_of(step * HALF, HALF)
        for i in range(0, COLUMNS, 2):
            place = (facet_row * (COLUMNS // 2) + i // 2) ^ (mine >> 1)
            odd = (mine & 1) == 1
            keep_ref[place, pl.ds(row, HALF), :] = jnp.where(odd, tiles[i + 1], tiles[i])
            send_ref[place, pl.ds(row, HALF), :] = jnp.where(odd, tiles[i], tiles[i + 1])

    owner = 4 * half_blocks

    @pl.when(jnp.logical_or(meta_ref[owner] == me, meta_ref[owner + 1] == me))
    def _():
        build(0)
        build(1)
        store(finish())


def grid_blocks(meta, own, other):
    facet_total = lax.axis_size("facet")
    half_blocks = own.shape[0]
    channels, lanes = other.shape[3:]
    out = jax.ShapeDtypeStruct((facet_total // 2, half_blocks * HALF, 128), jnp.float32)
    vmem = pl.BlockSpec(memory_space=pltpu.VMEM)
    return pl.pallas_call(
        grid_kernel,
        grid=(facet_total // COLUMNS, half_blocks),
        in_specs=[pl.BlockSpec(memory_space=pltpu.SMEM), vmem, vmem],
        out_specs=[vmem, vmem],
        scratch_shapes=[
            pltpu.VMEM((2, ROWS * channels, lanes), jnp.float32),
            pltpu.VMEM((2, BASE * channels, lanes), jnp.float32),
            pltpu.VMEM((2 * channels, 256 + PAD, lanes), jnp.bfloat16),
            pltpu.VMEM((2 * channels, 256 + PAD, lanes), jnp.bfloat16),
        ],
        out_shape=[out, out],
        compiler_params=pltpu.CompilerParams(vmem_limit_bytes=40 * 1024 * 1024),
        name="grid_blocks",
    )(meta, own, other)


def image_tables(band_total, scale):
    offsets = np.arange(SUB) - HALF
    pixels = np.arange(G) - G // 2
    taper = 1.0 - 0.8 * (offsets / HALF) ** 2
    spread = np.exp(2j * np.pi * np.outer(pixels, offsets) / G)
    table = spread @ np.exp(-2j * np.pi * np.outer(offsets, offsets) / SUB) * taper
    share = G // band_total
    first = np.zeros((2, band_total, 4, share, 4, SUB))
    for sign in range(2):
        for band in range(band_total):
            wave = table[band * share : (band + 1) * share, :: 1 if sign == 0 else -1]
            for odd in range(2):
                first[sign, band, 2 * odd, :, odd] = wave.real
                first[sign, band, 2 * odd + 1, :, odd] = wave.imag
                first[sign, band, 2 * odd, :, 2 + odd] = -wave.imag
                first[sign, band, 2 * odd + 1, :, 2 + odd] = wave.real
    first = first.reshape(2 * band_total, 1, 4 * share, 4 * SUB).astype(np.float32)
    high = first.astype(ml_dtypes.bfloat16)
    low = (first - high.astype(np.float32)).astype(ml_dtypes.bfloat16)
    upper, lower = table.T[HALF:], table.T[HALF - 1 :: -1]
    second = np.stack([(upper + lower).real, (upper + lower).imag, (upper - lower).real, (upper - lower).imag]) * scale
    return np.concatenate([high, low], axis=1), second.astype(np.float32)


def two_parts(value):
    high = value.astype(jnp.bfloat16)
    return high, (value - high.astype(jnp.float32)).astype(jnp.bfloat16)


def down_kernel(owners_ref, corners_ref, assign_ref, counts_ref, after_ref, down_ref, weight_ref):
    band = lax.axis_index("freq")
    blocks = corners_ref.shape[2]
    share, rows = down_ref.shape[1:]
    for item in range(2 * blocks):
        weight_ref[assign_ref[0, item]] = (item < counts_ref[0]).astype(jnp.int32)
    group = lax.broadcasted_iota(jnp.int32, (1, rows), 1) // HALF
    corner, weight = jnp.zeros((1, rows), jnp.int32), jnp.zeros((1, rows), jnp.int32)
    for b in range(2 * blocks):
        corner = jnp.where(group == b, corners_ref[0, owners_ref[b // blocks], b % blocks] - centre_shift, corner)
        weight = jnp.where(group == b, weight_ref[b], weight)
    down = lax.broadcasted_iota(jnp.int32, (share, 1), 0) - G // 2 + band * share
    wave = cos_sin(((down * corner) & (G - 1)).astype(jnp.float32) * (1.0 / G))
    for part in range(2):
        down_ref[part] = wave[part] * weight.astype(jnp.float32)


def across_kernel(
    owners_ref, corners_ref, second_ref, tables_ref, after_ref, across_ref, first_ref, turn_ref, first_sem
):
    left_half = (lax.axis_index("facet") % COLUMNS < COLUMNS // 2).astype(jnp.int32)
    index = left_half * lax.axis_size("freq") + lax.axis_index("freq")
    copy = pltpu.make_async_copy(tables_ref.at[index], first_ref, first_sem)
    copy.start()
    blocks = corners_ref.shape[2]
    rows = 2 * blocks * HALF
    pixels = across_ref.shape[2]
    across = lax.broadcasted_iota(jnp.int32, (1, pixels), 1) - pixels // 2
    for b in range(2 * blocks):
        turn_ref[b : b + 1] = across * (corners_ref[1, owners_ref[b // blocks], b % blocks] - centre_shift)
    wave = cos_sin((turn_ref[...] & (G - 1)).astype(jnp.float32) * (1.0 / G))
    full = rows - rows % 128
    for b in range(2 * blocks):
        for odd in range(2):
            real, imag = times((second_ref[2 * odd], second_ref[2 * odd + 1]), (wave[0][b : b + 1], wave[1][b : b + 1]))
            for k, value in enumerate((real, -imag)):
                kind = 2 * odd + k
                at = kind * full + HALF * b if HALF * b < full else 4 * full + kind * (rows - full) + HALF * b - full
                high, low = two_parts(value)
                across_ref[0, at : at + HALF] = high
                across_ref[1, at : at + HALF] = low
    copy.wait()


def image_kernel(own_ref, other_ref, down_ref, across_ref, first_ref, out_ref):
    core = lax.axis_index("freq") & 1
    share = out_ref.shape[1]
    mine = core == 0
    pieces = []
    for s in range(2):
        own, other = own_ref[s], other_ref[s]
        pieces += [jnp.where(mine, own, other), jnp.where(mine, other, own)]
    high, low = two_parts(jnp.concatenate(pieces, axis=0))
    table_high, table_low = first_ref[0], first_ref[1]
    half = dot(table_high, high, 1) + (dot(table_high, low, 1) + dot(table_low, high, 1))
    wave = (down_ref[0], down_ref[1])
    kinds = []
    for odd in range(2):
        at = 2 * odd * share
        kinds += list(times((half[at : at + share], half[at + share : at + 2 * share]), wave))
    rows = half.shape[1]
    full = rows - rows % 128
    pieces = [kind[:, :full] for kind in kinds] + ([kind[:, full:] for kind in kinds] if full < rows else [])
    high, low = two_parts(jnp.concatenate(pieces, axis=1))
    both = dot(jnp.concatenate([high, low], axis=0), across_ref[0], 0)
    out_ref[0] = both[:share] + (both[share:] + dot(high, across_ref[1], 0))


def down_of(owners, corners, assign, counts, after):
    share = G // lax.axis_size("freq")
    total = 2 * corners.shape[2]
    smem = pl.BlockSpec(memory_space=pltpu.SMEM)
    return pl.pallas_call(
        down_kernel,
        in_specs=[smem, smem, smem, smem, pl.BlockSpec(memory_space=pl.ANY)],
        out_specs=pl.BlockSpec(memory_space=pltpu.VMEM),
        out_shape=jax.ShapeDtypeStruct((2, share, total * HALF), jnp.float32),
        scratch_shapes=[pltpu.SMEM((total,), jnp.int32)],
        compiler_params=pltpu.CompilerParams(vmem_limit_bytes=32 * 1024 * 1024),
        cost_estimate=pl.CostEstimate(flops=10**7, bytes_accessed=10**6, transcendentals=0),
        name="image_down",
    )(owners, corners, assign, counts, after)


def across_of(owners, corners, second, first, after):
    total = 2 * corners.shape[2]
    smem, vmem = pl.BlockSpec(memory_space=pltpu.SMEM), pl.BlockSpec(memory_space=pltpu.VMEM)
    return pl.pallas_call(
        across_kernel,
        in_specs=[smem, smem, vmem] + [pl.BlockSpec(memory_space=pl.ANY)] * 2,
        out_specs=[vmem, vmem],
        out_shape=[
            jax.ShapeDtypeStruct((2, 4 * total * HALF, G), jnp.bfloat16),
            jax.ShapeDtypeStruct(first.shape[1:], first.dtype),
        ],
        scratch_shapes=[pltpu.VMEM((total, G), jnp.int32), pltpu.SemaphoreType.DMA(())],
        compiler_params=pltpu.CompilerParams(vmem_limit_bytes=32 * 1024 * 1024),
        cost_estimate=pl.CostEstimate(flops=10**8, bytes_accessed=6 * 10**6, transcendentals=0),
        name="image_across",
    )(owners, corners, second, first, after)


def image_blocks(down, across, first, own, other):
    share, pixels = down.shape[1], across.shape[2]
    return pl.pallas_call(
        image_kernel,
        in_specs=[pl.BlockSpec(memory_space=pltpu.VMEM)] * 5,
        out_specs=pl.BlockSpec(memory_space=pltpu.VMEM),
        out_shape=jax.ShapeDtypeStruct((1, share, pixels), jnp.float32),
        compiler_params=pltpu.CompilerParams(vmem_limit_bytes=40 * 1024 * 1024),
        name="image_blocks",
    )(own, other, down, across, first)


def swap(value, partner):
    facet_total, band_total = lax.axis_size("facet"), lax.axis_size("freq")
    pairs = []
    for f in range(facet_total):
        for q in range(band_total):
            to_f, to_q = partner(f, q)
            pairs.append((f * band_total + q, to_f * band_total + to_q))
    return lax.ppermute(value, ("facet", "freq"), pairs)


def on_device(visibilities, coords, corners, owners, assign, counts):
    facet_total, band_total = lax.axis_size("facet"), lax.axis_size("freq")
    facet_index, band_index = lax.axis_index("facet"), lax.axis_index("freq")
    channel_total = visibilities.shape[3] * band_total
    scale = 1.0 / (SUB * SUB * math.sqrt(2 * corners.shape[2] * visibilities.shape[4] * channel_total))
    first, second = (jnp.asarray(x) for x in image_tables(band_total, scale))
    other = swap(visibilities, lambda f, q: (f, q ^ 1))
    _, blocks, _, channels, lanes = visibilities.shape
    stacked = jnp.concatenate([visibilities[0].reshape(blocks, 2 * channels, lanes), coords[0]], axis=1)
    own = lax.dynamic_slice_in_dim(stacked, (band_index & 1) * (blocks // 2), blocks // 2, 0)
    meta = jnp.concatenate([lax.dynamic_index_in_dim(corners, facet_index, 1, False).reshape(-1), owners])
    meta, own, other = lax.optimization_barrier((meta, own, other))
    kept, sent = grid_blocks(meta, own, other)
    half_rows = kept.shape[1]
    kept, sent = kept[None], sent[None]
    for k in range(facet_total.bit_length() - 1):
        even, odd = (k, k ^ 1) if k < 2 else (k, k)
        if k > 0:
            parts = held.reshape(2, -1, 2, half_rows, 128)
            kept, sent = parts[:, :, 0], parts[:, :, 1]
        tables = ()
        if k == 0:
            tables = down_of(owners, corners, assign, counts, sent)
        if k == 1:
            tables = across_of(owners, corners, second, first, sent)
        came = swap(sent, lambda f, q: (f ^ (1 << (odd if q & 1 else even)), q))
        came, tables = lax.optimization_barrier((came, tables))
        if k == 0:
            down = tables
        if k == 1:
            across, first = tables
        bit = jnp.where(band_index & 1 == 1, odd, even)
        across_bit = ((owners ^ facet_index) >> bit & 1) == 1
        held = jnp.where(across_bit[:, None, None, None], came, kept)
    held = held.reshape(2, half_rows, 128)
    for k in range(1, band_total.bit_length() - 1):
        held = held + swap(held, lambda f, q: (f, q ^ (1 << k)))
    other = swap(held, lambda f, q: (f, q ^ 1))
    return image_blocks(down, across, first, held, other)


def solution(mesh):
    placed = (
        P("facet", None, None, "freq", None),
        P("facet", None, None, None),
        P(),
        P(),
        P("facet", None),
        P("facet"),
    )
    return jax.shard_map(
        on_device, mesh=mesh, in_specs=placed, out_specs=P("facet", "freq", None), check_vma=False
    )
```

time: 47.1 us -> 44.1 us (0.936)
  Pallas kernels: 19.7 us -> 4.91 us
  starting transfers between devices: 7.15 us -> 20.9 us
  waiting for transfers between devices: 17.2 us -> 10.5 us
  local copies, waits for them, and re-layouts: 0.07 us -> 4.22 us
  other arithmetic: 1.93 us -> 2.59 us
    pallas_call x2 -> x4, Pallas kernels: 19.7 us -> 4.91 us  [the longest x1 1.78 us: image_blocks(): pl.pallas_call(image_kernel, in_specs=[pl.BlockSpec(memory_space=pltpu.VM...]
    ppermute x6, starting transfers between devices: 7.15 us -> 20.9 us  [swap(): return lax.ppermute(value, ('facet', 'freq'), pairs)]
    ppermute x6, waiting for transfers between devices: 17.2 us -> 10.5 us  [swap(): return lax.ppermute(value, ('facet', 'freq'), pairs)]
    unnamed x10 -> x13, local copies, waits for them, and re-layouts: 0.02 us -> 3.38 us
    concatenate x0 -> x2, other arithmetic: none -> 1.66 us  [the longest x1 0.93 us: on_device(): jnp.concatenate([visibilities[0].reshape(blocks, 2 * channels, lanes), co...]
    add x1 -> x0, other arithmetic: 1.01 us -> none  [on_device(): held = (keep + swap(send, lambda f, q: (f, q ^ 1)))[None]]
    dynamic_slice x0 -> x1, local copies, waits for them, and re-layouts: none -> 0.72 us  [on_device(): lax.dynamic_index_in_dim(corners, facet_index, 1, False).reshape(-1)]
  transfers between devices with their start and end apart: 6 -> 6, of which waited for: 6 -> 4; matrix products, arithmetic and copies ran while one was open for 1% -> 9% of each run, Pallas kernels for 0% -> 5%
where the time goes in v3:
time: 44.1 us
  starting transfers between devices  20.9 us (47%)
  waiting for transfers between devices  10.5 us (24%)
  Pallas kernels  4.91 us (11%)
  local copies, waits for them, and re-layouts  4.22 us (10%)
  other arithmetic  2.59 us (6%)
  between operations  1 us (2%)
    ppermute x6, starting transfers between devices, swap(): return lax.ppermute(value, ('facet', 'freq'), pairs)  20.9 us
    ppermute x6, waiting for transfers between devices, swap(): return lax.ppermute(value, ('facet', 'freq'), pairs)  10.5 us
    unnamed x13, local copies, waits for them, and re-layouts  3.38 us
    pallas_call x1, Pallas kernels, image_blocks(): pl.pallas_call(image_kernel, in_specs=[pl.BlockSpec(memory_space=pltpu.VM...  1.78 us
    pallas_call x1, Pallas kernels, across_of(): pl.pallas_call(across_kernel, in_specs=[smem, smem, vmem] + [pl.BlockSpec...  1.45 us
    pallas_call x1, Pallas kernels, down_of(): pl.pallas_call(down_kernel, in_specs=[smem, smem, smem, smem, pl.BlockSpe...  0.96 us
    concatenate x1, other arithmetic, on_device(): jnp.concatenate([visibilities[0].reshape(blocks, 2 * channels, lanes), co...  0.93 us
  transfers between devices with their start and end apart: 6, of which 4 were waited for; matrix products, arithmetic and copies ran while one was open for 9% of the time, Pallas kernels for 5%

profile of v3, /device:TPU:0, one launch (start us, length us, event | category | flops | bytes accessed | tf_op | source)
XLA Modules:
  0.0 44.1 jit_solution(501036925707596867)
XLA Ops:
  0.0 0.5 %collective-permute-start = (f32[1,10,2,32,128]{4,3,2,1,0:T(8,128)}, f32[1,10,2,32,128]{4,3,2,1,0:T(8,128)S(1)}, u32[]{:S(2)}, u32[]{:S(2)}) collective-permute-start(f32[1,10,2,32,128]{4,3,2,1,0:T(8,128)} %param.8), channel_id=1, source_target_pairs={{0,1},{1,0},{2,3},{3,2},{4,5},{5,4},{6,7},{7,6},{8,9},{9,8},{10,11... | collective-permute-start | bytes 983048 | tf_op jit(solution)/shard_map/ppermute | solution.py:349
  1.3 0.7 %dynamic-slice_reduce_fusion = s32[2,10]{1,0:T(2,128)S(1)} fusion(s32[2,8,10]{2,1,0:T(8,128)} %corners_ref.3, s32[]{:T(128)S(6)} %select_n.30), kind=kLoop, calls=%fused_computation.13 | loop fusion | bytes 164 | tf_op jit(solution)/shard_map/jit(dynamic_index_in_dim)/dynamic_slice | solution.py:362
  2.1 0.1 reshape.21
  2.2 0.7 %copy.21 = f32[1,10,3,128]{3,2,0,1:T(4,128)S(1)} copy(f32[1,10,3,128]{3,0,2,1:T(1,128)} %param.9) | data formatting | bytes 30720
  2.9 0.7 %pad_add_fusion.meta_ref = s32[22]{0:T(128)S(1)} fusion(s32[2]{0:T(128)} %owners_ref.3, s32[20]{0:T(128)S(1)} %reshape.21), kind=kLoop, calls=%fused_computation.14 | loop fusion | flops 22 | bytes 176 | tf_op jit(solution)/shard_map/concatenate | solution.py:362
  3.6 0.9 %fusion.own_ref = f32[5,67,128]{2,1,0:T(8,128)S(1)} fusion(s32[]{:T(128)S(6)} %select_n.31, f32[10,64,128]{2,1,0:T(8,128)} %bitcast.30, f32[10,3,128]{2,1,0:T(4,128)S(1)} %bitcast.32), kind=kLoop, calls=%fused_computation.2 | loop fusion | flops 42880 | bytes 514564 | tf_op jit(solution)/shard_map/concatenate | solution.py:360
  4.5 0.0 collective-permute-done.other_ref
  4.5 0.7 %grid_blocks.1 = (f32[4,80,128]{2,1,0:T(8,128)S(1)}, f32[4,80,128]{2,1,0:T(8,128)S(1)}) custom-call(s32[22]{0:T(128)S(1)} %pad_add_fusion.meta_ref, f32[5,67,128]{2,1,0:T(8,128)S(1)} %fusion.own_ref, f32[1,10,2,32,128]{4,3,2,1,0:T(8,128)S(1)} %collective-permute-done.other_ref), custom_call_target="tpu_custom_call" | custom-call | tf_op jit(solution)/shard_map/grid_blocks/pallas_call | solution.py:182
  5.3 2.5 %collective-permute-start.1 = (f32[1,4,80,128]{3,2,1,0:T(8,128)S(1)}, f32[1,4,80,128]{3,2,1,0:T(8,128)S(1)}, u32[]{:S(2)}, u32[]{:S(2)}) collective-permute-start(f32[1,4,80,128]{3,2,1,0:T(8,128)S(1)} %bitcast.27), channel_id=1, source_target_pairs={{0,4},{1,9},{2,6},{3,11},{4,0},{5,13},{6,2},{7,15},{8,12},{9,1},{1... | collective-permute-start | bytes 491528 | tf_op jit(solution)/shard_map/ppermute | solution.py:349
  7.8 0.7 %and_compare_fusion.2 = (pred[2]{0:T(512)(128)(4,1)S(1)}, pred[2]{0:T(512)(128)(4,1)S(1)}, pred[2]{0:T(512)(128)(4,1)S(1)}) fusion(s32[2]{0:T(128)} %owners_ref.3, s32[]{:T(128)S(6)} %axis_index.23, s32[]{:T(128)S(6)} %select_n.28, s32[]{:T(128)S(6)} %select_n.29), kind=kLoop, calls=%fused_computation.17 | loop fusion | flops 20 | bytes 26 | tf_op jit(solution)/shard_map/eq | solution.py:384
  8.4 0.7 %copy-done.2 = s32[2,8,10]{2,1,0:T(8,128)S(1)} copy-done((s32[2,8,10]{2,1,0:T(8,128)S(1)}, s32[2,8,10]{2,1,0:T(8,128)}, u32[]{:S(2)}) %copy-start.2) | copy-done | bytes 664
  9.1 0.7 %copy-done.3 = s32[2]{0:T(128)S(1)} copy-done((s32[2]{0:T(128)S(1)}, s32[2]{0:T(128)}, u32[]{:S(2)}) %copy-start.3) | copy-done | bytes 32
  9.8 0.7 %copy-done.5 = s32[1,20]{1,0:T(1,128)S(1)} copy-done((s32[1,20]{1,0:T(1,128)S(1)}, s32[1,20]{1,0:T(1,128)}, u32[]{:S(2)}) %copy-start.5) | copy-done | bytes 104
  10.4 1.0 %image_down.1.down_ref = f32[2,128,320]{2,1,0:T(8,128)S(1)} custom-call(s32[2]{0:T(128)S(1)} %copy-done.3, s32[2,8,10]{2,1,0:T(8,128)S(1)} %copy-done.2, s32[1,20]{1,0:T(1,128)S(1)} %copy-done.5, s32[1]{0:T(128)S(6)} %copy.22.counts_ref, f32[1,4,80,128]{3,2,1,0:T(8,128)S(1)} %bitcast.28), custom_call_target="tpu_custom_call" | custom-call | flops 10000000 | bytes 1000000 | tf_op jit(solution)/shard_map/image_down/pallas_call | solution.py:300
  11.4 0.0 collective-permute-done.1
  11.4 0.1 broadcast_select_fusion
  11.5 1.8 %collective-permute-start.2 = (f32[2,2,80,128]{3,2,0,1:T(8,128)S(1)}, f32[2,2,80,128]{3,2,0,1:T(8,128)S(1)}, u32[]{:S(2)}, u32[]{:S(2)}) collective-permute-start(f32[2,2,80,128]{3,2,0,1:T(8,128)S(1)} %slice_bitcast_fusion.1), channel_id=1, source_target_pairs={{0,8},{1,5},{2,10},{3,7},{4,12},{5,1},{6,14},{7,3},{8,0},{9,13},{1... | collective-permute-start | bytes 491528 | tf_op jit(solution)/shard_map/ppermute | solution.py:349
  13.4 0.0 copy-done.1
  13.4 0.0 copy-done
  13.4 0.0 copy-start.4
  13.4 0.6 %copy-done.4 = s32[2]{0:T(128)S(1)} copy-done((s32[2]{0:T(128)S(1)}, s32[2]{0:T(128)}, u32[]{:S(2)}) %copy-start.4) | copy-done | bytes 32
  14.0 1.4 %image_across.1 = (bf16[2,1280,512]{2,1,0:T(8,128)(2,1)S(1)}, bf16[2,512,128]{2,1,0:T(8,128)(2,1)S(1)}) custom-call(s32[2]{0:T(128)S(1)} %copy-done.4, s32[2,8,10]{2,1,0:T(8,128)S(1)} %copy-done.2, f32[4,16,512]{2,1,0:T(8,128)S(1)} %copy-done.1, bf16[8,2,512,128]{3,2,1,0:T(8,128)(2,1)S(1)} %copy-done, f32[2,2,80,128]{3,2,1,0:T(8,128)S(1)} %copy.14.after_ref), custom_call_target="tpu_custom_call" | custom-call | flops 100000000 | bytes 6000000 | tf_op jit(solution)/shard_map/image_across/pallas_call | solution.py:315
  15.5 1.4 %collective-permute-done.2 = f32[2,2,80,128]{3,2,0,1:T(8,128)S(1)} collective-permute-done((f32[2,2,80,128]{3,2,0,1:T(8,128)S(1)}, f32[2,2,80,128]{3,2,0,1:T(8,128)S(1)}, u32[]{:S(2)}, u32[]{:S(2)}) %collective-permute-start.2) | collective-permute-done | bytes 163872 | tf_op jit(solution)/shard_map/ppermute | solution.py:349
  16.9 0.1 fusion.2
  17.0 15.5 %collective-permute-start.3 = (f32[2,1,80,128]{3,2,0,1:T(8,128)S(1)}, f32[2,1,80,128]{3,2,0,1:T(8,128)S(1)}, u32[]{:S(2)}, u32[]{:S(2)}) collective-permute-start(f32[2,1,80,128]{3,2,0,1:T(8,128)S(1)} %slice_bitcast_fusion.3), channel_id=1, source_target_pairs={{0,16},{1,17},{2,18},{3,19},{4,20},{5,21},{6,22},{7,23},{8,24},{9,... | collective-permute-start | bytes 245768 | tf_op jit(solution)/shard_map/ppermute | solution.py:349
  32.5 4.0 %collective-permute-done.3 = f32[2,1,80,128]{3,2,0,1:T(8,128)S(1)} collective-permute-done((f32[2,1,80,128]{3,2,0,1:T(8,128)S(1)}, f32[2,1,80,128]{3,2,0,1:T(8,128)S(1)}, u32[]{:S(2)}, u32[]{:S(2)}) %collective-permute-start.3) | collective-permute-done | bytes 81952 | tf_op jit(solution)/shard_map/ppermute | solution.py:349
  36.5 0.1 fusion.4
  36.5 0.6 %collective-permute-start.4 = (f32[2,80,128]{2,1,0:T(8,128)S(1)}, f32[2,80,128]{2,1,0:T(8,128)S(1)}, u32[]{:S(2)}, u32[]{:S(2)}) collective-permute-start(f32[2,80,128]{2,1,0:T(8,128)S(1)} %fusion.4), channel_id=1, source_target_pairs={{0,2},{1,3},{2,0},{3,1},{4,6},{5,7},{6,4},{7,5},{8,10},{9,11},{10,... | collective-permute-start | bytes 245768 | tf_op jit(solution)/shard_map/ppermute | solution.py:349
  37.2 3.8 %collective-permute-done.4 = f32[2,80,128]{2,1,0:T(8,128)S(1)} collective-permute-done((f32[2,80,128]{2,1,0:T(8,128)S(1)}, f32[2,80,128]{2,1,0:T(8,128)S(1)}, u32[]{:S(2)}, u32[]{:S(2)}) %collective-permute-start.4) | collective-permute-done | bytes 81952 | tf_op jit(solution)/shard_map/ppermute | solution.py:349
  41.0 0.1 collective-permute-start.5
  41.1 1.3 %collective-permute-done.5.other_ref = f32[2,80,128]{2,1,0:T(8,128)S(1)} collective-permute-done((f32[2,80,128]{2,1,0:T(8,128)S(1)}, f32[2,80,128]{2,1,0:T(8,128)S(1)}, u32[]{:S(2)}, u32[]{:S(2)}) %collective-permute-start.5) | collective-permute-done | bytes 81952 | tf_op jit(solution)/shard_map/ppermute | solution.py:349
  42.4 1.8 %image_blocks.1 = f32[1,128,512]{2,1,0:T(8,128)} custom-call(f32[2,80,128]{2,1,0:T(8,128)S(1)} %add.12.own_ref, f32[2,80,128]{2,1,0:T(8,128)S(1)} %collective-permute-done.5.other_ref, f32[2,128,320]{2,1,0:T(8,128)S(1)} %image_down.1.down_ref, bf16[2,1280,512]{2,1,0:T(8,128)(2,1)S(1)} %get-tuple-element.27.across_ref, ...), custom_call_target="tpu_custom_call" | custom-call | tf_op jit(solution)/shard_map/image_blocks/pallas_call | solution.py:332
  (9 shorter events, 0.1 us)
Async XLA Ops:
  0.0 13.4 %copy-start.1 = (f32[4,16,512]{2,1,0:T(8,128)S(1)}, f32[4,16,512]{2,1,0:T(8,128)}, u32[]{:S(2)}) copy-start(f32[4,16,512]{2,1,0:T(8,128)} %constant.30.clone.second_ref) | copy-start | bytes 393220
  0.0 13.4 %copy-start = (bf16[8,2,512,128]{3,2,1,0:T(8,128)(2,1)S(1)}, bf16[8,2,512,128]{3,2,1,0:T(8,128)(2,1)}, u32[]{:S(2)}) copy-start(bf16[8,2,512,128]{3,2,1,0:T(8,128)(2,1)} %constant.29.clone.tables_ref) | copy-start | bytes 6291460
  0.0 4.5 %collective-permute-start = (f32[1,10,2,32,128]{4,3,2,1,0:T(8,128)}, f32[1,10,2,32,128]{4,3,2,1,0:T(8,128)S(1)}, u32[]{:S(2)}, u32[]{:S(2)}) collective-permute-start(f32[1,10,2,32,128]{4,3,2,1,0:T(8,128)} %param.8), channel_id=1, source_target_pairs={{0,1},{1,0},{2,3},{3,2},{4,5},{5,4},{6,7},{7,6},{8,9},{9,8},{10,11... | collective-permute-start | bytes 983048 | tf_op jit(solution)/shard_map/ppermute | solution.py:349
  5.3 6.1 %collective-permute-start.1 = (f32[1,4,80,128]{3,2,1,0:T(8,128)S(1)}, f32[1,4,80,128]{3,2,1,0:T(8,128)S(1)}, u32[]{:S(2)}, u32[]{:S(2)}) collective-permute-start(f32[1,4,80,128]{3,2,1,0:T(8,128)S(1)} %bitcast.27), channel_id=1, source_target_pairs={{0,4},{1,9},{2,6},{3,11},{4,0},{5,13},{6,2},{7,15},{8,12},{9,1},{1... | collective-permute-start | bytes 491528 | tf_op jit(solution)/shard_map/ppermute | solution.py:349
  8.4 0.7 %copy-start.2 = (s32[2,8,10]{2,1,0:T(8,128)S(1)}, s32[2,8,10]{2,1,0:T(8,128)}, u32[]{:S(2)}) copy-start(s32[2,8,10]{2,1,0:T(8,128)} %corners_ref.3) | copy-start | bytes 1924
  9.1 0.7 %copy-start.3 = (s32[2]{0:T(128)S(1)}, s32[2]{0:T(128)}, u32[]{:S(2)}) copy-start(s32[2]{0:T(128)} %owners_ref.3) | copy-start | bytes 28
  9.8 0.7 %copy-start.5 = (s32[1,20]{1,0:T(1,128)S(1)}, s32[1,20]{1,0:T(1,128)}, u32[]{:S(2)}) copy-start(s32[1,20]{1,0:T(1,128)} %assign_ref.1) | copy-start | bytes 244
  11.5 5.4 %collective-permute-start.2 = (f32[2,2,80,128]{3,2,0,1:T(8,128)S(1)}, f32[2,2,80,128]{3,2,0,1:T(8,128)S(1)}, u32[]{:S(2)}, u32[]{:S(2)}) collective-permute-start(f32[2,2,80,128]{3,2,0,1:T(8,128)S(1)} %slice_bitcast_fusion.1), channel_id=1, source_target_pairs={{0,8},{1,5},{2,10},{3,7},{4,12},{5,1},{6,14},{7,3},{8,0},{9,13},{1... | collective-permute-start | bytes 491528 | tf_op jit(solution)/shard_map/ppermute | solution.py:349
  13.4 0.7 %copy-start.4 = (s32[2]{0:T(128)S(1)}, s32[2]{0:T(128)}, u32[]{:S(2)}) copy-start(s32[2]{0:T(128)} %owners_ref.3) | copy-start | bytes 28
  17.0 19.4 %collective-permute-start.3 = (f32[2,1,80,128]{3,2,0,1:T(8,128)S(1)}, f32[2,1,80,128]{3,2,0,1:T(8,128)S(1)}, u32[]{:S(2)}, u32[]{:S(2)}) collective-permute-start(f32[2,1,80,128]{3,2,0,1:T(8,128)S(1)} %slice_bitcast_fusion.3), channel_id=1, source_target_pairs={{0,16},{1,17},{2,18},{3,19},{4,20},{5,21},{6,22},{7,23},{8,24},{9,... | collective-permute-start | bytes 245768 | tf_op jit(solution)/shard_map/ppermute | solution.py:349
  36.5 4.4 %collective-permute-start.4 = (f32[2,80,128]{2,1,0:T(8,128)S(1)}, f32[2,80,128]{2,1,0:T(8,128)S(1)}, u32[]{:S(2)}, u32[]{:S(2)}) collective-permute-start(f32[2,80,128]{2,1,0:T(8,128)S(1)} %fusion.4), channel_id=1, source_target_pairs={{0,2},{1,3},{2,0},{3,1},{4,6},{5,7},{6,4},{7,5},{8,10},{9,11},{10,... | collective-permute-start | bytes 245768 | tf_op jit(solution)/shard_map/ppermute | solution.py:349
  41.0 1.3 %collective-permute-start.5 = (f32[2,80,128]{2,1,0:T(8,128)S(1)}, f32[2,80,128]{2,1,0:T(8,128)S(1)}, u32[]{:S(2)}, u32[]{:S(2)}) collective-permute-start(f32[2,80,128]{2,1,0:T(8,128)S(1)} %add.12.own_ref), channel_id=1, source_target_pairs={{0,1},{1,0},{2,3},{3,2},{4,5},{5,4},{6,7},{7,6},{8,9},{9,8},{10,11... | collective-permute-start | bytes 245768 | tf_op jit(solution)/shard_map/ppermute | solution.py:349

commit v4 on v3

--- a/solution.py
+++ b/solution.py
@@ -13,7 +13,7 @@
 G = 512
 HALF = SUB // 2
 COLUMNS = 8
-ROWS, BASE = 24, 40
+BASE = 40
 PAD = 16
 
 two_pi = 2.0 * math.pi
@@ -87,24 +87,27 @@
             radius = field_width * field_width * ((g + 0.5) ** 2 + row_vec * row_vec)
             w_shift = (-radius / (1.0 + jnp.sqrt(1.0 - radius)))[0:1]
             turned = times(vis, cos_sin(common + w_waves * w_shift))
-            z_ref[k, pl.ds(2 * g, channels, stride=ROWS), :] = turned[0]
-            z_ref[k, pl.ds(2 * g + 1, channels, stride=ROWS), :] = turned[1]
+            z_ref[k, 2 * g, 0:channels] = turned[0]
+            z_ref[k, 2 * g + 1, 0:channels] = turned[1]
         for axis, delta in enumerate((delta_u, delta_v)):
             wave = cos_sin(delta * (0.5 / SUB))
             turn = times(wave, wave)
             for j in range(8):
                 base_ref[k, pl.ds(16 * axis + j, channels, stride=BASE), :] = wave[0]
                 base_ref[k, pl.ds(16 * axis + 8 + j, channels, stride=BASE), :] = wave[1]
-                if j < 7:
-                    wave = times(wave, turn)
+                if j == 0:
+                    last, wave = wave, times(wave, turn)
+                    twice = 2.0 * turn[0]
+                elif j < 7:
+                    last, wave = wave, tuple(twice * wave[part] - last[part] for part in range(2))
             for _ in range(3):
                 turn = times(turn, turn)
-            z_ref[k, pl.ds(COLUMNS + 2 * axis, channels, stride=ROWS), :] = turn[0]
-            z_ref[k, pl.ds(COLUMNS + 2 * axis + 1, channels, stride=ROWS), :] = turn[1]
+            z_ref[k, COLUMNS + 2 * axis, 0:channels] = turn[0]
+            z_ref[k, COLUMNS + 2 * axis + 1, 0:channels] = turn[1]
         for c in range(channels):
 
             def row_of(i):
-                return z_ref[k, ROWS * c + i : ROWS * c + i + 1, :]
+                return z_ref[k, i, c : c + 1]
 
             def base_of(i):
                 return base_ref[k, BASE * c + 8 * i : BASE * c + 8 * i + 8, :]
@@ -185,7 +188,7 @@
         in_specs=[pl.BlockSpec(memory_space=pltpu.SMEM), vmem, vmem],
         out_specs=[vmem, vmem],
         scratch_shapes=[
-            pltpu.VMEM((2, ROWS * channels, lanes), jnp.float32),
+            pltpu.VMEM((2, COLUMNS + 4, channels + 8, lanes), jnp.float32),
             pltpu.VMEM((2, BASE * channels, lanes), jnp.float32),
             pltpu.VMEM((2 * channels, 256 + PAD, lanes), jnp.bfloat16),
             pltpu.VMEM((2 * channels, 256 + PAD, lanes), jnp.bfloat16),

time: 44.1 us -> 43.2 us (0.980); the launches traced: 44.1 us -> 42.7 us
  waiting for transfers between devices: 10.5 us -> 8.19 us
  starting transfers between devices: 20.9 us -> 21.8 us
    ppermute x6, waiting for transfers between devices: 10.5 us -> 8.19 us  [swap(): return lax.ppermute(value, ('facet', 'freq'), pairs)]
    ppermute x6, starting transfers between devices: 20.9 us -> 21.8 us  [swap(): return lax.ppermute(value, ('facet', 'freq'), pairs)]
  transfers between devices with their start and end apart: 6 -> 6, of which waited for: 4 -> 4; matrix products, arithmetic and copies ran while one was open for 9% -> 9% of each run, Pallas kernels for 5% -> 6%
where the time goes in v4:
time: 43.2 us; the launch traced here: 42.7 us
  starting transfers between devices  21.8 us (50%)
  waiting for transfers between devices  8.19 us (19%)
  Pallas kernels  4.91 us (11%)
  local copies, waits for them, and re-layouts  4.22 us (10%)
  other arithmetic  2.59 us (6%)
  between operations  1 us (2%)
    ppermute x6, starting transfers between devices, swap(): return lax.ppermute(value, ('facet', 'freq'), pairs)  21.8 us
    ppermute x6, waiting for transfers between devices, swap(): return lax.ppermute(value, ('facet', 'freq'), pairs)  8.19 us
    unnamed x13, local copies, waits for them, and re-layouts  3.38 us
    pallas_call x1, Pallas kernels, image_blocks(): pl.pallas_call(image_kernel, in_specs=[pl.BlockSpec(memory_space=pltpu.VM...  1.78 us
    pallas_call x1, Pallas kernels, across_of(): pl.pallas_call(across_kernel, in_specs=[smem, smem, vmem] + [pl.BlockSpec...  1.45 us
    pallas_call x1, Pallas kernels, down_of(): pl.pallas_call(down_kernel, in_specs=[smem, smem, smem, smem, pl.BlockSpe...  0.96 us
    concatenate x1, other arithmetic, on_device(): jnp.concatenate([visibilities[0].reshape(blocks, 2 * channels, lanes), co...  0.93 us
  transfers between devices with their start and end apart: 6, of which 4 were waited for; matrix products, arithmetic and copies ran while one was open for 9% of the time, Pallas kernels for 6%

profile of v4, /device:TPU:0, one launch (start us, length us, event | category | flops | bytes accessed | tf_op | source)
XLA Modules:
  0.0 42.7 jit_solution(5583585232888106564)
XLA Ops:
  0.0 0.5 %collective-permute-start = (f32[1,10,2,32,128]{4,3,2,1,0:T(8,128)}, f32[1,10,2,32,128]{4,3,2,1,0:T(8,128)S(1)}, u32[]{:S(2)}, u32[]{:S(2)}) collective-permute-start(f32[1,10,2,32,128]{4,3,2,1,0:T(8,128)} %param.8), channel_id=1, source_target_pairs={{0,1},{1,0},{2,3},{3,2},{4,5},{5,4},{6,7},{7,6},{8,9},{9,8},{10,11... | collective-permute-start | bytes 983048 | tf_op jit(solution)/shard_map/ppermute | solution.py:352
  1.3 0.7 %dynamic-slice_reduce_fusion = s32[2,10]{1,0:T(2,128)S(1)} fusion(s32[2,8,10]{2,1,0:T(8,128)} %corners_ref.3, s32[]{:T(128)S(6)} %select_n.30), kind=kLoop, calls=%fused_computation.13 | loop fusion | bytes 164 | tf_op jit(solution)/shard_map/jit(dynamic_index_in_dim)/dynamic_slice | solution.py:365
  2.1 0.1 reshape.21
  2.2 0.7 %copy.21 = f32[1,10,3,128]{3,2,0,1:T(4,128)S(1)} copy(f32[1,10,3,128]{3,0,2,1:T(1,128)} %param.9) | data formatting | bytes 30720
  2.9 0.7 %pad_add_fusion.meta_ref = s32[22]{0:T(128)S(1)} fusion(s32[2]{0:T(128)} %owners_ref.3, s32[20]{0:T(128)S(1)} %reshape.21), kind=kLoop, calls=%fused_computation.14 | loop fusion | flops 22 | bytes 176 | tf_op jit(solution)/shard_map/concatenate | solution.py:365
  3.6 0.9 %fusion.own_ref = f32[5,67,128]{2,1,0:T(8,128)S(1)} fusion(s32[]{:T(128)S(6)} %select_n.31, f32[10,64,128]{2,1,0:T(8,128)} %bitcast.30, f32[10,3,128]{2,1,0:T(4,128)S(1)} %bitcast.32), kind=kLoop, calls=%fused_computation.2 | loop fusion | flops 42880 | bytes 514564 | tf_op jit(solution)/shard_map/concatenate | solution.py:363
  4.5 0.0 collective-permute-done.other_ref
  4.5 0.7 %grid_blocks.1 = (f32[4,80,128]{2,1,0:T(8,128)S(1)}, f32[4,80,128]{2,1,0:T(8,128)S(1)}) custom-call(s32[22]{0:T(128)S(1)} %pad_add_fusion.meta_ref, f32[5,67,128]{2,1,0:T(8,128)S(1)} %fusion.own_ref, f32[1,10,2,32,128]{4,3,2,1,0:T(8,128)S(1)} %collective-permute-done.other_ref), custom_call_target="tpu_custom_call" | custom-call | tf_op jit(solution)/shard_map/grid_blocks/pallas_call | solution.py:185
  5.3 2.5 %collective-permute-start.1 = (f32[1,4,80,128]{3,2,1,0:T(8,128)S(1)}, f32[1,4,80,128]{3,2,1,0:T(8,128)S(1)}, u32[]{:S(2)}, u32[]{:S(2)}) collective-permute-start(f32[1,4,80,128]{3,2,1,0:T(8,128)S(1)} %bitcast.27), channel_id=1, source_target_pairs={{0,4},{1,9},{2,6},{3,11},{4,0},{5,13},{6,2},{7,15},{8,12},{9,1},{1... | collective-permute-start | bytes 491528 | tf_op jit(solution)/shard_map/ppermute | solution.py:352
  7.8 0.7 %and_compare_fusion.2 = (pred[2]{0:T(512)(128)(4,1)S(1)}, pred[2]{0:T(512)(128)(4,1)S(1)}, pred[2]{0:T(512)(128)(4,1)S(1)}) fusion(s32[2]{0:T(128)} %owners_ref.3, s32[]{:T(128)S(6)} %axis_index.23, s32[]{:T(128)S(6)} %select_n.28, s32[]{:T(128)S(6)} %select_n.29), kind=kLoop, calls=%fused_computation.17 | loop fusion | flops 20 | bytes 26 | tf_op jit(solution)/shard_map/eq | solution.py:387
  8.4 0.7 %copy-done.2 = s32[2,8,10]{2,1,0:T(8,128)S(1)} copy-done((s32[2,8,10]{2,1,0:T(8,128)S(1)}, s32[2,8,10]{2,1,0:T(8,128)}, u32[]{:S(2)}) %copy-start.2) | copy-done | bytes 664
  9.1 0.7 %copy-done.3 = s32[2]{0:T(128)S(1)} copy-done((s32[2]{0:T(128)S(1)}, s32[2]{0:T(128)}, u32[]{:S(2)}) %copy-start.3) | copy-done | bytes 32
  9.8 0.7 %copy-done.5 = s32[1,20]{1,0:T(1,128)S(1)} copy-done((s32[1,20]{1,0:T(1,128)S(1)}, s32[1,20]{1,0:T(1,128)}, u32[]{:S(2)}) %copy-start.5) | copy-done | bytes 104
  10.4 1.0 %image_down.1.down_ref = f32[2,128,320]{2,1,0:T(8,128)S(1)} custom-call(s32[2]{0:T(128)S(1)} %copy-done.3, s32[2,8,10]{2,1,0:T(8,128)S(1)} %copy-done.2, s32[1,20]{1,0:T(1,128)S(1)} %copy-done.5, s32[1]{0:T(128)S(6)} %copy.22.counts_ref, f32[1,4,80,128]{3,2,1,0:T(8,128)S(1)} %bitcast.28), custom_call_target="tpu_custom_call" | custom-call | flops 10000000 | bytes 1000000 | tf_op jit(solution)/shard_map/image_down/pallas_call | solution.py:303
  11.4 0.0 collective-permute-done.1
  11.4 0.1 broadcast_select_fusion
  11.5 1.8 %collective-permute-start.2 = (f32[2,2,80,128]{3,2,0,1:T(8,128)S(1)}, f32[2,2,80,128]{3,2,0,1:T(8,128)S(1)}, u32[]{:S(2)}, u32[]{:S(2)}) collective-permute-start(f32[2,2,80,128]{3,2,0,1:T(8,128)S(1)} %slice_bitcast_fusion.1), channel_id=1, source_target_pairs={{0,8},{1,5},{2,10},{3,7},{4,12},{5,1},{6,14},{7,3},{8,0},{9,13},{1... | collective-permute-start | bytes 491528 | tf_op jit(solution)/shard_map/ppermute | solution.py:352
  13.4 0.0 copy-done.1
  13.4 0.0 copy-done
  13.4 0.0 copy-start.4
  13.4 0.6 %copy-done.4 = s32[2]{0:T(128)S(1)} copy-done((s32[2]{0:T(128)S(1)}, s32[2]{0:T(128)}, u32[]{:S(2)}) %copy-start.4) | copy-done | bytes 32
  14.0 1.4 %image_across.1 = (bf16[2,1280,512]{2,1,0:T(8,128)(2,1)S(1)}, bf16[2,512,128]{2,1,0:T(8,128)(2,1)S(1)}) custom-call(s32[2]{0:T(128)S(1)} %copy-done.4, s32[2,8,10]{2,1,0:T(8,128)S(1)} %copy-done.2, f32[4,16,512]{2,1,0:T(8,128)S(1)} %copy-done.1, bf16[8,2,512,128]{3,2,1,0:T(8,128)(2,1)S(1)} %copy-done, f32[2,2,80,128]{3,2,1,0:T(8,128)S(1)} %copy.14.after_ref), custom_call_target="tpu_custom_call" | custom-call | flops 100000000 | bytes 6000000 | tf_op jit(solution)/shard_map/image_across/pallas_call | solution.py:318
  15.5 1.4 %collective-permute-done.2 = f32[2,2,80,128]{3,2,0,1:T(8,128)S(1)} collective-permute-done((f32[2,2,80,128]{3,2,0,1:T(8,128)S(1)}, f32[2,2,80,128]{3,2,0,1:T(8,128)S(1)}, u32[]{:S(2)}, u32[]{:S(2)}) %collective-permute-start.2) | collective-permute-done | bytes 163872 | tf_op jit(solution)/shard_map/ppermute | solution.py:352
  16.9 0.1 fusion.2
  17.0 15.4 %collective-permute-start.3 = (f32[2,1,80,128]{3,2,0,1:T(8,128)S(1)}, f32[2,1,80,128]{3,2,0,1:T(8,128)S(1)}, u32[]{:S(2)}, u32[]{:S(2)}) collective-permute-start(f32[2,1,80,128]{3,2,0,1:T(8,128)S(1)} %slice_bitcast_fusion.3), channel_id=1, source_target_pairs={{0,16},{1,17},{2,18},{3,19},{4,20},{5,21},{6,22},{7,23},{8,24},{9,... | collective-permute-start | bytes 245768 | tf_op jit(solution)/shard_map/ppermute | solution.py:352
  32.4 2.6 %collective-permute-done.3 = f32[2,1,80,128]{3,2,0,1:T(8,128)S(1)} collective-permute-done((f32[2,1,80,128]{3,2,0,1:T(8,128)S(1)}, f32[2,1,80,128]{3,2,0,1:T(8,128)S(1)}, u32[]{:S(2)}, u32[]{:S(2)}) %collective-permute-start.3) | collective-permute-done | bytes 81952 | tf_op jit(solution)/shard_map/ppermute | solution.py:352
  35.0 0.1 fusion.4
  35.1 1.5 %collective-permute-start.4 = (f32[2,80,128]{2,1,0:T(8,128)S(1)}, f32[2,80,128]{2,1,0:T(8,128)S(1)}, u32[]{:S(2)}, u32[]{:S(2)}) collective-permute-start(f32[2,80,128]{2,1,0:T(8,128)S(1)} %fusion.4), channel_id=1, source_target_pairs={{0,2},{1,3},{2,0},{3,1},{4,6},{5,7},{6,4},{7,5},{8,10},{9,11},{10,... | collective-permute-start | bytes 245768 | tf_op jit(solution)/shard_map/ppermute | solution.py:352
  36.6 2.9 %collective-permute-done.4 = f32[2,80,128]{2,1,0:T(8,128)S(1)} collective-permute-done((f32[2,80,128]{2,1,0:T(8,128)S(1)}, f32[2,80,128]{2,1,0:T(8,128)S(1)}, u32[]{:S(2)}, u32[]{:S(2)}) %collective-permute-start.4) | collective-permute-done | bytes 81952 | tf_op jit(solution)/shard_map/ppermute | solution.py:352
  39.6 0.1 collective-permute-start.5
  39.6 1.3 %collective-permute-done.5.other_ref = f32[2,80,128]{2,1,0:T(8,128)S(1)} collective-permute-done((f32[2,80,128]{2,1,0:T(8,128)S(1)}, f32[2,80,128]{2,1,0:T(8,128)S(1)}, u32[]{:S(2)}, u32[]{:S(2)}) %collective-permute-start.5) | collective-permute-done | bytes 81952 | tf_op jit(solution)/shard_map/ppermute | solution.py:352
  40.9 1.8 %image_blocks.1 = f32[1,128,512]{2,1,0:T(8,128)} custom-call(f32[2,80,128]{2,1,0:T(8,128)S(1)} %add.12.own_ref, f32[2,80,128]{2,1,0:T(8,128)S(1)} %collective-permute-done.5.other_ref, f32[2,128,320]{2,1,0:T(8,128)S(1)} %image_down.1.down_ref, bf16[2,1280,512]{2,1,0:T(8,128)(2,1)S(1)} %get-tuple-element.27.across_ref, ...), custom_call_target="tpu_custom_call" | custom-call | tf_op jit(solution)/shard_map/image_blocks/pallas_call | solution.py:335
  (9 shorter events, 0.1 us)
Async XLA Ops:
  0.0 13.4 %copy-start.1 = (f32[4,16,512]{2,1,0:T(8,128)S(1)}, f32[4,16,512]{2,1,0:T(8,128)}, u32[]{:S(2)}) copy-start(f32[4,16,512]{2,1,0:T(8,128)} %constant.30.clone.second_ref) | copy-start | bytes 393220
  0.0 13.4 %copy-start = (bf16[8,2,512,128]{3,2,1,0:T(8,128)(2,1)S(1)}, bf16[8,2,512,128]{3,2,1,0:T(8,128)(2,1)}, u32[]{:S(2)}) copy-start(bf16[8,2,512,128]{3,2,1,0:T(8,128)(2,1)} %constant.29.clone.tables_ref) | copy-start | bytes 6291460
  0.0 4.5 %collective-permute-start = (f32[1,10,2,32,128]{4,3,2,1,0:T(8,128)}, f32[1,10,2,32,128]{4,3,2,1,0:T(8,128)S(1)}, u32[]{:S(2)}, u32[]{:S(2)}) collective-permute-start(f32[1,10,2,32,128]{4,3,2,1,0:T(8,128)} %param.8), channel_id=1, source_target_pairs={{0,1},{1,0},{2,3},{3,2},{4,5},{5,4},{6,7},{7,6},{8,9},{9,8},{10,11... | collective-permute-start | bytes 983048 | tf_op jit(solution)/shard_map/ppermute | solution.py:352
  5.3 6.1 %collective-permute-start.1 = (f32[1,4,80,128]{3,2,1,0:T(8,128)S(1)}, f32[1,4,80,128]{3,2,1,0:T(8,128)S(1)}, u32[]{:S(2)}, u32[]{:S(2)}) collective-permute-start(f32[1,4,80,128]{3,2,1,0:T(8,128)S(1)} %bitcast.27), channel_id=1, source_target_pairs={{0,4},{1,9},{2,6},{3,11},{4,0},{5,13},{6,2},{7,15},{8,12},{9,1},{1... | collective-permute-start | bytes 491528 | tf_op jit(solution)/shard_map/ppermute | solution.py:352
  8.4 0.7 %copy-start.2 = (s32[2,8,10]{2,1,0:T(8,128)S(1)}, s32[2,8,10]{2,1,0:T(8,128)}, u32[]{:S(2)}) copy-start(s32[2,8,10]{2,1,0:T(8,128)} %corners_ref.3) | copy-start | bytes 1924
  9.1 0.7 %copy-start.3 = (s32[2]{0:T(128)S(1)}, s32[2]{0:T(128)}, u32[]{:S(2)}) copy-start(s32[2]{0:T(128)} %owners_ref.3) | copy-start | bytes 28
  9.8 0.7 %copy-start.5 = (s32[1,20]{1,0:T(1,128)S(1)}, s32[1,20]{1,0:T(1,128)}, u32[]{:S(2)}) copy-start(s32[1,20]{1,0:T(1,128)} %assign_ref.1) | copy-start | bytes 244
  11.5 5.4 %collective-permute-start.2 = (f32[2,2,80,128]{3,2,0,1:T(8,128)S(1)}, f32[2,2,80,128]{3,2,0,1:T(8,128)S(1)}, u32[]{:S(2)}, u32[]{:S(2)}) collective-permute-start(f32[2,2,80,128]{3,2,0,1:T(8,128)S(1)} %slice_bitcast_fusion.1), channel_id=1, source_target_pairs={{0,8},{1,5},{2,10},{3,7},{4,12},{5,1},{6,14},{7,3},{8,0},{9,13},{1... | collective-permute-start | bytes 491528 | tf_op jit(solution)/shard_map/ppermute | solution.py:352
  13.4 0.7 %copy-start.4 = (s32[2]{0:T(128)S(1)}, s32[2]{0:T(128)}, u32[]{:S(2)}) copy-start(s32[2]{0:T(128)} %owners_ref.3) | copy-start | bytes 28
  17.0 18.0 %collective-permute-start.3 = (f32[2,1,80,128]{3,2,0,1:T(8,128)S(1)}, f32[2,1,80,128]{3,2,0,1:T(8,128)S(1)}, u32[]{:S(2)}, u32[]{:S(2)}) collective-permute-start(f32[2,1,80,128]{3,2,0,1:T(8,128)S(1)} %slice_bitcast_fusion.3), channel_id=1, source_target_pairs={{0,16},{1,17},{2,18},{3,19},{4,20},{5,21},{6,22},{7,23},{8,24},{9,... | collective-permute-start | bytes 245768 | tf_op jit(solution)/shard_map/ppermute | solution.py:352
  35.1 4.4 %collective-permute-start.4 = (f32[2,80,128]{2,1,0:T(8,128)S(1)}, f32[2,80,128]{2,1,0:T(8,128)S(1)}, u32[]{:S(2)}, u32[]{:S(2)}) collective-permute-start(f32[2,80,128]{2,1,0:T(8,128)S(1)} %fusion.4), channel_id=1, source_target_pairs={{0,2},{1,3},{2,0},{3,1},{4,6},{5,7},{6,4},{7,5},{8,10},{9,11},{10,... | collective-permute-start | bytes 245768 | tf_op jit(solution)/shard_map/ppermute | solution.py:352
  39.6 1.3 %collective-permute-start.5 = (f32[2,80,128]{2,1,0:T(8,128)S(1)}, f32[2,80,128]{2,1,0:T(8,128)S(1)}, u32[]{:S(2)}, u32[]{:S(2)}) collective-permute-start(f32[2,80,128]{2,1,0:T(8,128)S(1)} %add.12.own_ref), channel_id=1, source_target_pairs={{0,1},{1,0},{2,3},{3,2},{4,5},{5,4},{6,7},{7,6},{8,9},{9,8},{10,11... | collective-permute-start | bytes 245768 | tf_op jit(solution)/shard_map/ppermute | solution.py:352

commit v5 on v4

--- a/solution.py
+++ b/solution.py
@@ -50,7 +50,52 @@
     return (value & ~3) | ((value & 1) << 1) | ((value >> 1) & 1)
 
 
-def grid_kernel(meta_ref, own_ref, other_ref, keep_ref, send_ref, z_ref, base_ref, left_ref, right_ref):
+def gather_kernel(
+    owners_hbm, corners_hbm, coords_hbm, vis_hbm, out_ref, owners_ref, corners_ref, coords_ref, sems
+):
+    me = lax.axis_index("facet")
+    half_blocks = out_ref.shape[0]
+    first = (lax.axis_index("freq") & 1) * half_blocks
+    rows, lanes = vis_hbm.shape[1:]
+    ends = (
+        (vis_hbm.at[pl.ds(first, half_blocks)], out_ref.at[:, pl.ds(0, rows)]),
+        (owners_hbm, owners_ref),
+        (corners_hbm, corners_ref),
+        (coords_hbm.at[pl.ds(first, half_blocks)], coords_ref),
+    )
+    copies = [pltpu.make_async_copy(source, target, sems.at[k]) for k, (source, target) in enumerate(ends)]
+    for copy in copies:
+        copy.start()
+    for copy in copies[1:]:
+        copy.wait()
+    active = jnp.logical_or(owners_ref[0] == me, owners_ref[1] == me).astype(jnp.float32)
+    for b in range(half_blocks):
+        shifts = [(centre_shift - corners_ref[i, me, first + b]).astype(jnp.float32) for i in range(2)]
+        for i, value in enumerate([coords_ref[b, i] for i in range(3)] + shifts + [active]):
+            out_ref[b, rows + 8 * i : rows + 8 * i + 8] = jnp.broadcast_to(value, (8, lanes))
+    copies[0].wait()
+
+
+def gather(owners, corners, coords, visibilities):
+    _, blocks, _, channels, lanes = visibilities.shape
+    rows = 2 * channels
+    return pl.pallas_call(
+        gather_kernel,
+        in_specs=[pl.BlockSpec(memory_space=pltpu.HBM)] * 4,
+        out_specs=pl.BlockSpec(memory_space=pltpu.VMEM),
+        out_shape=jax.ShapeDtypeStruct((blocks // 2, rows + 48, lanes), jnp.float32),
+        scratch_shapes=[
+            pltpu.SMEM(owners.shape, jnp.int32),
+            pltpu.SMEM(corners.shape, jnp.int32),
+            pltpu.VMEM((blocks // 2, 3, 1, lanes), jnp.float32),
+            pltpu.SemaphoreType.DMA((4,)),
+        ],
+        compiler_params=pltpu.CompilerParams(vmem_limit_bytes=60 * 1024 * 1024),
+        name="gather_blocks",
+    )(owners, corners, coords.reshape(blocks, 3, 1, lanes), visibilities.reshape(blocks, rows, lanes))
+
+
+def grid_kernel(own_ref, other_ref, keep_ref, send_ref, z_ref, base_ref, left_ref, right_ref):
     me = lax.axis_index("facet")
     band = lax.axis_index("freq")
     band_total = lax.axis_size("freq")
@@ -63,22 +108,17 @@
     block = core * half_blocks + step
 
     def build(k):
-        corner_u = meta_ref[block]
-        corner_v = meta_ref[2 * half_blocks + block]
         first_channel = (band ^ k) * channels
         channel = (first_channel + lax.broadcasted_iota(jnp.int32, (channels, lanes), 0)).astype(jnp.float32)
         ratio = 1.0 + band_spread * channel / (channels * band_total)
-        u_cells = own_ref[step, 2 * channels : 2 * channels + 1] * ratio
-        v_cells = own_ref[step, 2 * channels + 1 : 2 * channels + 2] * ratio
-        w_waves = own_ref[step, 2 * channels + 2 : 2 * channels + 3] * ratio
-        shift_u = centre_shift - corner_u
-        delta_u = u_cells + shift_u.astype(jnp.float32)
-        delta_v = v_cells + (centre_shift - corner_v).astype(jnp.float32)
+        u, v, w, shift_u, shift_v = (own_ref[step, 2 * channels + 8 * i : 2 * channels + 8 * i + 1] for i in range(5))
+        u_cells, v_cells, w_waves = u * ratio, v * ratio, w * ratio
+        delta_u = u_cells + shift_u
+        delta_v = v_cells + shift_v
+        half_turn = 0.5 * shift_u - jnp.round(0.5 * shift_u)
         row_pos = facet_row.astype(jnp.float32) - (facet_rows - 1) / 2.0
         row_vec = jnp.full((8, lanes), row_pos, jnp.float32)
-        common = (
-            v_cells * row_pos - (delta_u + delta_v) * (0.5 / SUB) + 0.5 * (shift_u & 1).astype(jnp.float32)
-        )
+        common = v_cells * row_pos - (delta_u + delta_v) * (0.5 / SUB) + half_turn
         if k == 0:
             vis = (own_ref[step, 0:channels], own_ref[step, channels : 2 * channels])
         else:
@@ -167,16 +207,14 @@
             keep_ref[place, pl.ds(row, HALF), :] = jnp.where(odd, tiles[i + 1], tiles[i])
             send_ref[place, pl.ds(row, HALF), :] = jnp.where(odd, tiles[i], tiles[i + 1])
 
-    owner = 4 * half_blocks
-
-    @pl.when(jnp.logical_or(meta_ref[owner] == me, meta_ref[owner + 1] == me))
+    @pl.when(jnp.max(own_ref[step, 2 * channels + 40 : 2 * channels + 48]) > 0.0)
     def _():
         build(0)
         build(1)
         store(finish())
 
 
-def grid_blocks(meta, own, other):
+def grid_blocks(own, other):
     facet_total = lax.axis_size("facet")
     half_blocks = own.shape[0]
     channels, lanes = other.shape[3:]
@@ -185,7 +223,7 @@
     return pl.pallas_call(
         grid_kernel,
         grid=(facet_total // COLUMNS, half_blocks),
-        in_specs=[pl.BlockSpec(memory_space=pltpu.SMEM), vmem, vmem],
+        in_specs=[vmem, vmem],
         out_specs=[vmem, vmem],
         scratch_shapes=[
             pltpu.VMEM((2, COLUMNS + 4, channels + 8, lanes), jnp.float32),
@@ -196,7 +234,7 @@
         out_shape=[out, out],
         compiler_params=pltpu.CompilerParams(vmem_limit_bytes=40 * 1024 * 1024),
         name="grid_blocks",
-    )(meta, own, other)
+    )(own, other)
 
 
 def image_tables(band_total, scale):
@@ -359,12 +397,8 @@
     scale = 1.0 / (SUB * SUB * math.sqrt(2 * corners.shape[2] * visibilities.shape[4] * channel_total))
     first, second = (jnp.asarray(x) for x in image_tables(band_total, scale))
     other = swap(visibilities, lambda f, q: (f, q ^ 1))
-    _, blocks, _, channels, lanes = visibilities.shape
-    stacked = jnp.concatenate([visibilities[0].reshape(blocks, 2 * channels, lanes), coords[0]], axis=1)
-    own = lax.dynamic_slice_in_dim(stacked, (band_index & 1) * (blocks // 2), blocks // 2, 0)
-    meta = jnp.concatenate([lax.dynamic_index_in_dim(corners, facet_index, 1, False).reshape(-1), owners])
-    meta, own, other = lax.optimization_barrier((meta, own, other))
-    kept, sent = grid_blocks(meta, own, other)
+    own = gather(owners, corners, coords, visibilities)
+    kept, sent = grid_blocks(own, other)
     half_rows = kept.shape[1]
     kept, sent = kept[None], sent[None]
     for k in range(facet_total.bit_length() - 1):

time: 43.2 us -> 43.1 us (level)
  starting transfers between devices: 21.8 us -> 6.45 us
  Pallas kernels: 4.91 us -> 19.4 us
  waiting for transfers between devices: 8.19 us -> 11.2 us
  other arithmetic: 2.59 us -> 0.93 us
    ppermute x6, starting transfers between devices: 21.8 us -> 6.45 us  [swap(): return lax.ppermute(value, ('facet', 'freq'), pairs)]
    pallas_call x1, Pallas kernels: 0.73 us -> 13.5 us  [grid_blocks(): pl.pallas_call(grid_kernel, grid=(facet_total // COLUMNS, half_blocks), i...]
    ppermute x6, waiting for transfers between devices: 8.19 us -> 11.2 us  [swap(): return lax.ppermute(value, ('facet', 'freq'), pairs)]
    pallas_call x0 -> x1, Pallas kernels: none -> 1.7 us  [gather(): pl.pallas_call(gather_kernel, in_specs=[pl.BlockSpec(memory_space=pltpu.H...]
    concatenate x2 -> x0, other arithmetic: 1.66 us -> none  [the longest x1 0.93 us: on_device(): jnp.concatenate([visibilities[0].reshape(blocks, 2 * channels, lanes), co...]
    dynamic_slice x1 -> x0, local copies, waits for them, and re-layouts: 0.72 us -> none  [on_device(): lax.dynamic_index_in_dim(corners, facet_index, 1, False).reshape(-1)]
    unnamed x13 -> x12, local copies, waits for them, and re-layouts: 3.38 us -> 3.86 us
  transfers between devices with their start and end apart: 6 -> 6, of which waited for: 4 -> 5; matrix products, arithmetic and copies ran while one was open for 9% -> 2% of each run, Pallas kernels for 6% -> 10%
where the time goes in v5:
time: 43.1 us; the launch traced here: 42.9 us
  Pallas kernels  19.4 us (45%)
  waiting for transfers between devices  11.2 us (26%)
  starting transfers between devices  6.45 us (15%)
  local copies, waits for them, and re-layouts  3.89 us (9%)
  between operations  0.96 us (2%)
  other arithmetic  0.93 us (2%)
    pallas_call x1, Pallas kernels, grid_blocks(): pl.pallas_call(grid_kernel, grid=(facet_total // COLUMNS, half_blocks), i...  13.5 us
    ppermute x6, waiting for transfers between devices, swap(): return lax.ppermute(value, ('facet', 'freq'), pairs)  11.2 us
    ppermute x6, starting transfers between devices, swap(): return lax.ppermute(value, ('facet', 'freq'), pairs)  6.45 us
    unnamed x12, local copies, waits for them, and re-layouts  3.86 us
    pallas_call x1, Pallas kernels, image_blocks(): pl.pallas_call(image_kernel, in_specs=[pl.BlockSpec(memory_space=pltpu.VM...  1.78 us
    pallas_call x1, Pallas kernels, gather(): pl.pallas_call(gather_kernel, in_specs=[pl.BlockSpec(memory_space=pltpu.H...  1.7 us
    pallas_call x1, Pallas kernels, across_of(): pl.pallas_call(across_kernel, in_specs=[smem, smem, vmem] + [pl.BlockSpec...  1.45 us
    pallas_call x1, Pallas kernels, down_of(): pl.pallas_call(down_kernel, in_specs=[smem, smem, smem, smem, pl.BlockSpe...  0.96 us
  transfers between devices with their start and end apart: 6, of which 5 were waited for; matrix products, arithmetic and copies ran while one was open for 2% of the time, Pallas kernels for 10%

profile of v5, /device:TPU:0, one launch (start us, length us, event | category | flops | bytes accessed | tf_op | source)
XLA Modules:
  0.0 42.9 jit_solution(10892589504695316227)
XLA Ops:
  0.0 0.0 copy-start
  0.0 0.5 %collective-permute-start = (f32[1,10,2,32,128]{4,3,2,1,0:T(8,128)}, f32[1,10,2,32,128]{4,3,2,1,0:T(8,128)S(1)}, u32[]{:S(2)}, u32[]{:S(2)}) collective-permute-start(f32[1,10,2,32,128]{4,3,2,1,0:T(8,128)} %param.8), channel_id=1, source_target_pairs={{0,1},{1,0},{2,3},{3,2},{4,5},{5,4},{6,7},{7,6},{8,9},{9,8},{10,11... | collective-permute-start | bytes 983048 | tf_op jit(solution)/shard_map/ppermute | solution.py:390
  1.3 1.7 %gather_blocks.1.own_ref = f32[5,112,128]{2,1,0:T(8,128)} custom-call(s32[2]{0:T(128)} %owners_ref.3, s32[2,8,10]{2,1,0:T(8,128)} %corners_ref.3, f32[10,3,1,128]{3,2,1,0:T(1,128)} %bitcast.30, f32[10,64,128]{2,1,0:T(8,128)} %bitcast.28), custom_call_target="tpu_custom_call" | custom-call | tf_op jit(solution)/shard_map/gather_blocks/pallas_call | solution.py:82
  3.0 0.0 collective-permute-done.other_ref
  3.0 0.0 copy-start.1
  3.0 0.9 %copy-done.1 = f32[5,112,128]{2,1,0:T(8,128)S(1)} copy-done((f32[5,112,128]{2,1,0:T(8,128)S(1)}, f32[5,112,128]{2,1,0:T(8,128)}, u32[]{:S(2)}) %copy-start.1) | copy-done | bytes 286744
  4.0 13.5 %grid_blocks.1 = (f32[4,80,128]{2,1,0:T(8,128)S(1)}, f32[4,80,128]{2,1,0:T(8,128)S(1)}) custom-call(f32[5,112,128]{2,1,0:T(8,128)S(1)} %copy-done.1, f32[1,10,2,32,128]{4,3,2,1,0:T(8,128)S(1)} %collective-permute-done.other_ref), custom_call_target="tpu_custom_call" | custom-call | tf_op jit(solution)/shard_map/grid_blocks/pallas_call | solution.py:223
  17.5 0.1 collective-permute-start.1
  17.5 0.7 %and_compare_fusion.2 = (pred[2]{0:T(512)(128)(4,1)S(1)}, pred[2]{0:T(512)(128)(4,1)S(1)}, pred[2]{0:T(512)(128)(4,1)S(1)}) fusion(s32[2]{0:T(128)} %owners_ref.3, s32[]{:T(128)S(6)} %axis_index.23, s32[]{:T(128)S(6)} %select_n.21, s32[]{:T(128)S(6)} %select_n.22), kind=kLoop, calls=%fused_computation.11 | loop fusion | flops 20 | bytes 26 | tf_op jit(solution)/shard_map/eq | solution.py:421
  18.2 0.0 copy-start.3
  18.2 0.7 %copy-done.3 = s32[2,8,10]{2,1,0:T(8,128)S(1)} copy-done((s32[2,8,10]{2,1,0:T(8,128)S(1)}, s32[2,8,10]{2,1,0:T(8,128)}, u32[]{:S(2)}) %copy-start.3) | copy-done | bytes 664
  18.9 0.0 copy-start.4
  18.9 0.7 %copy-done.4 = s32[2]{0:T(128)S(1)} copy-done((s32[2]{0:T(128)S(1)}, s32[2]{0:T(128)}, u32[]{:S(2)}) %copy-start.4) | copy-done | bytes 32
  19.6 0.7 %copy-done.5 = s32[1,20]{1,0:T(1,128)S(1)} copy-done((s32[1,20]{1,0:T(1,128)S(1)}, s32[1,20]{1,0:T(1,128)}, u32[]{:S(2)}) %copy-start.5) | copy-done | bytes 104
  20.2 1.0 %image_down.1.down_ref = f32[2,128,320]{2,1,0:T(8,128)S(1)} custom-call(s32[2]{0:T(128)S(1)} %copy-done.4, s32[2,8,10]{2,1,0:T(8,128)S(1)} %copy-done.3, s32[1,20]{1,0:T(1,128)S(1)} %copy-done.5, s32[1]{0:T(128)S(6)} %copy.16.counts_ref, f32[1,4,80,128]{3,2,1,0:T(8,128)S(1)} %bitcast.26), custom_call_target="tpu_custom_call" | custom-call | flops 10000000 | bytes 1000000 | tf_op jit(solution)/shard_map/image_down/pallas_call | solution.py:341
  21.2 1.7 %collective-permute-done.1 = f32[1,4,80,128]{3,2,1,0:T(8,128)S(1)} collective-permute-done((f32[1,4,80,128]{3,2,1,0:T(8,128)S(1)}, f32[1,4,80,128]{3,2,1,0:T(8,128)S(1)}, u32[]{:S(2)}, u32[]{:S(2)}) %collective-permute-start.1) | collective-permute-done | bytes 163872 | tf_op jit(solution)/shard_map/ppermute | solution.py:390
  22.8 0.1 broadcast_select_fusion
  23.0 0.1 collective-permute-start.2
  23.1 0.0 copy-done
  23.1 0.0 copy-start.2
  23.1 0.9 %copy-done.2 = f32[4,16,512]{2,1,0:T(8,128)S(1)} copy-done((f32[4,16,512]{2,1,0:T(8,128)S(1)}, f32[4,16,512]{2,1,0:T(8,128)}, u32[]{:S(2)}) %copy-start.2) | copy-done | bytes 131096
  24.0 1.4 %image_across.1 = (bf16[2,1280,512]{2,1,0:T(8,128)(2,1)S(1)}, bf16[2,512,128]{2,1,0:T(8,128)(2,1)S(1)}) custom-call(s32[2]{0:T(128)S(1)} %copy-done.4, s32[2,8,10]{2,1,0:T(8,128)S(1)} %copy-done.3, f32[4,16,512]{2,1,0:T(8,128)S(1)} %copy-done.2, bf16[8,2,512,128]{3,2,1,0:T(8,128)(2,1)S(1)} %copy-done, f32[2,2,80,128]{3,2,1,0:T(8,128)S(1)} %copy.11.after_ref), custom_call_target="tpu_custom_call" | custom-call | flops 100000000 | bytes 6000000 | tf_op jit(solution)/shard_map/image_across/pallas_call | solution.py:356
  25.4 2.9 %collective-permute-done.2 = f32[2,2,80,128]{3,2,0,1:T(8,128)S(1)} collective-permute-done((f32[2,2,80,128]{3,2,0,1:T(8,128)S(1)}, f32[2,2,80,128]{3,2,0,1:T(8,128)S(1)}, u32[]{:S(2)}, u32[]{:S(2)}) %collective-permute-start.2) | collective-permute-done | bytes 163872 | tf_op jit(solution)/shard_map/ppermute | solution.py:390
  28.3 0.1 fusion.1
  28.4 3.0 %collective-permute-start.3 = (f32[2,1,80,128]{3,2,0,1:T(8,128)S(1)}, f32[2,1,80,128]{3,2,0,1:T(8,128)S(1)}, u32[]{:S(2)}, u32[]{:S(2)}) collective-permute-start(f32[2,1,80,128]{3,2,0,1:T(8,128)S(1)} %slice_bitcast_fusion.3), channel_id=1, source_target_pairs={{0,16},{1,17},{2,18},{3,19},{4,20},{5,21},{6,22},{7,23},{8,24},{9,... | collective-permute-start | bytes 245768 | tf_op jit(solution)/shard_map/ppermute | solution.py:390
  31.4 3.0 %collective-permute-done.3 = f32[2,1,80,128]{3,2,0,1:T(8,128)S(1)} collective-permute-done((f32[2,1,80,128]{3,2,0,1:T(8,128)S(1)}, f32[2,1,80,128]{3,2,0,1:T(8,128)S(1)}, u32[]{:S(2)}, u32[]{:S(2)}) %collective-permute-start.3) | collective-permute-done | bytes 81952 | tf_op jit(solution)/shard_map/ppermute | solution.py:390
  34.4 0.1 fusion.3
  34.5 2.8 %collective-permute-start.4 = (f32[2,80,128]{2,1,0:T(8,128)S(1)}, f32[2,80,128]{2,1,0:T(8,128)S(1)}, u32[]{:S(2)}, u32[]{:S(2)}) collective-permute-start(f32[2,80,128]{2,1,0:T(8,128)S(1)} %fusion.3), channel_id=1, source_target_pairs={{0,2},{1,3},{2,0},{3,1},{4,6},{5,7},{6,4},{7,5},{8,10},{9,11},{10,... | collective-permute-start | bytes 245768 | tf_op jit(solution)/shard_map/ppermute | solution.py:390
  37.3 2.4 %collective-permute-done.4 = f32[2,80,128]{2,1,0:T(8,128)S(1)} collective-permute-done((f32[2,80,128]{2,1,0:T(8,128)S(1)}, f32[2,80,128]{2,1,0:T(8,128)S(1)}, u32[]{:S(2)}, u32[]{:S(2)}) %collective-permute-start.4) | collective-permute-done | bytes 81952 | tf_op jit(solution)/shard_map/ppermute | solution.py:390
  39.7 0.1 collective-permute-start.5
  39.8 1.3 %collective-permute-done.5.other_ref = f32[2,80,128]{2,1,0:T(8,128)S(1)} collective-permute-done((f32[2,80,128]{2,1,0:T(8,128)S(1)}, f32[2,80,128]{2,1,0:T(8,128)S(1)}, u32[]{:S(2)}, u32[]{:S(2)}) %collective-permute-start.5) | collective-permute-done | bytes 81952 | tf_op jit(solution)/shard_map/ppermute | solution.py:390
  41.1 1.8 %image_blocks.1 = f32[1,128,512]{2,1,0:T(8,128)} custom-call(f32[2,80,128]{2,1,0:T(8,128)S(1)} %add.3.own_ref, f32[2,80,128]{2,1,0:T(8,128)S(1)} %collective-permute-done.5.other_ref, f32[2,128,320]{2,1,0:T(8,128)S(1)} %image_down.1.down_ref, bf16[2,1280,512]{2,1,0:T(8,128)(2,1)S(1)} %get-tuple-element.21.across_ref, ...), custom_call_target="tpu_custom_call" | custom-call | tf_op jit(solution)/shard_map/image_blocks/pallas_call | solution.py:373
  (5 shorter events, 0.0 us)
Async XLA Ops:
  0.0 23.1 %copy-start = (bf16[8,2,512,128]{3,2,1,0:T(8,128)(2,1)S(1)}, bf16[8,2,512,128]{3,2,1,0:T(8,128)(2,1)}, u32[]{:S(2)}) copy-start(bf16[8,2,512,128]{3,2,1,0:T(8,128)(2,1)} %constant.20.clone.tables_ref) | copy-start | bytes 6291460
  0.0 3.0 %collective-permute-start = (f32[1,10,2,32,128]{4,3,2,1,0:T(8,128)}, f32[1,10,2,32,128]{4,3,2,1,0:T(8,128)S(1)}, u32[]{:S(2)}, u32[]{:S(2)}) collective-permute-start(f32[1,10,2,32,128]{4,3,2,1,0:T(8,128)} %param.8), channel_id=1, source_target_pairs={{0,1},{1,0},{2,3},{3,2},{4,5},{5,4},{6,7},{7,6},{8,9},{9,8},{10,11... | collective-permute-start | bytes 983048 | tf_op jit(solution)/shard_map/ppermute | solution.py:390
  3.0 1.0 %copy-start.1 = (f32[5,112,128]{2,1,0:T(8,128)S(1)}, f32[5,112,128]{2,1,0:T(8,128)}, u32[]{:S(2)}) copy-start(f32[5,112,128]{2,1,0:T(8,128)} %gather_blocks.1.own_ref) | copy-start | bytes 860164
  17.5 5.4 %collective-permute-start.1 = (f32[1,4,80,128]{3,2,1,0:T(8,128)S(1)}, f32[1,4,80,128]{3,2,1,0:T(8,128)S(1)}, u32[]{:S(2)}, u32[]{:S(2)}) collective-permute-start(f32[1,4,80,128]{3,2,1,0:T(8,128)S(1)} %bitcast.25), channel_id=1, source_target_pairs={{0,4},{1,9},{2,6},{3,11},{4,0},{5,13},{6,2},{7,15},{8,12},{9,1},{1... | collective-permute-start | bytes 491528 | tf_op jit(solution)/shard_map/ppermute | solution.py:390
  18.2 0.7 %copy-start.3 = (s32[2,8,10]{2,1,0:T(8,128)S(1)}, s32[2,8,10]{2,1,0:T(8,128)}, u32[]{:S(2)}) copy-start(s32[2,8,10]{2,1,0:T(8,128)} %corners_ref.3) | copy-start | bytes 1924
  18.9 0.7 %copy-start.4 = (s32[2]{0:T(128)S(1)}, s32[2]{0:T(128)}, u32[]{:S(2)}) copy-start(s32[2]{0:T(128)} %owners_ref.3) | copy-start | bytes 28
  19.6 0.7 %copy-start.5 = (s32[1,20]{1,0:T(1,128)S(1)}, s32[1,20]{1,0:T(1,128)}, u32[]{:S(2)}) copy-start(s32[1,20]{1,0:T(1,128)} %assign_ref.1) | copy-start | bytes 244
  23.0 5.4 %collective-permute-start.2 = (f32[2,2,80,128]{3,2,0,1:T(8,128)S(1)}, f32[2,2,80,128]{3,2,0,1:T(8,128)S(1)}, u32[]{:S(2)}, u32[]{:S(2)}) collective-permute-start(f32[2,2,80,128]{3,2,0,1:T(8,128)S(1)} %slice_bitcast_fusion.1), channel_id=1, source_target_pairs={{0,8},{1,5},{2,10},{3,7},{4,12},{5,1},{6,14},{7,3},{8,0},{9,13},{1... | collective-permute-start | bytes 491528 | tf_op jit(solution)/shard_map/ppermute | solution.py:390
  23.1 0.9 %copy-start.2 = (f32[4,16,512]{2,1,0:T(8,128)S(1)}, f32[4,16,512]{2,1,0:T(8,128)}, u32[]{:S(2)}) copy-start(f32[4,16,512]{2,1,0:T(8,128)} %constant.21.clone.second_ref) | copy-start | bytes 393220
  28.4 6.0 %collective-permute-start.3 = (f32[2,1,80,128]{3,2,0,1:T(8,128)S(1)}, f32[2,1,80,128]{3,2,0,1:T(8,128)S(1)}, u32[]{:S(2)}, u32[]{:S(2)}) collective-permute-start(f32[2,1,80,128]{3,2,0,1:T(8,128)S(1)} %slice_bitcast_fusion.3), channel_id=1, source_target_pairs={{0,16},{1,17},{2,18},{3,19},{4,20},{5,21},{6,22},{7,23},{8,24},{9,... | collective-permute-start | bytes 245768 | tf_op jit(solution)/shard_map/ppermute | solution.py:390
  34.5 5.2 %collective-permute-start.4 = (f32[2,80,128]{2,1,0:T(8,128)S(1)}, f32[2,80,128]{2,1,0:T(8,128)S(1)}, u32[]{:S(2)}, u32[]{:S(2)}) collective-permute-start(f32[2,80,128]{2,1,0:T(8,128)S(1)} %fusion.3), channel_id=1, source_target_pairs={{0,2},{1,3},{2,0},{3,1},{4,6},{5,7},{6,4},{7,5},{8,10},{9,11},{10,... | collective-permute-start | bytes 245768 | tf_op jit(solution)/shard_map/ppermute | solution.py:390
  39.7 1.3 %collective-permute-start.5 = (f32[2,80,128]{2,1,0:T(8,128)S(1)}, f32[2,80,128]{2,1,0:T(8,128)S(1)}, u32[]{:S(2)}, u32[]{:S(2)}) collective-permute-start(f32[2,80,128]{2,1,0:T(8,128)S(1)} %add.3.own_ref), channel_id=1, source_target_pairs={{0,1},{1,0},{2,3},{3,2},{4,5},{5,4},{6,7},{7,6},{8,9},{9,8},{10,11... | collective-permute-start | bytes 245768 | tf_op jit(solution)/shard_map/ppermute | solution.py:390

commit v6 on v5

--- a/solution.py
+++ b/solution.py
@@ -144,45 +144,39 @@
                 turn = times(turn, turn)
             z_ref[k, COLUMNS + 2 * axis, 0:channels] = turn[0]
             z_ref[k, COLUMNS + 2 * axis + 1, 0:channels] = turn[1]
-        for c in range(channels):
-
-            def row_of(i):
-                return z_ref[k, i, c : c + 1]
-
-            def base_of(i):
-                return base_ref[k, BASE * c + 8 * i : BASE * c + 8 * i + 8, :]
-
-            at = k * channels + c
-            turn = (row_of(COLUMNS), row_of(COLUMNS + 1))
-            twice = 2.0 * turn[0]
-            wave = (base_of(0), base_of(1))
-            after = times(wave, turn)
-            for i in range(COLUMNS):
-                for part in range(2):
-                    left_ref[at, 128 * part + 16 * i : 128 * part + 16 * i + 16] = jnp.concatenate(
-                        [wave[part], after[part]], axis=0
-                    ).astype(jnp.bfloat16)
-                if i < COLUMNS - 1:
-                    wave = tuple(twice * after[part] - wave[part] for part in range(2))
-                    after = tuple(twice * wave[part] - after[part] for part in range(2))
-            turn = (row_of(COLUMNS + 2), row_of(COLUMNS + 3))
-            wave = (base_of(2), base_of(3))
-            after = times(wave, turn)
-            both = tuple(jnp.concatenate([wave[part], after[part]], axis=0) for part in range(2))
-            for g in range(COLUMNS // 2):
-                for part in range(2):
-                    turned = row_of(2 * g + part)
-                    for kind in range(2):
-                        row = 64 * g + 32 * part + 16 * kind
-                        right_ref[at, row : row + 16] = (turned * both[kind]).astype(jnp.bfloat16)
-
-    def finish():
-        product = None
-        for c in range(0, 2 * channels, 2):
-            right = jnp.concatenate([right_ref[c, 0:256], right_ref[c + 1, 0:256]], axis=1)
-            left = jnp.concatenate([left_ref[c, 0:256], left_ref[c + 1, 0:256]], axis=1)
-            term = dot(right, left, 1)
-            product = term if product is None else product + term
+
+    def add_rows(k, c):
+        def row_of(i):
+            return z_ref[k, i, c : c + 1]
+
+        def base_of(i):
+            return base_ref[k, BASE * c + 8 * i : BASE * c + 8 * i + 8, :]
+
+        at = k * channels + c
+        turn = (row_of(COLUMNS), row_of(COLUMNS + 1))
+        twice = 2.0 * turn[0]
+        wave = (base_of(0), base_of(1))
+        after = times(wave, turn)
+        for i in range(COLUMNS):
+            for part in range(2):
+                left_ref[at, 128 * part + 16 * i : 128 * part + 16 * i + 16] = jnp.concatenate(
+                    [wave[part], after[part]], axis=0
+                ).astype(jnp.bfloat16)
+            if i < COLUMNS - 1:
+                wave = tuple(twice * after[part] - wave[part] for part in range(2))
+                after = tuple(twice * wave[part] - after[part] for part in range(2))
+        turn = (row_of(COLUMNS + 2), row_of(COLUMNS + 3))
+        wave = (base_of(2), base_of(3))
+        after = times(wave, turn)
+        both = tuple(jnp.concatenate([wave[part], after[part]], axis=0) for part in range(2))
+        for g in range(COLUMNS // 2):
+            for part in range(2):
+                turned = row_of(2 * g + part)
+                for kind in range(2):
+                    row = 64 * g + 32 * part + 16 * kind
+                    right_ref[at, row : row + 16] = (turned * both[kind]).astype(jnp.bfloat16)
+
+    def finish(product):
         group = lax.broadcasted_iota(jnp.int32, (HALF, 128), 1) // SUB
         tiles = [None] * COLUMNS
         for sign in (1, -1):
@@ -210,8 +204,17 @@
     @pl.when(jnp.max(own_ref[step, 2 * channels + 40 : 2 * channels + 48]) > 0.0)
     def _():
         build(0)
-        build(1)
-        store(finish())
+        product = None
+        for c in range(0, 2 * channels, 2):
+            if c == channels // 2:
+                build(1)
+            for i in range(2):
+                add_rows(c // channels, c % channels + i)
+            right = jnp.concatenate([right_ref[c, 0:256], right_ref[c + 1, 0:256]], axis=1)
+            left = jnp.concatenate([left_ref[c, 0:256], left_ref[c + 1, 0:256]], axis=1)
+            term = dot(right, left, 1)
+            product = term if product is None else product + term
+        store(finish(product))
 
 
 def grid_blocks(own, other):

time: 43.1 us -> 42.5 us (0.986)
  starting transfers between devices: 6.45 us -> 21.6 us
  Pallas kernels: 19.4 us -> 6.55 us
  waiting for transfers between devices: 11.2 us -> 8.46 us
    ppermute x6, starting transfers between devices: 6.45 us -> 21.6 us  [swap(): return lax.ppermute(value, ('facet', 'freq'), pairs)]
    pallas_call x1, Pallas kernels: 13.5 us -> 0.66 us  [grid_blocks(): pl.pallas_call(grid_kernel, grid=(facet_total // COLUMNS, half_blocks), i...]
    ppermute x6, waiting for transfers between devices: 11.2 us -> 8.46 us  [swap(): return lax.ppermute(value, ('facet', 'freq'), pairs)]
  transfers between devices with their start and end apart: 6 -> 6, of which waited for: 5 -> 4; matrix products, arithmetic and copies ran while one was open for 2% -> 2% of each run, Pallas kernels for 10% -> 10%
where the time goes in v6:
time: 42.5 us; the launch traced here: 42.4 us
  starting transfers between devices  21.6 us (51%)
  waiting for transfers between devices  8.46 us (20%)
  Pallas kernels  6.55 us (15%)
  local copies, waits for them, and re-layouts  3.89 us (9%)
  between operations  0.95 us (2%)
  other arithmetic  0.93 us (2%)
    ppermute x6, starting transfers between devices, swap(): return lax.ppermute(value, ('facet', 'freq'), pairs)  21.6 us
    ppermute x6, waiting for transfers between devices, swap(): return lax.ppermute(value, ('facet', 'freq'), pairs)  8.46 us
    unnamed x12, local copies, waits for them, and re-layouts  3.86 us
    pallas_call x1, Pallas kernels, image_blocks(): pl.pallas_call(image_kernel, in_specs=[pl.BlockSpec(memory_space=pltpu.VM...  1.77 us
    pallas_call x1, Pallas kernels, gather(): pl.pallas_call(gather_kernel, in_specs=[pl.BlockSpec(memory_space=pltpu.H...  1.7 us
    pallas_call x1, Pallas kernels, across_of(): pl.pallas_call(across_kernel, in_specs=[smem, smem, vmem] + [pl.BlockSpec...  1.45 us
    pallas_call x1, Pallas kernels, down_of(): pl.pallas_call(down_kernel, in_specs=[smem, smem, smem, smem, pl.BlockSpe...  0.96 us
  transfers between devices with their start and end apart: 6, of which 4 were waited for; matrix products, arithmetic and copies ran while one was open for 2% of the time, Pallas kernels for 10%

profile of v6, /device:TPU:0, one launch (start us, length us, event | category | flops | bytes accessed | tf_op | source)
XLA Modules:
  0.0 42.4 jit_solution(17577690518125580636)
XLA Ops:
  0.0 0.0 copy-start
  0.0 0.5 %collective-permute-start = (f32[1,10,2,32,128]{4,3,2,1,0:T(8,128)}, f32[1,10,2,32,128]{4,3,2,1,0:T(8,128)S(1)}, u32[]{:S(2)}, u32[]{:S(2)}) collective-permute-start(f32[1,10,2,32,128]{4,3,2,1,0:T(8,128)} %param.8), channel_id=1, source_target_pairs={{0,1},{1,0},{2,3},{3,2},{4,5},{5,4},{6,7},{7,6},{8,9},{9,8},{10,11... | collective-permute-start | bytes 983048 | tf_op jit(solution)/shard_map/ppermute | solution.py:393
  1.3 1.7 %gather_blocks.1.own_ref = f32[5,112,128]{2,1,0:T(8,128)} custom-call(s32[2]{0:T(128)} %owners_ref.3, s32[2,8,10]{2,1,0:T(8,128)} %corners_ref.3, f32[10,3,1,128]{3,2,1,0:T(1,128)} %bitcast.30, f32[10,64,128]{2,1,0:T(8,128)} %bitcast.28), custom_call_target="tpu_custom_call" | custom-call | tf_op jit(solution)/shard_map/gather_blocks/pallas_call | solution.py:82
  3.0 0.0 collective-permute-done.other_ref
  3.0 0.0 copy-start.1
  3.0 0.9 %copy-done.1 = f32[5,112,128]{2,1,0:T(8,128)S(1)} copy-done((f32[5,112,128]{2,1,0:T(8,128)S(1)}, f32[5,112,128]{2,1,0:T(8,128)}, u32[]{:S(2)}) %copy-start.1) | copy-done | bytes 286744
  4.0 0.7 %grid_blocks.1 = (f32[4,80,128]{2,1,0:T(8,128)S(1)}, f32[4,80,128]{2,1,0:T(8,128)S(1)}) custom-call(f32[5,112,128]{2,1,0:T(8,128)S(1)} %copy-done.1, f32[1,10,2,32,128]{4,3,2,1,0:T(8,128)S(1)} %collective-permute-done.other_ref), custom_call_target="tpu_custom_call" | custom-call | tf_op jit(solution)/shard_map/grid_blocks/pallas_call | solution.py:226
  4.6 2.5 %collective-permute-start.1 = (f32[1,4,80,128]{3,2,1,0:T(8,128)S(1)}, f32[1,4,80,128]{3,2,1,0:T(8,128)S(1)}, u32[]{:S(2)}, u32[]{:S(2)}) collective-permute-start(f32[1,4,80,128]{3,2,1,0:T(8,128)S(1)} %bitcast.25), channel_id=1, source_target_pairs={{0,4},{1,9},{2,6},{3,11},{4,0},{5,13},{6,2},{7,15},{8,12},{9,1},{1... | collective-permute-start | bytes 491528 | tf_op jit(solution)/shard_map/ppermute | solution.py:393
  7.2 0.7 %and_compare_fusion.2 = (pred[2]{0:T(512)(128)(4,1)S(1)}, pred[2]{0:T(512)(128)(4,1)S(1)}, pred[2]{0:T(512)(128)(4,1)S(1)}) fusion(s32[2]{0:T(128)} %owners_ref.3, s32[]{:T(128)S(6)} %axis_index.23, s32[]{:T(128)S(6)} %select_n.21, s32[]{:T(128)S(6)} %select_n.22), kind=kLoop, calls=%fused_computation.11 | loop fusion | flops 20 | bytes 26 | tf_op jit(solution)/shard_map/eq | solution.py:424
  7.8 0.0 copy-start.3
  7.8 0.7 %copy-done.3 = s32[2,8,10]{2,1,0:T(8,128)S(1)} copy-done((s32[2,8,10]{2,1,0:T(8,128)S(1)}, s32[2,8,10]{2,1,0:T(8,128)}, u32[]{:S(2)}) %copy-start.3) | copy-done | bytes 664
  8.5 0.0 copy-start.4
  8.5 0.7 %copy-done.4 = s32[2]{0:T(128)S(1)} copy-done((s32[2]{0:T(128)S(1)}, s32[2]{0:T(128)}, u32[]{:S(2)}) %copy-start.4) | copy-done | bytes 32
  9.2 0.7 %copy-done.5 = s32[1,20]{1,0:T(1,128)S(1)} copy-done((s32[1,20]{1,0:T(1,128)S(1)}, s32[1,20]{1,0:T(1,128)}, u32[]{:S(2)}) %copy-start.5) | copy-done | bytes 104
  9.8 1.0 %image_down.1.down_ref = f32[2,128,320]{2,1,0:T(8,128)S(1)} custom-call(s32[2]{0:T(128)S(1)} %copy-done.4, s32[2,8,10]{2,1,0:T(8,128)S(1)} %copy-done.3, s32[1,20]{1,0:T(1,128)S(1)} %copy-done.5, s32[1]{0:T(128)S(6)} %copy.16.counts_ref, f32[1,4,80,128]{3,2,1,0:T(8,128)S(1)} %bitcast.26), custom_call_target="tpu_custom_call" | custom-call | flops 10000000 | bytes 1000000 | tf_op jit(solution)/shard_map/image_down/pallas_call | solution.py:344
  10.8 0.0 collective-permute-done.1
  10.8 0.1 broadcast_select_fusion
  10.9 1.8 %collective-permute-start.2 = (f32[2,2,80,128]{3,2,0,1:T(8,128)S(1)}, f32[2,2,80,128]{3,2,0,1:T(8,128)S(1)}, u32[]{:S(2)}, u32[]{:S(2)}) collective-permute-start(f32[2,2,80,128]{3,2,0,1:T(8,128)S(1)} %slice_bitcast_fusion.1), channel_id=1, source_target_pairs={{0,8},{1,5},{2,10},{3,7},{4,12},{5,1},{6,14},{7,3},{8,0},{9,13},{1... | collective-permute-start | bytes 491528 | tf_op jit(solution)/shard_map/ppermute | solution.py:393
  12.8 0.0 copy-done
  12.8 0.0 copy-start.2
  12.8 0.9 %copy-done.2 = f32[4,16,512]{2,1,0:T(8,128)S(1)} copy-done((f32[4,16,512]{2,1,0:T(8,128)S(1)}, f32[4,16,512]{2,1,0:T(8,128)}, u32[]{:S(2)}) %copy-start.2) | copy-done | bytes 131096
  13.7 1.4 %image_across.1 = (bf16[2,1280,512]{2,1,0:T(8,128)(2,1)S(1)}, bf16[2,512,128]{2,1,0:T(8,128)(2,1)S(1)}) custom-call(s32[2]{0:T(128)S(1)} %copy-done.4, s32[2,8,10]{2,1,0:T(8,128)S(1)} %copy-done.3, f32[4,16,512]{2,1,0:T(8,128)S(1)} %copy-done.2, bf16[8,2,512,128]{3,2,1,0:T(8,128)(2,1)S(1)} %copy-done, f32[2,2,80,128]{3,2,1,0:T(8,128)S(1)} %copy.11.after_ref), custom_call_target="tpu_custom_call" | custom-call | flops 100000000 | bytes 6000000 | tf_op jit(solution)/shard_map/image_across/pallas_call | solution.py:359
  15.1 1.2 %collective-permute-done.2 = f32[2,2,80,128]{3,2,0,1:T(8,128)S(1)} collective-permute-done((f32[2,2,80,128]{3,2,0,1:T(8,128)S(1)}, f32[2,2,80,128]{3,2,0,1:T(8,128)S(1)}, u32[]{:S(2)}, u32[]{:S(2)}) %collective-permute-start.2) | collective-permute-done | bytes 163872 | tf_op jit(solution)/shard_map/ppermute | solution.py:393
  16.3 0.1 fusion.1
  16.4 15.2 %collective-permute-start.3 = (f32[2,1,80,128]{3,2,0,1:T(8,128)S(1)}, f32[2,1,80,128]{3,2,0,1:T(8,128)S(1)}, u32[]{:S(2)}, u32[]{:S(2)}) collective-permute-start(f32[2,1,80,128]{3,2,0,1:T(8,128)S(1)} %slice_bitcast_fusion.3), channel_id=1, source_target_pairs={{0,16},{1,17},{2,18},{3,19},{4,20},{5,21},{6,22},{7,23},{8,24},{9,... | collective-permute-start | bytes 245768 | tf_op jit(solution)/shard_map/ppermute | solution.py:393
  31.6 3.1 %collective-permute-done.3 = f32[2,1,80,128]{3,2,0,1:T(8,128)S(1)} collective-permute-done((f32[2,1,80,128]{3,2,0,1:T(8,128)S(1)}, f32[2,1,80,128]{3,2,0,1:T(8,128)S(1)}, u32[]{:S(2)}, u32[]{:S(2)}) %collective-permute-start.3) | collective-permute-done | bytes 81952 | tf_op jit(solution)/shard_map/ppermute | solution.py:393
  34.7 0.1 fusion.3
  34.8 1.5 %collective-permute-start.4 = (f32[2,80,128]{2,1,0:T(8,128)S(1)}, f32[2,80,128]{2,1,0:T(8,128)S(1)}, u32[]{:S(2)}, u32[]{:S(2)}) collective-permute-start(f32[2,80,128]{2,1,0:T(8,128)S(1)} %fusion.3), channel_id=1, source_target_pairs={{0,2},{1,3},{2,0},{3,1},{4,6},{5,7},{6,4},{7,5},{8,10},{9,11},{10,... | collective-permute-start | bytes 245768 | tf_op jit(solution)/shard_map/ppermute | solution.py:393
  36.3 2.9 %collective-permute-done.4 = f32[2,80,128]{2,1,0:T(8,128)S(1)} collective-permute-done((f32[2,80,128]{2,1,0:T(8,128)S(1)}, f32[2,80,128]{2,1,0:T(8,128)S(1)}, u32[]{:S(2)}, u32[]{:S(2)}) %collective-permute-start.4) | collective-permute-done | bytes 81952 | tf_op jit(solution)/shard_map/ppermute | solution.py:393
  39.2 0.1 collective-permute-start.5
  39.3 1.3 %collective-permute-done.5.other_ref = f32[2,80,128]{2,1,0:T(8,128)S(1)} collective-permute-done((f32[2,80,128]{2,1,0:T(8,128)S(1)}, f32[2,80,128]{2,1,0:T(8,128)S(1)}, u32[]{:S(2)}, u32[]{:S(2)}) %collective-permute-start.5) | collective-permute-done | bytes 81952 | tf_op jit(solution)/shard_map/ppermute | solution.py:393
  40.6 1.8 %image_blocks.1 = f32[1,128,512]{2,1,0:T(8,128)} custom-call(f32[2,80,128]{2,1,0:T(8,128)S(1)} %add.3.own_ref, f32[2,80,128]{2,1,0:T(8,128)S(1)} %collective-permute-done.5.other_ref, f32[2,128,320]{2,1,0:T(8,128)S(1)} %image_down.1.down_ref, bf16[2,1280,512]{2,1,0:T(8,128)(2,1)S(1)} %get-tuple-element.21.across_ref, ...), custom_call_target="tpu_custom_call" | custom-call | tf_op jit(solution)/shard_map/image_blocks/pallas_call | solution.py:376
  (5 shorter events, 0.0 us)
Async XLA Ops:
  0.0 12.8 %copy-start = (bf16[8,2,512,128]{3,2,1,0:T(8,128)(2,1)S(1)}, bf16[8,2,512,128]{3,2,1,0:T(8,128)(2,1)}, u32[]{:S(2)}) copy-start(bf16[8,2,512,128]{3,2,1,0:T(8,128)(2,1)} %constant.20.clone.tables_ref) | copy-start | bytes 6291460
  0.0 3.0 %collective-permute-start = (f32[1,10,2,32,128]{4,3,2,1,0:T(8,128)}, f32[1,10,2,32,128]{4,3,2,1,0:T(8,128)S(1)}, u32[]{:S(2)}, u32[]{:S(2)}) collective-permute-start(f32[1,10,2,32,128]{4,3,2,1,0:T(8,128)} %param.8), channel_id=1, source_target_pairs={{0,1},{1,0},{2,3},{3,2},{4,5},{5,4},{6,7},{7,6},{8,9},{9,8},{10,11... | collective-permute-start | bytes 983048 | tf_op jit(solution)/shard_map/ppermute | solution.py:393
  3.0 1.0 %copy-start.1 = (f32[5,112,128]{2,1,0:T(8,128)S(1)}, f32[5,112,128]{2,1,0:T(8,128)}, u32[]{:S(2)}) copy-start(f32[5,112,128]{2,1,0:T(8,128)} %gather_blocks.1.own_ref) | copy-start | bytes 860164
  4.6 6.2 %collective-permute-start.1 = (f32[1,4,80,128]{3,2,1,0:T(8,128)S(1)}, f32[1,4,80,128]{3,2,1,0:T(8,128)S(1)}, u32[]{:S(2)}, u32[]{:S(2)}) collective-permute-start(f32[1,4,80,128]{3,2,1,0:T(8,128)S(1)} %bitcast.25), channel_id=1, source_target_pairs={{0,4},{1,9},{2,6},{3,11},{4,0},{5,13},{6,2},{7,15},{8,12},{9,1},{1... | collective-permute-start | bytes 491528 | tf_op jit(solution)/shard_map/ppermute | solution.py:393
  7.8 0.7 %copy-start.3 = (s32[2,8,10]{2,1,0:T(8,128)S(1)}, s32[2,8,10]{2,1,0:T(8,128)}, u32[]{:S(2)}) copy-start(s32[2,8,10]{2,1,0:T(8,128)} %corners_ref.3) | copy-start | bytes 1924
  8.5 0.7 %copy-start.4 = (s32[2]{0:T(128)S(1)}, s32[2]{0:T(128)}, u32[]{:S(2)}) copy-start(s32[2]{0:T(128)} %owners_ref.3) | copy-start | bytes 28
  9.2 0.7 %copy-start.5 = (s32[1,20]{1,0:T(1,128)S(1)}, s32[1,20]{1,0:T(1,128)}, u32[]{:S(2)}) copy-start(s32[1,20]{1,0:T(1,128)} %assign_ref.1) | copy-start | bytes 244
  10.9 5.4 %collective-permute-start.2 = (f32[2,2,80,128]{3,2,0,1:T(8,128)S(1)}, f32[2,2,80,128]{3,2,0,1:T(8,128)S(1)}, u32[]{:S(2)}, u32[]{:S(2)}) collective-permute-start(f32[2,2,80,128]{3,2,0,1:T(8,128)S(1)} %slice_bitcast_fusion.1), channel_id=1, source_target_pairs={{0,8},{1,5},{2,10},{3,7},{4,12},{5,1},{6,14},{7,3},{8,0},{9,13},{1... | collective-permute-start | bytes 491528 | tf_op jit(solution)/shard_map/ppermute | solution.py:393
  12.8 0.9 %copy-start.2 = (f32[4,16,512]{2,1,0:T(8,128)S(1)}, f32[4,16,512]{2,1,0:T(8,128)}, u32[]{:S(2)}) copy-start(f32[4,16,512]{2,1,0:T(8,128)} %constant.21.clone.second_ref) | copy-start | bytes 393220
  16.4 18.3 %collective-permute-start.3 = (f32[2,1,80,128]{3,2,0,1:T(8,128)S(1)}, f32[2,1,80,128]{3,2,0,1:T(8,128)S(1)}, u32[]{:S(2)}, u32[]{:S(2)}) collective-permute-start(f32[2,1,80,128]{3,2,0,1:T(8,128)S(1)} %slice_bitcast_fusion.3), channel_id=1, source_target_pairs={{0,16},{1,17},{2,18},{3,19},{4,20},{5,21},{6,22},{7,23},{8,24},{9,... | collective-permute-start | bytes 245768 | tf_op jit(solution)/shard_map/ppermute | solution.py:393
  34.8 4.4 %collective-permute-start.4 = (f32[2,80,128]{2,1,0:T(8,128)S(1)}, f32[2,80,128]{2,1,0:T(8,128)S(1)}, u32[]{:S(2)}, u32[]{:S(2)}) collective-permute-start(f32[2,80,128]{2,1,0:T(8,128)S(1)} %fusion.3), channel_id=1, source_target_pairs={{0,2},{1,3},{2,0},{3,1},{4,6},{5,7},{6,4},{7,5},{8,10},{9,11},{10,... | collective-permute-start | bytes 245768 | tf_op jit(solution)/shard_map/ppermute | solution.py:393
  39.2 1.3 %collective-permute-start.5 = (f32[2,80,128]{2,1,0:T(8,128)S(1)}, f32[2,80,128]{2,1,0:T(8,128)S(1)}, u32[]{:S(2)}, u32[]{:S(2)}) collective-permute-start(f32[2,80,128]{2,1,0:T(8,128)S(1)} %add.3.own_ref), channel_id=1, source_target_pairs={{0,1},{1,0},{2,3},{3,2},{4,5},{5,4},{6,7},{7,6},{8,9},{9,8},{10,11... | collective-permute-start | bytes 245768 | tf_op jit(solution)/shard_map/ppermute | solution.py:393

commit v7 on v6

--- a/solution.py
+++ b/solution.py
@@ -13,7 +13,7 @@
 G = 512
 HALF = SUB // 2
 COLUMNS = 8
-BASE = 40
+BASE = 56
 PAD = 16
 
 two_pi = 2.0 * math.pi
@@ -132,14 +132,17 @@
         for axis, delta in enumerate((delta_u, delta_v)):
             wave = cos_sin(delta * (0.5 / SUB))
             turn = times(wave, wave)
-            for j in range(8):
+            count = 8 + 8 * axis
+            for j in range(count):
                 base_ref[k, pl.ds(16 * axis + j, channels, stride=BASE), :] = wave[0]
-                base_ref[k, pl.ds(16 * axis + 8 + j, channels, stride=BASE), :] = wave[1]
+                base_ref[k, pl.ds(16 * axis + count + j, channels, stride=BASE), :] = wave[1]
                 if j == 0:
                     last, wave = wave, times(wave, turn)
                     twice = 2.0 * turn[0]
-                elif j < 7:
+                elif j < count - 1:
                     last, wave = wave, tuple(twice * wave[part] - last[part] for part in range(2))
+            if axis == 1:
+                break
             for _ in range(3):
                 turn = times(turn, turn)
             z_ref[k, COLUMNS + 2 * axis, 0:channels] = turn[0]
@@ -165,10 +168,7 @@
             if i < COLUMNS - 1:
                 wave = tuple(twice * after[part] - wave[part] for part in range(2))
                 after = tuple(twice * wave[part] - after[part] for part in range(2))
-        turn = (row_of(COLUMNS + 2), row_of(COLUMNS + 3))
-        wave = (base_of(2), base_of(3))
-        after = times(wave, turn)
-        both = tuple(jnp.concatenate([wave[part], after[part]], axis=0) for part in range(2))
+        both = tuple(base_ref[k, BASE * c + 16 + 16 * i : BASE * c + 32 + 16 * i, :] for i in range(2))
         for g in range(COLUMNS // 2):
             for part in range(2):
                 turned = row_of(2 * g + part)

time: 42.5 us -> 42.7 us (level)
  starting transfers between devices: 21.6 us -> 6.46 us
  Pallas kernels: 6.55 us -> 19.2 us
  waiting for transfers between devices: 8.46 us -> 11.2 us
    ppermute x6, starting transfers between devices: 21.6 us -> 6.46 us  [swap(): return lax.ppermute(value, ('facet', 'freq'), pairs)]
    pallas_call x1, Pallas kernels: 0.66 us -> 13.3 us  [grid_blocks(): pl.pallas_call(grid_kernel, grid=(facet_total // COLUMNS, half_blocks), i...]
    ppermute x6, waiting for transfers between devices: 8.46 us -> 11.2 us  [swap(): return lax.ppermute(value, ('facet', 'freq'), pairs)]
  transfers between devices with their start and end apart: 6 -> 6, of which waited for: 4 -> 5; matrix products, arithmetic and copies ran while one was open for 2% -> 2% of each run, Pallas kernels for 10% -> 10%
where the time goes in v7:
time: 42.7 us
  Pallas kernels  19.2 us (45%)
  waiting for transfers between devices  11.2 us (26%)
  starting transfers between devices  6.46 us (15%)
  local copies, waits for them, and re-layouts  3.89 us (9%)
  between operations  0.96 us (2%)
  other arithmetic  0.93 us (2%)
    pallas_call x1, Pallas kernels, grid_blocks(): pl.pallas_call(grid_kernel, grid=(facet_total // COLUMNS, half_blocks), i...  13.3 us
    ppermute x6, waiting for transfers between devices, swap(): return lax.ppermute(value, ('facet', 'freq'), pairs)  11.2 us
    ppermute x6, starting transfers between devices, swap(): return lax.ppermute(value, ('facet', 'freq'), pairs)  6.46 us
    unnamed x12, local copies, waits for them, and re-layouts  3.86 us
    pallas_call x1, Pallas kernels, image_blocks(): pl.pallas_call(image_kernel, in_specs=[pl.BlockSpec(memory_space=pltpu.VM...  1.78 us
    pallas_call x1, Pallas kernels, gather(): pl.pallas_call(gather_kernel, in_specs=[pl.BlockSpec(memory_space=pltpu.H...  1.7 us
    pallas_call x1, Pallas kernels, across_of(): pl.pallas_call(across_kernel, in_specs=[smem, smem, vmem] + [pl.BlockSpec...  1.45 us
    pallas_call x1, Pallas kernels, down_of(): pl.pallas_call(down_kernel, in_specs=[smem, smem, smem, smem, pl.BlockSpe...  0.96 us
  transfers between devices with their start and end apart: 6, of which 5 were waited for; matrix products, arithmetic and copies ran while one was open for 2% of the time, Pallas kernels for 10%

profile of v7, /device:TPU:0, one launch (start us, length us, event | category | flops | bytes accessed | tf_op | source)
XLA Modules:
  0.0 42.7 jit_solution(14364060072047303277)
XLA Ops:
  0.0 0.0 copy-start
  0.0 0.5 %collective-permute-start = (f32[1,10,2,32,128]{4,3,2,1,0:T(8,128)}, f32[1,10,2,32,128]{4,3,2,1,0:T(8,128)S(1)}, u32[]{:S(2)}, u32[]{:S(2)}) collective-permute-start(f32[1,10,2,32,128]{4,3,2,1,0:T(8,128)} %param.8), channel_id=1, source_target_pairs={{0,1},{1,0},{2,3},{3,2},{4,5},{5,4},{6,7},{7,6},{8,9},{9,8},{10,11... | collective-permute-start | bytes 983048 | tf_op jit(solution)/shard_map/ppermute | solution.py:393
  1.3 1.7 %gather_blocks.1.own_ref = f32[5,112,128]{2,1,0:T(8,128)} custom-call(s32[2]{0:T(128)} %owners_ref.3, s32[2,8,10]{2,1,0:T(8,128)} %corners_ref.3, f32[10,3,1,128]{3,2,1,0:T(1,128)} %bitcast.30, f32[10,64,128]{2,1,0:T(8,128)} %bitcast.28), custom_call_target="tpu_custom_call" | custom-call | tf_op jit(solution)/shard_map/gather_blocks/pallas_call | solution.py:82
  3.0 0.0 collective-permute-done.other_ref
  3.0 0.0 copy-start.1
  3.0 0.9 %copy-done.1 = f32[5,112,128]{2,1,0:T(8,128)S(1)} copy-done((f32[5,112,128]{2,1,0:T(8,128)S(1)}, f32[5,112,128]{2,1,0:T(8,128)}, u32[]{:S(2)}) %copy-start.1) | copy-done | bytes 286744
  4.0 13.3 %grid_blocks.1 = (f32[4,80,128]{2,1,0:T(8,128)S(1)}, f32[4,80,128]{2,1,0:T(8,128)S(1)}) custom-call(f32[5,112,128]{2,1,0:T(8,128)S(1)} %copy-done.1, f32[1,10,2,32,128]{4,3,2,1,0:T(8,128)S(1)} %collective-permute-done.other_ref), custom_call_target="tpu_custom_call" | custom-call | tf_op jit(solution)/shard_map/grid_blocks/pallas_call | solution.py:226
  17.3 0.1 collective-permute-start.1
  17.4 0.7 %and_compare_fusion.2 = (pred[2]{0:T(512)(128)(4,1)S(1)}, pred[2]{0:T(512)(128)(4,1)S(1)}, pred[2]{0:T(512)(128)(4,1)S(1)}) fusion(s32[2]{0:T(128)} %owners_ref.3, s32[]{:T(128)S(6)} %axis_index.23, s32[]{:T(128)S(6)} %select_n.21, s32[]{:T(128)S(6)} %select_n.22), kind=kLoop, calls=%fused_computation.11 | loop fusion | flops 20 | bytes 26 | tf_op jit(solution)/shard_map/eq | solution.py:424
  18.0 0.0 copy-start.3
  18.0 0.7 %copy-done.3 = s32[2,8,10]{2,1,0:T(8,128)S(1)} copy-done((s32[2,8,10]{2,1,0:T(8,128)S(1)}, s32[2,8,10]{2,1,0:T(8,128)}, u32[]{:S(2)}) %copy-start.3) | copy-done | bytes 664
  18.7 0.0 copy-start.4
  18.7 0.7 %copy-done.4 = s32[2]{0:T(128)S(1)} copy-done((s32[2]{0:T(128)S(1)}, s32[2]{0:T(128)}, u32[]{:S(2)}) %copy-start.4) | copy-done | bytes 32
  19.4 0.7 %copy-done.5 = s32[1,20]{1,0:T(1,128)S(1)} copy-done((s32[1,20]{1,0:T(1,128)S(1)}, s32[1,20]{1,0:T(1,128)}, u32[]{:S(2)}) %copy-start.5) | copy-done | bytes 104
  20.0 1.0 %image_down.1.down_ref = f32[2,128,320]{2,1,0:T(8,128)S(1)} custom-call(s32[2]{0:T(128)S(1)} %copy-done.4, s32[2,8,10]{2,1,0:T(8,128)S(1)} %copy-done.3, s32[1,20]{1,0:T(1,128)S(1)} %copy-done.5, s32[1]{0:T(128)S(6)} %copy.16.counts_ref, f32[1,4,80,128]{3,2,1,0:T(8,128)S(1)} %bitcast.26), custom_call_target="tpu_custom_call" | custom-call | flops 10000000 | bytes 1000000 | tf_op jit(solution)/shard_map/image_down/pallas_call | solution.py:344
  21.0 1.7 %collective-permute-done.1 = f32[1,4,80,128]{3,2,1,0:T(8,128)S(1)} collective-permute-done((f32[1,4,80,128]{3,2,1,0:T(8,128)S(1)}, f32[1,4,80,128]{3,2,1,0:T(8,128)S(1)}, u32[]{:S(2)}, u32[]{:S(2)}) %collective-permute-start.1) | collective-permute-done | bytes 163872 | tf_op jit(solution)/shard_map/ppermute | solution.py:393
  22.7 0.1 broadcast_select_fusion
  22.8 0.1 collective-permute-start.2
  22.9 0.0 copy-done
  22.9 0.0 copy-start.2
  22.9 0.9 %copy-done.2 = f32[4,16,512]{2,1,0:T(8,128)S(1)} copy-done((f32[4,16,512]{2,1,0:T(8,128)S(1)}, f32[4,16,512]{2,1,0:T(8,128)}, u32[]{:S(2)}) %copy-start.2) | copy-done | bytes 131096
  23.8 1.4 %image_across.1 = (bf16[2,1280,512]{2,1,0:T(8,128)(2,1)S(1)}, bf16[2,512,128]{2,1,0:T(8,128)(2,1)S(1)}) custom-call(s32[2]{0:T(128)S(1)} %copy-done.4, s32[2,8,10]{2,1,0:T(8,128)S(1)} %copy-done.3, f32[4,16,512]{2,1,0:T(8,128)S(1)} %copy-done.2, bf16[8,2,512,128]{3,2,1,0:T(8,128)(2,1)S(1)} %copy-done, f32[2,2,80,128]{3,2,1,0:T(8,128)S(1)} %copy.11.after_ref), custom_call_target="tpu_custom_call" | custom-call | flops 100000000 | bytes 6000000 | tf_op jit(solution)/shard_map/image_across/pallas_call | solution.py:359
  25.3 2.9 %collective-permute-done.2 = f32[2,2,80,128]{3,2,0,1:T(8,128)S(1)} collective-permute-done((f32[2,2,80,128]{3,2,0,1:T(8,128)S(1)}, f32[2,2,80,128]{3,2,0,1:T(8,128)S(1)}, u32[]{:S(2)}, u32[]{:S(2)}) %collective-permute-start.2) | collective-permute-done | bytes 163872 | tf_op jit(solution)/shard_map/ppermute | solution.py:393
  28.2 0.1 fusion.1
  28.3 3.0 %collective-permute-start.3 = (f32[2,1,80,128]{3,2,0,1:T(8,128)S(1)}, f32[2,1,80,128]{3,2,0,1:T(8,128)S(1)}, u32[]{:S(2)}, u32[]{:S(2)}) collective-permute-start(f32[2,1,80,128]{3,2,0,1:T(8,128)S(1)} %slice_bitcast_fusion.3), channel_id=1, source_target_pairs={{0,16},{1,17},{2,18},{3,19},{4,20},{5,21},{6,22},{7,23},{8,24},{9,... | collective-permute-start | bytes 245768 | tf_op jit(solution)/shard_map/ppermute | solution.py:393
  31.3 3.0 %collective-permute-done.3 = f32[2,1,80,128]{3,2,0,1:T(8,128)S(1)} collective-permute-done((f32[2,1,80,128]{3,2,0,1:T(8,128)S(1)}, f32[2,1,80,128]{3,2,0,1:T(8,128)S(1)}, u32[]{:S(2)}, u32[]{:S(2)}) %collective-permute-start.3) | collective-permute-done | bytes 81952 | tf_op jit(solution)/shard_map/ppermute | solution.py:393
  34.3 0.1 fusion.3
  34.3 2.8 %collective-permute-start.4 = (f32[2,80,128]{2,1,0:T(8,128)S(1)}, f32[2,80,128]{2,1,0:T(8,128)S(1)}, u32[]{:S(2)}, u32[]{:S(2)}) collective-permute-start(f32[2,80,128]{2,1,0:T(8,128)S(1)} %fusion.3), channel_id=1, source_target_pairs={{0,2},{1,3},{2,0},{3,1},{4,6},{5,7},{6,4},{7,5},{8,10},{9,11},{10,... | collective-permute-start | bytes 245768 | tf_op jit(solution)/shard_map/ppermute | solution.py:393
  37.1 2.4 %collective-permute-done.4 = f32[2,80,128]{2,1,0:T(8,128)S(1)} collective-permute-done((f32[2,80,128]{2,1,0:T(8,128)S(1)}, f32[2,80,128]{2,1,0:T(8,128)S(1)}, u32[]{:S(2)}, u32[]{:S(2)}) %collective-permute-start.4) | collective-permute-done | bytes 81952 | tf_op jit(solution)/shard_map/ppermute | solution.py:393
  39.6 0.1 collective-permute-start.5
  39.6 1.3 %collective-permute-done.5.other_ref = f32[2,80,128]{2,1,0:T(8,128)S(1)} collective-permute-done((f32[2,80,128]{2,1,0:T(8,128)S(1)}, f32[2,80,128]{2,1,0:T(8,128)S(1)}, u32[]{:S(2)}, u32[]{:S(2)}) %collective-permute-start.5) | collective-permute-done | bytes 81952 | tf_op jit(solution)/shard_map/ppermute | solution.py:393
  40.9 1.8 %image_blocks.1 = f32[1,128,512]{2,1,0:T(8,128)} custom-call(f32[2,80,128]{2,1,0:T(8,128)S(1)} %add.3.own_ref, f32[2,80,128]{2,1,0:T(8,128)S(1)} %collective-permute-done.5.other_ref, f32[2,128,320]{2,1,0:T(8,128)S(1)} %image_down.1.down_ref, bf16[2,1280,512]{2,1,0:T(8,128)(2,1)S(1)} %get-tuple-element.21.across_ref, ...), custom_call_target="tpu_custom_call" | custom-call | tf_op jit(solution)/shard_map/image_blocks/pallas_call | solution.py:376
  (5 shorter events, 0.0 us)
Async XLA Ops:
  0.0 22.9 %copy-start = (bf16[8,2,512,128]{3,2,1,0:T(8,128)(2,1)S(1)}, bf16[8,2,512,128]{3,2,1,0:T(8,128)(2,1)}, u32[]{:S(2)}) copy-start(bf16[8,2,512,128]{3,2,1,0:T(8,128)(2,1)} %constant.20.clone.tables_ref) | copy-start | bytes 6291460
  0.0 3.0 %collective-permute-start = (f32[1,10,2,32,128]{4,3,2,1,0:T(8,128)}, f32[1,10,2,32,128]{4,3,2,1,0:T(8,128)S(1)}, u32[]{:S(2)}, u32[]{:S(2)}) collective-permute-start(f32[1,10,2,32,128]{4,3,2,1,0:T(8,128)} %param.8), channel_id=1, source_target_pairs={{0,1},{1,0},{2,3},{3,2},{4,5},{5,4},{6,7},{7,6},{8,9},{9,8},{10,11... | collective-permute-start | bytes 983048 | tf_op jit(solution)/shard_map/ppermute | solution.py:393
  3.0 1.0 %copy-start.1 = (f32[5,112,128]{2,1,0:T(8,128)S(1)}, f32[5,112,128]{2,1,0:T(8,128)}, u32[]{:S(2)}) copy-start(f32[5,112,128]{2,1,0:T(8,128)} %gather_blocks.1.own_ref) | copy-start | bytes 860164
  17.3 5.4 %collective-permute-start.1 = (f32[1,4,80,128]{3,2,1,0:T(8,128)S(1)}, f32[1,4,80,128]{3,2,1,0:T(8,128)S(1)}, u32[]{:S(2)}, u32[]{:S(2)}) collective-permute-start(f32[1,4,80,128]{3,2,1,0:T(8,128)S(1)} %bitcast.25), channel_id=1, source_target_pairs={{0,4},{1,9},{2,6},{3,11},{4,0},{5,13},{6,2},{7,15},{8,12},{9,1},{1... | collective-permute-start | bytes 491528 | tf_op jit(solution)/shard_map/ppermute | solution.py:393
  18.0 0.7 %copy-start.3 = (s32[2,8,10]{2,1,0:T(8,128)S(1)}, s32[2,8,10]{2,1,0:T(8,128)}, u32[]{:S(2)}) copy-start(s32[2,8,10]{2,1,0:T(8,128)} %corners_ref.3) | copy-start | bytes 1924
  18.7 0.7 %copy-start.4 = (s32[2]{0:T(128)S(1)}, s32[2]{0:T(128)}, u32[]{:S(2)}) copy-start(s32[2]{0:T(128)} %owners_ref.3) | copy-start | bytes 28
  19.4 0.7 %copy-start.5 = (s32[1,20]{1,0:T(1,128)S(1)}, s32[1,20]{1,0:T(1,128)}, u32[]{:S(2)}) copy-start(s32[1,20]{1,0:T(1,128)} %assign_ref.1) | copy-start | bytes 244
  22.8 5.4 %collective-permute-start.2 = (f32[2,2,80,128]{3,2,0,1:T(8,128)S(1)}, f32[2,2,80,128]{3,2,0,1:T(8,128)S(1)}, u32[]{:S(2)}, u32[]{:S(2)}) collective-permute-start(f32[2,2,80,128]{3,2,0,1:T(8,128)S(1)} %slice_bitcast_fusion.1), channel_id=1, source_target_pairs={{0,8},{1,5},{2,10},{3,7},{4,12},{5,1},{6,14},{7,3},{8,0},{9,13},{1... | collective-permute-start | bytes 491528 | tf_op jit(solution)/shard_map/ppermute | solution.py:393
  22.9 0.9 %copy-start.2 = (f32[4,16,512]{2,1,0:T(8,128)S(1)}, f32[4,16,512]{2,1,0:T(8,128)}, u32[]{:S(2)}) copy-start(f32[4,16,512]{2,1,0:T(8,128)} %constant.21.clone.second_ref) | copy-start | bytes 393220
  28.3 6.0 %collective-permute-start.3 = (f32[2,1,80,128]{3,2,0,1:T(8,128)S(1)}, f32[2,1,80,128]{3,2,0,1:T(8,128)S(1)}, u32[]{:S(2)}, u32[]{:S(2)}) collective-permute-start(f32[2,1,80,128]{3,2,0,1:T(8,128)S(1)} %slice_bitcast_fusion.3), channel_id=1, source_target_pairs={{0,16},{1,17},{2,18},{3,19},{4,20},{5,21},{6,22},{7,23},{8,24},{9,... | collective-permute-start | bytes 245768 | tf_op jit(solution)/shard_map/ppermute | solution.py:393
  34.3 5.2 %collective-permute-start.4 = (f32[2,80,128]{2,1,0:T(8,128)S(1)}, f32[2,80,128]{2,1,0:T(8,128)S(1)}, u32[]{:S(2)}, u32[]{:S(2)}) collective-permute-start(f32[2,80,128]{2,1,0:T(8,128)S(1)} %fusion.3), channel_id=1, source_target_pairs={{0,2},{1,3},{2,0},{3,1},{4,6},{5,7},{6,4},{7,5},{8,10},{9,11},{10,... | collective-permute-start | bytes 245768 | tf_op jit(solution)/shard_map/ppermute | solution.py:393
  39.6 1.3 %collective-permute-start.5 = (f32[2,80,128]{2,1,0:T(8,128)S(1)}, f32[2,80,128]{2,1,0:T(8,128)S(1)}, u32[]{:S(2)}, u32[]{:S(2)}) collective-permute-start(f32[2,80,128]{2,1,0:T(8,128)S(1)} %add.3.own_ref), channel_id=1, source_target_pairs={{0,1},{1,0},{2,3},{3,2},{4,5},{5,4},{6,7},{7,6},{8,9},{9,8},{10,11... | collective-permute-start | bytes 245768 | tf_op jit(solution)/shard_map/ppermute | solution.py:393

commit v8 on v7

--- a/solution.py
+++ b/solution.py
@@ -13,7 +13,7 @@
 G = 512
 HALF = SUB // 2
 COLUMNS = 8
-BASE = 56
+BASE = 72
 PAD = 16
 
 two_pi = 2.0 * math.pi
@@ -132,21 +132,19 @@
         for axis, delta in enumerate((delta_u, delta_v)):
             wave = cos_sin(delta * (0.5 / SUB))
             turn = times(wave, wave)
-            count = 8 + 8 * axis
-            for j in range(count):
-                base_ref[k, pl.ds(16 * axis + j, channels, stride=BASE), :] = wave[0]
-                base_ref[k, pl.ds(16 * axis + count + j, channels, stride=BASE), :] = wave[1]
+            for j in range(16):
+                base_ref[k, pl.ds(32 * axis + j, channels, stride=BASE), :] = wave[0]
+                base_ref[k, pl.ds(32 * axis + 16 + j, channels, stride=BASE), :] = wave[1]
                 if j == 0:
                     last, wave = wave, times(wave, turn)
                     twice = 2.0 * turn[0]
-                elif j < count - 1:
+                elif j < 15:
                     last, wave = wave, tuple(twice * wave[part] - last[part] for part in range(2))
             if axis == 1:
                 break
             for _ in range(3):
                 turn = times(turn, turn)
-            z_ref[k, COLUMNS + 2 * axis, 0:channels] = turn[0]
-            z_ref[k, COLUMNS + 2 * axis + 1, 0:channels] = turn[1]
+            z_ref[k, COLUMNS, 0:channels] = 2.0 * turn[0]
 
     def add_rows(k, c):
         def row_of(i):
@@ -156,10 +154,9 @@
             return base_ref[k, BASE * c + 8 * i : BASE * c + 8 * i + 8, :]
 
         at = k * channels + c
-        turn = (row_of(COLUMNS), row_of(COLUMNS + 1))
-        twice = 2.0 * turn[0]
-        wave = (base_of(0), base_of(1))
-        after = times(wave, turn)
+        twice = row_of(COLUMNS)
+        wave = (base_of(0), base_of(2))
+        after = (base_of(1), base_of(3))
         for i in range(COLUMNS):
             for part in range(2):
                 left_ref[at, 128 * part + 16 * i : 128 * part + 16 * i + 16] = jnp.concatenate(
@@ -168,7 +165,7 @@
             if i < COLUMNS - 1:
                 wave = tuple(twice * after[part] - wave[part] for part in range(2))
                 after = tuple(twice * wave[part] - after[part] for part in range(2))
-        both = tuple(base_ref[k, BASE * c + 16 + 16 * i : BASE * c + 32 + 16 * i, :] for i in range(2))
+        both = tuple(base_ref[k, BASE * c + 32 + 16 * i : BASE * c + 48 + 16 * i, :] for i in range(2))
         for g in range(COLUMNS // 2):
             for part in range(2):
                 turned = row_of(2 * g + part)

time: 42.7 us -> 42.5 us (level)
  starting transfers between devices: 6.46 us -> 21.4 us
  Pallas kernels: 19.2 us -> 6.55 us
  waiting for transfers between devices: 11.2 us -> 8.43 us
    ppermute x6, starting transfers between devices: 6.46 us -> 21.4 us  [swap(): return lax.ppermute(value, ('facet', 'freq'), pairs)]
    pallas_call x1, Pallas kernels: 13.3 us -> 0.66 us  [grid_blocks(): pl.pallas_call(grid_kernel, grid=(facet_total // COLUMNS, half_blocks), i...]
    ppermute x6, waiting for transfers between devices: 11.2 us -> 8.43 us  [swap(): return lax.ppermute(value, ('facet', 'freq'), pairs)]
  transfers between devices with their start and end apart: 6 -> 6, of which waited for: 5 -> 4; matrix products, arithmetic and copies ran while one was open for 2% -> 2% of each run, Pallas kernels for 10% -> 10%
where the time goes in v8:
time: 42.5 us; the launch traced here: 42.2 us
  starting transfers between devices  21.4 us (50%)
  waiting for transfers between devices  8.43 us (20%)
  Pallas kernels  6.55 us (15%)
  local copies, waits for them, and re-layouts  3.89 us (9%)
  between operations  0.95 us (2%)
  other arithmetic  0.93 us (2%)
    ppermute x6, starting transfers between devices, swap(): return lax.ppermute(value, ('facet', 'freq'), pairs)  21.4 us
    ppermute x6, waiting for transfers between devices, swap(): return lax.ppermute(value, ('facet', 'freq'), pairs)  8.43 us
    unnamed x12, local copies, waits for them, and re-layouts  3.86 us
    pallas_call x1, Pallas kernels, image_blocks(): pl.pallas_call(image_kernel, in_specs=[pl.BlockSpec(memory_space=pltpu.VM...  1.78 us
    pallas_call x1, Pallas kernels, gather(): pl.pallas_call(gather_kernel, in_specs=[pl.BlockSpec(memory_space=pltpu.H...  1.7 us
    pallas_call x1, Pallas kernels, across_of(): pl.pallas_call(across_kernel, in_specs=[smem, smem, vmem] + [pl.BlockSpec...  1.45 us
    pallas_call x1, Pallas kernels, down_of(): pl.pallas_call(down_kernel, in_specs=[smem, smem, smem, smem, pl.BlockSpe...  0.96 us
  transfers between devices with their start and end apart: 6, of which 4 were waited for; matrix products, arithmetic and copies ran while one was open for 2% of the time, Pallas kernels for 10%

profile of v8, /device:TPU:0, one launch (start us, length us, event | category | flops | bytes accessed | tf_op | source)
XLA Modules:
  0.0 42.2 jit_solution(8502222093059764594)
XLA Ops:
  0.0 0.0 copy-start
  0.0 0.5 %collective-permute-start = (f32[1,10,2,32,128]{4,3,2,1,0:T(8,128)}, f32[1,10,2,32,128]{4,3,2,1,0:T(8,128)S(1)}, u32[]{:S(2)}, u32[]{:S(2)}) collective-permute-start(f32[1,10,2,32,128]{4,3,2,1,0:T(8,128)} %param.8), channel_id=1, source_target_pairs={{0,1},{1,0},{2,3},{3,2},{4,5},{5,4},{6,7},{7,6},{8,9},{9,8},{10,11... | collective-permute-start | bytes 983048 | tf_op jit(solution)/shard_map/ppermute | solution.py:390
  1.3 1.7 %gather_blocks.1.own_ref = f32[5,112,128]{2,1,0:T(8,128)} custom-call(s32[2]{0:T(128)} %owners_ref.3, s32[2,8,10]{2,1,0:T(8,128)} %corners_ref.3, f32[10,3,1,128]{3,2,1,0:T(1,128)} %bitcast.30, f32[10,64,128]{2,1,0:T(8,128)} %bitcast.28), custom_call_target="tpu_custom_call" | custom-call | tf_op jit(solution)/shard_map/gather_blocks/pallas_call | solution.py:82
  3.0 0.0 collective-permute-done.other_ref
  3.0 0.0 copy-start.1
  3.0 0.9 %copy-done.1 = f32[5,112,128]{2,1,0:T(8,128)S(1)} copy-done((f32[5,112,128]{2,1,0:T(8,128)S(1)}, f32[5,112,128]{2,1,0:T(8,128)}, u32[]{:S(2)}) %copy-start.1) | copy-done | bytes 286744
  4.0 0.7 %grid_blocks.1 = (f32[4,80,128]{2,1,0:T(8,128)S(1)}, f32[4,80,128]{2,1,0:T(8,128)S(1)}) custom-call(f32[5,112,128]{2,1,0:T(8,128)S(1)} %copy-done.1, f32[1,10,2,32,128]{4,3,2,1,0:T(8,128)S(1)} %collective-permute-done.other_ref), custom_call_target="tpu_custom_call" | custom-call | tf_op jit(solution)/shard_map/grid_blocks/pallas_call | solution.py:223
  4.6 2.5 %collective-permute-start.1 = (f32[1,4,80,128]{3,2,1,0:T(8,128)S(1)}, f32[1,4,80,128]{3,2,1,0:T(8,128)S(1)}, u32[]{:S(2)}, u32[]{:S(2)}) collective-permute-start(f32[1,4,80,128]{3,2,1,0:T(8,128)S(1)} %bitcast.25), channel_id=1, source_target_pairs={{0,4},{1,9},{2,6},{3,11},{4,0},{5,13},{6,2},{7,15},{8,12},{9,1},{1... | collective-permute-start | bytes 491528 | tf_op jit(solution)/shard_map/ppermute | solution.py:390
  7.2 0.7 %and_compare_fusion.2 = (pred[2]{0:T(512)(128)(4,1)S(1)}, pred[2]{0:T(512)(128)(4,1)S(1)}, pred[2]{0:T(512)(128)(4,1)S(1)}) fusion(s32[2]{0:T(128)} %owners_ref.3, s32[]{:T(128)S(6)} %axis_index.23, s32[]{:T(128)S(6)} %select_n.21, s32[]{:T(128)S(6)} %select_n.22), kind=kLoop, calls=%fused_computation.11 | loop fusion | flops 20 | bytes 26 | tf_op jit(solution)/shard_map/eq | solution.py:421
  7.8 0.0 copy-start.3
  7.8 0.7 %copy-done.3 = s32[2,8,10]{2,1,0:T(8,128)S(1)} copy-done((s32[2,8,10]{2,1,0:T(8,128)S(1)}, s32[2,8,10]{2,1,0:T(8,128)}, u32[]{:S(2)}) %copy-start.3) | copy-done | bytes 664
  8.5 0.0 copy-start.4
  8.5 0.7 %copy-done.4 = s32[2]{0:T(128)S(1)} copy-done((s32[2]{0:T(128)S(1)}, s32[2]{0:T(128)}, u32[]{:S(2)}) %copy-start.4) | copy-done | bytes 32
  9.2 0.7 %copy-done.5 = s32[1,20]{1,0:T(1,128)S(1)} copy-done((s32[1,20]{1,0:T(1,128)S(1)}, s32[1,20]{1,0:T(1,128)}, u32[]{:S(2)}) %copy-start.5) | copy-done | bytes 104
  9.8 1.0 %image_down.1.down_ref = f32[2,128,320]{2,1,0:T(8,128)S(1)} custom-call(s32[2]{0:T(128)S(1)} %copy-done.4, s32[2,8,10]{2,1,0:T(8,128)S(1)} %copy-done.3, s32[1,20]{1,0:T(1,128)S(1)} %copy-done.5, s32[1]{0:T(128)S(6)} %copy.16.counts_ref, f32[1,4,80,128]{3,2,1,0:T(8,128)S(1)} %bitcast.26), custom_call_target="tpu_custom_call" | custom-call | flops 10000000 | bytes 1000000 | tf_op jit(solution)/shard_map/image_down/pallas_call | solution.py:341
  10.8 0.0 collective-permute-done.1
  10.8 0.1 broadcast_select_fusion
  10.9 1.8 %collective-permute-start.2 = (f32[2,2,80,128]{3,2,0,1:T(8,128)S(1)}, f32[2,2,80,128]{3,2,0,1:T(8,128)S(1)}, u32[]{:S(2)}, u32[]{:S(2)}) collective-permute-start(f32[2,2,80,128]{3,2,0,1:T(8,128)S(1)} %slice_bitcast_fusion.1), channel_id=1, source_target_pairs={{0,8},{1,5},{2,10},{3,7},{4,12},{5,1},{6,14},{7,3},{8,0},{9,13},{1... | collective-permute-start | bytes 491528 | tf_op jit(solution)/shard_map/ppermute | solution.py:390
  12.8 0.0 copy-done
  12.8 0.0 copy-start.2
  12.8 0.9 %copy-done.2 = f32[4,16,512]{2,1,0:T(8,128)S(1)} copy-done((f32[4,16,512]{2,1,0:T(8,128)S(1)}, f32[4,16,512]{2,1,0:T(8,128)}, u32[]{:S(2)}) %copy-start.2) | copy-done | bytes 131096
  13.7 1.4 %image_across.1 = (bf16[2,1280,512]{2,1,0:T(8,128)(2,1)S(1)}, bf16[2,512,128]{2,1,0:T(8,128)(2,1)S(1)}) custom-call(s32[2]{0:T(128)S(1)} %copy-done.4, s32[2,8,10]{2,1,0:T(8,128)S(1)} %copy-done.3, f32[4,16,512]{2,1,0:T(8,128)S(1)} %copy-done.2, bf16[8,2,512,128]{3,2,1,0:T(8,128)(2,1)S(1)} %copy-done, f32[2,2,80,128]{3,2,1,0:T(8,128)S(1)} %copy.11.after_ref), custom_call_target="tpu_custom_call" | custom-call | flops 100000000 | bytes 6000000 | tf_op jit(solution)/shard_map/image_across/pallas_call | solution.py:356
  15.1 1.2 %collective-permute-done.2 = f32[2,2,80,128]{3,2,0,1:T(8,128)S(1)} collective-permute-done((f32[2,2,80,128]{3,2,0,1:T(8,128)S(1)}, f32[2,2,80,128]{3,2,0,1:T(8,128)S(1)}, u32[]{:S(2)}, u32[]{:S(2)}) %collective-permute-start.2) | collective-permute-done | bytes 163872 | tf_op jit(solution)/shard_map/ppermute | solution.py:390
  16.3 0.1 fusion.1
  16.4 15.0 %collective-permute-start.3 = (f32[2,1,80,128]{3,2,0,1:T(8,128)S(1)}, f32[2,1,80,128]{3,2,0,1:T(8,128)S(1)}, u32[]{:S(2)}, u32[]{:S(2)}) collective-permute-start(f32[2,1,80,128]{3,2,0,1:T(8,128)S(1)} %slice_bitcast_fusion.3), channel_id=1, source_target_pairs={{0,16},{1,17},{2,18},{3,19},{4,20},{5,21},{6,22},{7,23},{8,24},{9,... | collective-permute-start | bytes 245768 | tf_op jit(solution)/shard_map/ppermute | solution.py:390
  31.5 3.1 %collective-permute-done.3 = f32[2,1,80,128]{3,2,0,1:T(8,128)S(1)} collective-permute-done((f32[2,1,80,128]{3,2,0,1:T(8,128)S(1)}, f32[2,1,80,128]{3,2,0,1:T(8,128)S(1)}, u32[]{:S(2)}, u32[]{:S(2)}) %collective-permute-start.3) | collective-permute-done | bytes 81952 | tf_op jit(solution)/shard_map/ppermute | solution.py:390
  34.5 0.1 fusion.3
  34.6 1.5 %collective-permute-start.4 = (f32[2,80,128]{2,1,0:T(8,128)S(1)}, f32[2,80,128]{2,1,0:T(8,128)S(1)}, u32[]{:S(2)}, u32[]{:S(2)}) collective-permute-start(f32[2,80,128]{2,1,0:T(8,128)S(1)} %fusion.3), channel_id=1, source_target_pairs={{0,2},{1,3},{2,0},{3,1},{4,6},{5,7},{6,4},{7,5},{8,10},{9,11},{10,... | collective-permute-start | bytes 245768 | tf_op jit(solution)/shard_map/ppermute | solution.py:390
  36.1 2.9 %collective-permute-done.4 = f32[2,80,128]{2,1,0:T(8,128)S(1)} collective-permute-done((f32[2,80,128]{2,1,0:T(8,128)S(1)}, f32[2,80,128]{2,1,0:T(8,128)S(1)}, u32[]{:S(2)}, u32[]{:S(2)}) %collective-permute-start.4) | collective-permute-done | bytes 81952 | tf_op jit(solution)/shard_map/ppermute | solution.py:390
  39.1 0.1 collective-permute-start.5
  39.2 1.3 %collective-permute-done.5.other_ref = f32[2,80,128]{2,1,0:T(8,128)S(1)} collective-permute-done((f32[2,80,128]{2,1,0:T(8,128)S(1)}, f32[2,80,128]{2,1,0:T(8,128)S(1)}, u32[]{:S(2)}, u32[]{:S(2)}) %collective-permute-start.5) | collective-permute-done | bytes 81952 | tf_op jit(solution)/shard_map/ppermute | solution.py:390
  40.4 1.8 %image_blocks.1 = f32[1,128,512]{2,1,0:T(8,128)} custom-call(f32[2,80,128]{2,1,0:T(8,128)S(1)} %add.3.own_ref, f32[2,80,128]{2,1,0:T(8,128)S(1)} %collective-permute-done.5.other_ref, f32[2,128,320]{2,1,0:T(8,128)S(1)} %image_down.1.down_ref, bf16[2,1280,512]{2,1,0:T(8,128)(2,1)S(1)} %get-tuple-element.21.across_ref, ...), custom_call_target="tpu_custom_call" | custom-call | tf_op jit(solution)/shard_map/image_blocks/pallas_call | solution.py:373
  (5 shorter events, 0.0 us)
Async XLA Ops:
  0.0 12.8 %copy-start = (bf16[8,2,512,128]{3,2,1,0:T(8,128)(2,1)S(1)}, bf16[8,2,512,128]{3,2,1,0:T(8,128)(2,1)}, u32[]{:S(2)}) copy-start(bf16[8,2,512,128]{3,2,1,0:T(8,128)(2,1)} %constant.20.clone.tables_ref) | copy-start | bytes 6291460
  0.0 3.0 %collective-permute-start = (f32[1,10,2,32,128]{4,3,2,1,0:T(8,128)}, f32[1,10,2,32,128]{4,3,2,1,0:T(8,128)S(1)}, u32[]{:S(2)}, u32[]{:S(2)}) collective-permute-start(f32[1,10,2,32,128]{4,3,2,1,0:T(8,128)} %param.8), channel_id=1, source_target_pairs={{0,1},{1,0},{2,3},{3,2},{4,5},{5,4},{6,7},{7,6},{8,9},{9,8},{10,11... | collective-permute-start | bytes 983048 | tf_op jit(solution)/shard_map/ppermute | solution.py:390
  3.0 1.0 %copy-start.1 = (f32[5,112,128]{2,1,0:T(8,128)S(1)}, f32[5,112,128]{2,1,0:T(8,128)}, u32[]{:S(2)}) copy-start(f32[5,112,128]{2,1,0:T(8,128)} %gather_blocks.1.own_ref) | copy-start | bytes 860164
  4.6 6.2 %collective-permute-start.1 = (f32[1,4,80,128]{3,2,1,0:T(8,128)S(1)}, f32[1,4,80,128]{3,2,1,0:T(8,128)S(1)}, u32[]{:S(2)}, u32[]{:S(2)}) collective-permute-start(f32[1,4,80,128]{3,2,1,0:T(8,128)S(1)} %bitcast.25), channel_id=1, source_target_pairs={{0,4},{1,9},{2,6},{3,11},{4,0},{5,13},{6,2},{7,15},{8,12},{9,1},{1... | collective-permute-start | bytes 491528 | tf_op jit(solution)/shard_map/ppermute | solution.py:390
  7.8 0.7 %copy-start.3 = (s32[2,8,10]{2,1,0:T(8,128)S(1)}, s32[2,8,10]{2,1,0:T(8,128)}, u32[]{:S(2)}) copy-start(s32[2,8,10]{2,1,0:T(8,128)} %corners_ref.3) | copy-start | bytes 1924
  8.5 0.7 %copy-start.4 = (s32[2]{0:T(128)S(1)}, s32[2]{0:T(128)}, u32[]{:S(2)}) copy-start(s32[2]{0:T(128)} %owners_ref.3) | copy-start | bytes 28
  9.2 0.7 %copy-start.5 = (s32[1,20]{1,0:T(1,128)S(1)}, s32[1,20]{1,0:T(1,128)}, u32[]{:S(2)}) copy-start(s32[1,20]{1,0:T(1,128)} %assign_ref.1) | copy-start | bytes 244
  10.9 5.4 %collective-permute-start.2 = (f32[2,2,80,128]{3,2,0,1:T(8,128)S(1)}, f32[2,2,80,128]{3,2,0,1:T(8,128)S(1)}, u32[]{:S(2)}, u32[]{:S(2)}) collective-permute-start(f32[2,2,80,128]{3,2,0,1:T(8,128)S(1)} %slice_bitcast_fusion.1), channel_id=1, source_target_pairs={{0,8},{1,5},{2,10},{3,7},{4,12},{5,1},{6,14},{7,3},{8,0},{9,13},{1... | collective-permute-start | bytes 491528 | tf_op jit(solution)/shard_map/ppermute | solution.py:390
  12.8 0.9 %copy-start.2 = (f32[4,16,512]{2,1,0:T(8,128)S(1)}, f32[4,16,512]{2,1,0:T(8,128)}, u32[]{:S(2)}) copy-start(f32[4,16,512]{2,1,0:T(8,128)} %constant.21.clone.second_ref) | copy-start | bytes 393220
  16.4 18.1 %collective-permute-start.3 = (f32[2,1,80,128]{3,2,0,1:T(8,128)S(1)}, f32[2,1,80,128]{3,2,0,1:T(8,128)S(1)}, u32[]{:S(2)}, u32[]{:S(2)}) collective-permute-start(f32[2,1,80,128]{3,2,0,1:T(8,128)S(1)} %slice_bitcast_fusion.3), channel_id=1, source_target_pairs={{0,16},{1,17},{2,18},{3,19},{4,20},{5,21},{6,22},{7,23},{8,24},{9,... | collective-permute-start | bytes 245768 | tf_op jit(solution)/shard_map/ppermute | solution.py:390
  34.6 4.4 %collective-permute-start.4 = (f32[2,80,128]{2,1,0:T(8,128)S(1)}, f32[2,80,128]{2,1,0:T(8,128)S(1)}, u32[]{:S(2)}, u32[]{:S(2)}) collective-permute-start(f32[2,80,128]{2,1,0:T(8,128)S(1)} %fusion.3), channel_id=1, source_target_pairs={{0,2},{1,3},{2,0},{3,1},{4,6},{5,7},{6,4},{7,5},{8,10},{9,11},{10,... | collective-permute-start | bytes 245768 | tf_op jit(solution)/shard_map/ppermute | solution.py:390
  39.1 1.3 %collective-permute-start.5 = (f32[2,80,128]{2,1,0:T(8,128)S(1)}, f32[2,80,128]{2,1,0:T(8,128)S(1)}, u32[]{:S(2)}, u32[]{:S(2)}) collective-permute-start(f32[2,80,128]{2,1,0:T(8,128)S(1)} %add.3.own_ref), channel_id=1, source_target_pairs={{0,1},{1,0},{2,3},{3,2},{4,5},{5,4},{6,7},{7,6},{8,9},{9,8},{10,11... | collective-permute-start | bytes 245768 | tf_op jit(solution)/shard_map/ppermute | solution.py:390
